TPU v7x, 32 devices: a whole 2x2x4 slice. The times are simulated.
32 devices in a mesh: dp: 8 (over y, x, core), tensor: 4 (over z).
Axes of the slice: x: 2, y: 2, z: 4, core: 2. Of those that a mesh axis runs over, the one named last changes fastest.
Arguments:
- tokens: bfloat16 [8192, 2048], P(('dp', 'tensor')), may hold values from -6 to 6
- segments: int32 [8192], P('dp'), may hold values from 0 to 2, as said below
- attn_gain: bfloat16 [2048], P('dp'), may hold values from 0.5 to 1.5
- w_query: bfloat16 [2048, 2048], P('dp', 'tensor'), may hold values from -0.125 to 0.125
- w_key: bfloat16 [2048, 256], P('dp', 'tensor'), may hold values from -0.125 to 0.125
- w_value: bfloat16 [2048, 256], P('dp', 'tensor'), may hold values from -0.125 to 0.125
- w_out: bfloat16 [2048, 2048], P('tensor', 'dp'), may hold values from -1 to 1
- mlp_gain: bfloat16 [2048], P('dp'), may hold values from 0.5 to 1.5
- w_gate: bfloat16 [2048, 5632], P('dp', 'tensor'), may hold values from -0.125 to 0.125
- w_up: bfloat16 [2048, 5632], P('dp', 'tensor'), may hold values from -0.125 to 0.125
- w_down: bfloat16 [5632, 2048], P('tensor', 'dp'), may hold values from -0.078125 to 0.078125
- cotangent: bfloat16 [8192, 2048], P(('dp', 'tensor')), may hold values from -6 to 6
Outputs:
- output: bfloat16 [8192, 2048], P(('dp', 'tensor'))
- grad_tokens: float32 [8192, 2048], P(('dp', 'tensor'))
- grad_attn_gain: float32 [2048], P('dp')
- grad_query: float32 [2048, 2048], P('dp', 'tensor')
- grad_key: float32 [2048, 256], P('dp', 'tensor')
- grad_value: float32 [2048, 256], P('dp', 'tensor')
- grad_out: float32 [2048, 2048], P('tensor', 'dp')
- grad_mlp_gain: float32 [2048], P('dp')
- grad_gate: float32 [2048, 5632], P('dp', 'tensor')
- grad_up: float32 [2048, 5632], P('dp', 'tensor')
- grad_down: float32 [5632, 2048], P('tensor', 'dp')
Inputs may be any that keep to these rules, and one draw needn't show every extreme that they name: `segments`: within each group of 1024 tokens (one index of dp) segment numbers never fall and name three sequences: the first starts at token 0 and is shorter than 256, the last has at most 64 tokens, the middle one holds the rest.
All inputs are finite; a program needn't handle non-finite values.
Results may differ from a plain program's by a relative error of at most 0.02.
Values may be sent and summed in bfloat16 or wider, within the bound.
A program may use at most 192 MiB of HBM per device.

v0:
```python
import math

import jax
import jax.numpy as jnp
from jax import lax
from jax.sharding import PartitionSpec as P

HEADS = 32
KV = 4
HD = 64
QBLOCK = 512


EPSILON = 1e-05
MASKED = -1e30


def contract_rows(left, right):
    return lax.dot_general(
        left, right, (((0,), (0,)), ((), ())), preferred_element_type=jnp.float32
    )


def contract_cols(left, right):
    return lax.dot_general(
        left, right, (((1,), (1,)), ((), ())), preferred_element_type=jnp.float32
    )


def rms_forward(values_in, gain_row):
    factor = lax.rsqrt(jnp.mean(values_in * values_in, axis=-1, keepdims=True) + EPSILON)
    return (values_in * factor * gain_row, factor)


def rms_backward(values_in, factor, gain_row, gradient):
    scaled = gain_row * gradient
    grad_gain = jnp.sum(gradient * values_in * factor, axis=0)
    grad_input = factor * scaled - values_in * (factor * factor * factor) * jnp.mean(
        scaled * values_in, axis=-1, keepdims=True
    )
    return (grad_input, grad_gain)


def positions_of(segment_row):
    indices = jnp.arange(segment_row.shape[0], dtype=jnp.int32)
    starts = jnp.concatenate([jnp.ones((1,), jnp.bool_), segment_row[1:] != segment_row[:-1]])
    first_index = lax.cummax(jnp.where(starts, indices, jnp.zeros_like(indices)), axis=0)
    return indices - first_index


def rope_tables(positions, head_width):
    half_width = head_width // 2
    frequency = jnp.exp(
        jnp.arange(half_width, dtype=jnp.float32) * (-2.0 * math.log(10000.0) / head_width)
    )
    angles = positions.astype(jnp.float32)[:, None] * frequency[None, :]
    cosine = jnp.cos(angles)
    sine_rows = jnp.sin(angles)
    return (jnp.concatenate([cosine, cosine], 1), jnp.concatenate([sine_rows, sine_rows], 1))


def rotate(arrays, cosine, sine_rows):
    half_width = arrays.shape[-1] // 2
    turned = jnp.concatenate([-arrays[..., half_width:], arrays[..., :half_width]], -1)
    return arrays * cosine + turned * sine_rows


def rotate_back(gradient, cosine, sine_rows):
    half_width = gradient.shape[-1] // 2
    shifted = gradient * sine_rows
    return gradient * cosine + jnp.concatenate(
        [shifted[..., half_width:], -shifted[..., :half_width]], -1
    )


def block_scores(query_head, key_head, attn_mask, block_start, block_end):
    scores = jnp.einsum(
        "qd,kd->qk",
        query_head[block_start:block_end],
        key_head[:block_end],
        preferred_element_type=jnp.float32,
    )
    return jnp.where(attn_mask[block_start:block_end, :block_end], scores, MASKED)


def head_forward(query_head, key_head, value_head, attn_mask):
    group_len = query_head.shape[0]
    outputs = []
    log_totals = []
    for block_start in range(0, group_len, QBLOCK):
        block_end = block_start + QBLOCK
        scores = block_scores(query_head, key_head, attn_mask, block_start, block_end)
        row_peak = jnp.max(scores, axis=-1, keepdims=True)
        exponent = jnp.exp(scores - row_peak)
        row_total = jnp.sum(exponent, axis=-1, keepdims=True)
        prob_rows = (exponent / row_total).astype(jnp.bfloat16)
        outputs.append(
            jnp.dot(prob_rows, value_head[:block_end], preferred_element_type=jnp.float32)
        )
        log_totals.append(row_peak[:, 0] + jnp.log(row_total[:, 0]))
    return (jnp.concatenate(outputs, 0), jnp.concatenate(log_totals, 0))


def head_backward(query_head, key_head, value_head, grad_head, log_totals, attn_mask):
    group_len = query_head.shape[0]
    grad_queries = []
    grad_keys = jnp.zeros(key_head.shape, jnp.float32)
    grad_values = jnp.zeros(value_head.shape, jnp.float32)
    for block_start in range(0, group_len, QBLOCK):
        block_end = block_start + QBLOCK
        scores = block_scores(query_head, key_head, attn_mask, block_start, block_end)
        prob_rows = jnp.exp(scores - log_totals[block_start:block_end, None])
        grad_block = grad_head[block_start:block_end]
        grad_probs = jnp.einsum(
            "qd,kd->qk", grad_block, value_head[:block_end], preferred_element_type=jnp.float32
        )
        row_delta = jnp.sum(prob_rows * grad_probs, axis=-1, keepdims=True)
        grad_scores = (prob_rows * (grad_probs - row_delta)).astype(jnp.bfloat16)
        grad_queries.append(
            jnp.dot(grad_scores, key_head[:block_end], preferred_element_type=jnp.float32)
        )
        grad_keys = grad_keys.at[:block_end].add(
            contract_rows(grad_scores, query_head[block_start:block_end])
        )
        grad_values = grad_values.at[:block_end].add(
            contract_rows(prob_rows.astype(jnp.bfloat16), grad_block)
        )
    return (jnp.concatenate(grad_queries, 0), grad_keys, grad_values)


def body(
    tokens,
    segments,
    attn_gain,
    w_query,
    w_key,
    w_value,
    w_out,
    mlp_gain,
    w_gate,
    w_up,
    w_down,
    cotangent,
):
    token_rows = tokens.shape[0]
    model_width = tokens.shape[1]
    group_len = segments.shape[0]
    query_cols = w_query.shape[1]
    key_cols = w_key.shape[1]
    hidden_cols = w_gate.shape[1]
    query_heads = query_cols // HD
    kv_heads = key_cols // HD
    group_ratio = HEADS // KV
    query_scale = HD ** (-0.5)
    positions = positions_of(segments)
    cosine, sine_rows = rope_tables(positions, HD)
    indices = jnp.arange(group_len)
    attn_mask = (indices[None, :] <= indices[:, None]) & (segments[None, :] == segments[:, None])
    attn_set = (
        lax.all_gather(w_query, "dp", axis=0, tiled=True),
        lax.all_gather(w_key, "dp", axis=0, tiled=True),
        lax.all_gather(w_value, "dp", axis=0, tiled=True),
        lax.all_gather(w_out, "dp", axis=1, tiled=True),
        lax.all_gather(attn_gain, "dp", axis=0, tiled=True),
    )
    full_query, full_key, full_value, full_out, full_gain1 = attn_set
    w_qkv = jnp.concatenate([full_query, full_key, full_value], 1)
    token_float = tokens.astype(jnp.float32)
    gain_attn = full_gain1.astype(jnp.float32)
    normed1, factor1 = rms_forward(token_float, gain_attn)
    rows_attn = lax.all_gather(normed1.astype(jnp.bfloat16), "tensor", axis=0, tiled=True)
    qkv_value = jnp.dot(rows_attn, w_qkv, preferred_element_type=jnp.float32)
    queries = qkv_value[:, :query_cols].reshape(group_len, query_heads, HD).transpose(1, 0, 2)
    keys_raw = (
        qkv_value[:, query_cols : query_cols + key_cols]
        .reshape(group_len, kv_heads, HD)
        .transpose(1, 0, 2)
    )
    values_raw = (
        qkv_value[:, query_cols + key_cols :].reshape(group_len, kv_heads, HD).transpose(1, 0, 2)
    )
    query_rot = (rotate(queries, cosine, sine_rows) * query_scale).astype(jnp.bfloat16)
    key_rot = rotate(keys_raw, cosine, sine_rows).astype(jnp.bfloat16)
    value_low = values_raw.astype(jnp.bfloat16)
    key_repeat = jnp.repeat(key_rot, group_ratio, axis=0)
    value_repeat = jnp.repeat(value_low, group_ratio, axis=0)

    def forward_heads(bundle):
        return head_forward(bundle[0], bundle[1], bundle[2], attn_mask)

    attended, log_totals = lax.map(forward_heads, (query_rot, key_repeat, value_repeat))
    mixed = attended.transpose(1, 0, 2).reshape(group_len, query_cols).astype(jnp.bfloat16)
    attn_part = lax.psum_scatter(
        jnp.dot(
            lax.slice_in_dim(mixed, 0, token_rows * lax.axis_size("tensor"), axis=0),
            full_out,
            preferred_element_type=jnp.float32,
        ),
        "tensor",
        scatter_dimension=0,
        tiled=True,
    )
    residual = token_float + attn_part
    mlp_set = (
        lax.all_gather(w_gate, "dp", axis=0, tiled=True),
        lax.all_gather(w_up, "dp", axis=0, tiled=True),
        lax.all_gather(w_down, "dp", axis=1, tiled=True),
        lax.all_gather(mlp_gain, "dp", axis=0, tiled=True),
    )
    full_gate, full_up, full_down, full_gain2 = mlp_set
    w_gate_up = jnp.concatenate([full_gate, full_up], 1)
    gain_mlp = full_gain2.astype(jnp.float32)
    normed2, factor2 = rms_forward(residual, gain_mlp)
    rows_mlp = lax.all_gather(normed2.astype(jnp.bfloat16), "tensor", axis=0, tiled=True)
    gate_up = jnp.dot(rows_mlp, w_gate_up, preferred_element_type=jnp.float32)
    gate_value = gate_up[:, :hidden_cols]
    up_value = gate_up[:, hidden_cols:]
    sigmoid_gate = jax.nn.sigmoid(gate_value)
    activated = gate_value * sigmoid_gate
    hidden = (activated * up_value).astype(jnp.bfloat16)
    mlp_part = lax.psum_scatter(
        jnp.dot(
            lax.slice_in_dim(hidden, 0, token_rows * lax.axis_size("tensor"), axis=0),
            full_down,
            preferred_element_type=jnp.float32,
        ).astype(jnp.bfloat16),
        "tensor",
        scatter_dimension=0,
        tiled=True,
    ).astype(jnp.float32)
    output = (residual + mlp_part).astype(jnp.bfloat16)
    piece_rows = lax.all_gather(cotangent, "tensor", axis=0, tiled=True)
    grad_down_sum = jnp.zeros((hidden_cols, model_width), jnp.float32)
    row_count = piece_rows.shape[0]
    grad_hidden = contract_cols(piece_rows, full_down)
    hidden_rows = lax.slice_in_dim(hidden, 0, row_count, axis=0)
    grad_hidden, grad_down_part = (
        grad_hidden,
        grad_down_sum + contract_rows(hidden_rows, piece_rows),
    )
    grad_gate_rows = (
        grad_hidden * up_value * (sigmoid_gate * (1.0 + gate_value * (1.0 - sigmoid_gate)))
    )
    grad_up_rows = grad_hidden * activated
    grad_gate_up = jnp.concatenate([grad_gate_rows, grad_up_rows], 1).astype(jnp.bfloat16)
    grad_gate_up_part = contract_rows(rows_mlp, grad_gate_up)
    grad_normed2 = lax.psum_scatter(
        contract_cols(
            lax.slice_in_dim(grad_gate_up, 0, token_rows * lax.axis_size("tensor"), axis=0),
            w_gate_up,
        ),
        "tensor",
        scatter_dimension=0,
        tiled=True,
    )
    grad_res_norm, grad_gain2_part = rms_backward(residual, factor2, gain_mlp, grad_normed2)
    grad_residual = cotangent.astype(jnp.float32) + grad_res_norm
    piece_rows = lax.all_gather(grad_residual.astype(jnp.bfloat16), "tensor", axis=0, tiled=True)
    start_row = jnp.int32(0)
    grad_mixed = jnp.zeros((group_len, query_cols), jnp.float32)
    grad_out_sum = jnp.zeros((query_cols, model_width), jnp.float32)
    row_count = piece_rows.shape[0]
    grad_mixed = lax.dynamic_update_slice_in_dim(
        grad_mixed, contract_cols(piece_rows, full_out), start_row, 0
    )
    mixed_rows = lax.dynamic_slice_in_dim(mixed, start_row, row_count, 0)
    grad_mixed, grad_out_part = (grad_mixed, grad_out_sum + contract_rows(mixed_rows, piece_rows))
    grad_heads = (
        grad_mixed.astype(jnp.bfloat16).reshape(group_len, query_heads, HD).transpose(1, 0, 2)
    )

    def backward_heads(bundle):
        return head_backward(bundle[0], bundle[1], bundle[2], bundle[3], bundle[4], attn_mask)

    grad_query_rot, grad_key_rep, grad_value_rep = lax.map(
        backward_heads, (query_rot, key_repeat, value_repeat, grad_heads, log_totals)
    )
    grad_key_rot = grad_key_rep.reshape(kv_heads, group_ratio, group_len, HD).sum(axis=1)
    grad_value_low = grad_value_rep.reshape(kv_heads, group_ratio, group_len, HD).sum(axis=1)
    grad_query_raw = rotate_back(grad_query_rot * query_scale, cosine, sine_rows)
    grad_key_raw = rotate_back(grad_key_rot, cosine, sine_rows)
    grad_qkv = jnp.concatenate(
        [
            grad_query_raw.transpose(1, 0, 2).reshape(group_len, query_cols),
            grad_key_raw.transpose(1, 0, 2).reshape(group_len, key_cols),
            grad_value_low.transpose(1, 0, 2).reshape(group_len, key_cols),
        ],
        1,
    ).astype(jnp.bfloat16)
    grad_qkv_part = contract_rows(rows_attn, grad_qkv)
    grad_normed1 = lax.psum_scatter(
        contract_cols(grad_qkv, w_qkv).astype(jnp.bfloat16),
        "tensor",
        scatter_dimension=0,
        tiled=True,
    ).astype(jnp.float32)
    grad_in_norm, grad_gain1_part = rms_backward(token_float, factor1, gain_attn, grad_normed1)
    grad_tokens = grad_residual + grad_in_norm
    grad_query_part = grad_qkv_part[:, :query_cols]
    grad_key_part = grad_qkv_part[:, query_cols : query_cols + key_cols]
    grad_value_part = grad_qkv_part[:, query_cols + key_cols :]
    all_sums = (
        lax.psum_scatter(
            grad_query_part.astype(jnp.bfloat16), "dp", scatter_dimension=0, tiled=True
        ).astype(jnp.float32),
        lax.psum_scatter(
            grad_key_part.astype(jnp.bfloat16), "dp", scatter_dimension=0, tiled=True
        ).astype(jnp.float32),
        lax.psum_scatter(
            grad_value_part.astype(jnp.bfloat16), "dp", scatter_dimension=0, tiled=True
        ).astype(jnp.float32),
        lax.psum_scatter(
            grad_out_part.astype(jnp.bfloat16), "dp", scatter_dimension=1, tiled=True
        ).astype(jnp.float32),
        lax.psum_scatter(
            grad_gain1_part.astype(jnp.bfloat16), "dp", scatter_dimension=0, tiled=True
        ).astype(jnp.float32),
        lax.psum_scatter(
            grad_gate_up_part.astype(jnp.bfloat16), "dp", scatter_dimension=0, tiled=True
        ).astype(jnp.float32),
        lax.psum_scatter(
            grad_down_part.astype(jnp.bfloat16), "dp", scatter_dimension=1, tiled=True
        ).astype(jnp.float32),
        lax.psum_scatter(
            grad_gain2_part.astype(jnp.bfloat16), "dp", scatter_dimension=0, tiled=True
        ).astype(jnp.float32),
    )
    (
        grad_query,
        grad_key,
        grad_value,
        grad_out,
        gain1_share,
        grad_gate_up,
        grad_down,
        gain2_share,
    ) = all_sums
    grad_attn_gain, grad_mlp_gain = lax.psum((gain1_share, gain2_share), "tensor")
    grad_gate = grad_gate_up[:, :hidden_cols]
    grad_up = grad_gate_up[:, hidden_cols:]
    return (
        output,
        grad_tokens,
        grad_attn_gain,
        grad_query,
        grad_key,
        grad_value,
        grad_out,
        grad_mlp_gain,
        grad_gate,
        grad_up,
        grad_down,
    )


def solution(mesh):
    return jax.shard_map(
        body,
        mesh=mesh,
        in_specs=(
            P(("dp", "tensor"), None),
            P("dp"),
            P("dp"),
            P("dp", "tensor"),
            P("dp", "tensor"),
            P("dp", "tensor"),
            P("tensor", "dp"),
            P("dp"),
            P("dp", "tensor"),
            P("dp", "tensor"),
            P("tensor", "dp"),
            P(("dp", "tensor"), None),
        ),
        out_specs=(
            P(("dp", "tensor"), None),
            P(("dp", "tensor"), None),
            P("dp"),
            P("dp", "tensor"),
            P("dp", "tensor"),
            P("dp", "tensor"),
            P("tensor", "dp"),
            P("dp"),
            P("dp", "tensor"),
            P("dp", "tensor"),
            P("tensor", "dp"),
        ),
        check_vma=False,
    )
```

profile of v0, /device:TPU:0, one launch (start us, length us, event | category | flops | bytes accessed | tf_op | source)
XLA Modules:
  0.0 1482.5 jit_solution(16352107110189093500)
XLA Ops:
  26.2 10.9 all_gather.42
  48.7 76.0 %all-gather.12.cloned.1.call-done = bf16[1024,2048]{1,0:T(8,128)(2,1)} async-done(((bf16[256,2048]{1,0:T(8,128)(2,1)}), bf16[1024,2048]{1,0:T(8,128)(2,1)}) %all-gather.12.cloned.1.call-update) | async-done | bytes 4194320 | tf_op jit(solution)/shard_map/all_gather | solution.py:171
  157.5 95.9 %while.37 = (s32[]{:T(128)}, bf16[8,1024,64]{1,2,0:T(8,128)(2,1)}, f32[8,1024]{1,0:T(8,128)}, pred[1024,1024]{0,1:T(32,128)(4,1)S(1)}, bf16[8,1024,64]{2,1,0:T(8...) while((s32[]{:T(128)}, bf16[8,1024,64]{1,2,0:T(8,128)(2,1)}, ...), condition=%wide.region_8.9_spmd.clone, body=%wide.region_3.8_spmd.sunk.clone | while | flops 207093760 | bytes 18009724 | solution.py:191
  271.1 133.0 %reduce-scatter.11.cloned.1.call-done = f32[256,2048]{1,0:T(8,128)} async-done(((f32[1024,2048]{1,0:T(8,128)}), f32[256,2048]{1,0:T(8,128)}) %reduce-scatter.11.cloned.1.call-update) | async-done | bytes 2097168 | tf_op jit(solution)/shard_map/reduce_scatter | solution.py:193
  409.1 40.8 %all-gather.20.cloned.1.call-done = bf16[2048,1408]{1,0:T(8,128)(2,1)} async-done(((bf16[256,1408]{1,0:T(8,128)(2,1)}), bf16[2048,1408]{1,0:T(8,128)(2,1)}) %all-gather.20.cloned.1.call-update) | async-done | bytes 5767184 | tf_op jit(solution)/shard_map/all_gather | solution.py:205
  455.4 39.5 %all-gather.22.cloned.1.call-done = bf16[2048,1408]{1,0:T(8,128)(2,1)} async-done(((bf16[256,1408]{1,0:T(8,128)(2,1)}), bf16[2048,1408]{1,0:T(8,128)(2,1)}) %all-gather.22.cloned.1.call-update) | async-done | bytes 5767184 | tf_op jit(solution)/shard_map/all_gather | solution.py:206
  500.6 77.3 %all-gather.18.cloned.1.call-done = bf16[1024,2048]{1,0:T(8,128)(2,1)} async-done(((bf16[256,2048]{1,0:T(8,128)(2,1)}), bf16[1024,2048]{1,0:T(8,128)(2,1)}) %all-gather.18.cloned.1.call-update) | async-done | bytes 4194320 | tf_op jit(solution)/shard_map/all_gather | solution.py:214
  577.9 18.9 %fusion.81 = f32[1024,2816]{1,0:T(8,128)} fusion(bf16[1024,2048]{1,0:T(8,128)(2,1)} %all-gather.18.cloned.1.call-done, bf16[2048,2816]{1,0:T(8,128)(2,1)} %constant_dynamic-update-slice_fusion), kind=kOutput, calls=%fused_computation.176 | convolution fusion | flops 11811160064 | bytes 27262976 | tf_op jit(solution)/shard_map/dot_general | solution.py:215
  596.9 62.0 %all-gather.26.cloned.1.call-done = bf16[1024,2048]{1,0:T(8,128)(2,1)} async-done(((bf16[256,2048]{1,0:T(8,128)(2,1)}), bf16[1024,2048]{1,0:T(8,128)(2,1)}) %all-gather.26.cloned.1.call-update) | async-done | bytes 4194320 | tf_op jit(solution)/shard_map/all_gather | solution.py:232
  658.8 44.8 %all-gather.24.cloned.1.call-done = bf16[1408,2048]{1,0:T(8,128)(2,1)} async-done(((bf16[1408,256]{1,0:T(8,128)(2,1)}), bf16[1408,2048]{1,0:T(8,128)(2,1)}) %all-gather.24.cloned.1.call-update) | async-done | bytes 5767184 | tf_op jit(solution)/shard_map/all_gather | solution.py:207
  703.6 16.1 %multiply_convert_fusion.3 = (bf16[1024,1408]{1,0:T(8,128)(2,1)S(1)}, bf16[1024,1408]{1,0:T(8,128)(2,1)S(1)}, bf16[1024,1408]{1,0:T(8,128)(2,1)}) fusion(f32[1024,2816]{1,0:T(8,128)} %fusion.81, bf16[1024,2048]{1,0:T(8,128)(2,1)} %all-gather.26.cloned.1.call-done, bf16[1408,2048]{1,0:T(8,128)(2,1)} %all-gather.24.cloned.1.call-done), kind=kOutput, calls=%fused_computation.78 | convolution fusion | flops 5927206912 | bytes 30146560 | tf_op jit(solution)/shard_map/dot_general | solution.py:25
  722.2 16.9 %fusion.49 = f32[1024,2048]{1,0:T(8,128)} fusion(bf16[2048,2816]{1,0:T(8,128)(2,1)} %constant_dynamic-update-slice_fusion, bf16[1024,1408]{1,0:T(8,128)(2,1)S(1)} %get-tuple-element.375, bf16[1024,1408]{1,0:T(8,128)(2,1)S(1)} %get-tuple-element.374), kind=kOutput, calls=%fused_computation.97 | convolution fusion | flops 11822694400 | bytes 25690112 | tf_op jit(solution)/shard_map/dot_general | solution.py:25
  739.2 11.3 convolution_convert_fusion.3
  750.6 133.2 %reduce-scatter.15.cloned.1.call-done = f32[256,2048]{1,0:T(8,128)} async-done(((f32[1024,2048]{1,0:T(8,128)}), f32[256,2048]{1,0:T(8,128)}) %reduce-scatter.15.cloned.1.call-update) | async-done | bytes 2097168 | tf_op jit(solution)/shard_map/reduce_scatter | solution.py:247
  885.9 77.7 %reduce-scatter.13.cloned.1.call-done = bf16[256,2048]{1,0:T(8,128)(2,1)} async-done(((bf16[1024,2048]{1,0:T(8,128)(2,1)}), bf16[256,2048]{1,0:T(8,128)(2,1)}) %reduce-scatter.13.cloned.1.call-update) | async-done | bytes 1048592 | tf_op jit(solution)/shard_map/reduce_scatter | solution.py:221
  979.2 18.5 %convolution_convert_fusion = bf16[2048,2816]{1,0:T(8,128)(2,1)} fusion(bf16[1024,2048]{1,0:T(8,128)(2,1)} %all-gather.18.cloned.1.call-done, bf16[1024,1408]{1,0:T(8,128)(2,1)} %copy-done.34, bf16[1024,1408]{1,0:T(8,128)(2,1)} %copy-done.33), kind=kOutput, calls=%fused_computation.74 | convolution fusion | flops 11828461568 | bytes 21495808 | tf_op jit(solution)/shard_map/dot_general | solution.py:19
  997.8 52.2 %all-gather.28.cloned.1.call-done = bf16[1024,2048]{1,0:T(8,128)(2,1)} async-done(((bf16[256,2048]{1,0:T(8,128)(2,1)}), bf16[1024,2048]{1,0:T(8,128)(2,1)}) %all-gather.28.cloned.1.call-update) | async-done | bytes 4194320 | tf_op jit(solution)/shard_map/all_gather | solution.py:258
  1057.8 130.5 %while.38 = (s32[]{:T(128)}, f32[8,1024,64]{1,2,0:T(8,128)}, f32[8,1024,64]{1,2,0:T(8,128)}, f32[8,1024,64]{1,2,0:T(8,128)}, pred[1024,1024]{0,1:T(32,128)(4,1)S...) while((s32[]{:T(128)}, f32[8,1024,64]{1,2,0:T(8,128)}, ...), condition=%wide.region_17.18_spmd.clone, body=%wide.region_14.17_spmd.sunk.clone | while | flops 509803520 | bytes 30568588 | solution.py:275
  1240.1 36.0 %reduce-scatter.23.cloned.1.call-done = bf16[256,64]{0,1:T(8,128)(2,1)} async-done(((bf16[2048,64]{0,1:T(8,128)(2,1)}), bf16[256,64]{0,1:T(8,128)(2,1)}) %reduce-scatter.23.cloned.1.call-update) | async-done | bytes 32784 | tf_op jit(solution)/shard_map/reduce_scatter | solution.py:309
  1277.5 43.0 %reduce-scatter.25.cloned.1.call-done = bf16[512,256]{1,0:T(8,128)(2,1)} async-done(((bf16[512,2048]{1,0:T(8,128)(2,1)}), bf16[512,256]{1,0:T(8,128)(2,1)}) %reduce-scatter.25.cloned.1.call-update) | async-done | bytes 262160 | tf_op jit(solution)/shard_map/reduce_scatter | solution.py:312
  1322.3 43.6 %reduce-scatter.19.cloned.1.call-done = bf16[256,512]{0,1:T(8,128)(2,1)} async-done(((bf16[2048,512]{0,1:T(8,128)(2,1)}), bf16[256,512]{0,1:T(8,128)(2,1)}) %reduce-scatter.19.cloned.1.call-update) | async-done | bytes 262160 | tf_op jit(solution)/shard_map/reduce_scatter | solution.py:303
  1367.7 77.2 %reduce-scatter.17.cloned.1.call-done = bf16[256,2048]{1,0:T(8,128)(2,1)} async-done(((bf16[1024,2048]{1,0:T(8,128)(2,1)}), bf16[256,2048]{1,0:T(8,128)(2,1)}) %reduce-scatter.17.cloned.1.call-update) | async-done | bytes 1048592 | tf_op jit(solution)/shard_map/reduce_scatter | solution.py:291
  1446.8 14.0 all-reduce.5
  1460.9 11.7 all-reduce.4
  (413 shorter events, 411.8 us)
Async XLA Ops:
  7.2 41.6 %all-gather.14.cloned.1.call-start = ((), (), s32[]{:S(2)}) async-start(), calls=%async_computation.11 | async-start | bytes 2359296 | tf_op jit(solution)/shard_map/all_gather | solution.py:160
  7.9 116.8 %all-gather.12.cloned.1.call-start = ((), (), s32[]{:S(2)}) async-start(), calls=%async_computation.10 | async-start | bytes 5242880 | tf_op jit(solution)/shard_map/all_gather | solution.py:171
  23.6 229.7 %all-gather.16.cloned.1.call-start = ((), (), s32[]{:S(2)}) async-start(), calls=%async_computation.12 | async-start | bytes 2359296 | tf_op jit(solution)/shard_map/all_gather | solution.py:163
  24.4 379.7 %reduce-scatter.11.cloned.1.call-start = ((), (), s32[]{:S(2)}) async-start(), calls=%async_computation.13 | async-start | bytes 10485760 | tf_op jit(solution)/shard_map/reduce_scatter | solution.py:193
  260.9 189.0 %all-gather.20.cloned.1.call-start = ((), (), s32[]{:S(2)}) async-start(), calls=%async_computation.15 | async-start | bytes 6488064 | tf_op jit(solution)/shard_map/all_gather | solution.py:205
  261.5 233.5 %all-gather.22.cloned.1.call-start = ((), (), s32[]{:S(2)}) async-start(), calls=%async_computation.16 | async-start | bytes 6488064 | tf_op jit(solution)/shard_map/all_gather | solution.py:206
  262.1 315.8 %all-gather.18.cloned.1.call-start = ((), (), s32[]{:S(2)}) async-start(), calls=%async_computation.14 | async-start | bytes 5242880 | tf_op jit(solution)/shard_map/all_gather | solution.py:214
  407.5 251.3 %all-gather.26.cloned.1.call-start = ((), (), s32[]{:S(2)}) async-start(), calls=%async_computation.19 | async-start | bytes 5242880 | tf_op jit(solution)/shard_map/all_gather | solution.py:232
  408.3 295.3 %all-gather.24.cloned.1.call-start = ((), (), s32[]{:S(2)}) async-start(), calls=%async_computation.17 | async-start | bytes 6488064 | tf_op jit(solution)/shard_map/all_gather | solution.py:207
  409.0 474.8 %reduce-scatter.15.cloned.1.call-start = ((), (), s32[]{:S(2)}) async-start(), calls=%async_computation.20 | async-start | bytes 10485760 | tf_op jit(solution)/shard_map/reduce_scatter | solution.py:247
  739.2 224.5 %reduce-scatter.13.cloned.1.call-start = ((), (), s32[]{:S(2)}) async-start(), calls=%async_computation.18 | async-start | bytes 5242880 | tf_op jit(solution)/shard_map/reduce_scatter | solution.py:221
  750.6 299.4 %all-gather.28.cloned.1.call-start = ((), (), s32[]{:S(2)}) async-start(), calls=%async_computation.21 | async-start | bytes 5242880 | tf_op jit(solution)/shard_map/all_gather | solution.py:258
  968.6 255.5 %reduce-scatter.29.cloned.1.call-start = ((), (), s32[]{:S(2)}) async-start(), calls=%async_computation.28 | async-start | bytes 6488064 | tf_op jit(solution)/shard_map/reduce_scatter | solution.py:321
  979.1 247.3 %reduce-scatter.27.cloned.1.call-start = ((), (), s32[]{:S(2)}) async-start(), calls=%async_computation.27 | async-start | bytes 12976128 | tf_op jit(solution)/shard_map/reduce_scatter | solution.py:318
  997.7 241.0 %reduce-scatter.21.cloned.1.call-start = ((), (), s32[]{:S(2)}) async-start(), calls=%async_computation.24 | async-start | bytes 294912 | tf_op jit(solution)/shard_map/reduce_scatter | solution.py:306
  1202.4 73.7 %reduce-scatter.23.cloned.1.call-start = ((), (), s32[]{:S(2)}) async-start(), calls=%async_computation.25 | async-start | bytes 294912 | tf_op jit(solution)/shard_map/reduce_scatter | solution.py:309
  1203.0 117.5 %reduce-scatter.25.cloned.1.call-start = ((), (), s32[]{:S(2)}) async-start(), calls=%async_computation.26 | async-start | bytes 2359296 | tf_op jit(solution)/shard_map/reduce_scatter | solution.py:312
  1209.2 156.6 %reduce-scatter.19.cloned.1.call-start = ((), (), s32[]{:S(2)}) async-start(), calls=%async_computation.23 | async-start | bytes 2359296 | tf_op jit(solution)/shard_map/reduce_scatter | solution.py:303
  1212.5 232.4 %reduce-scatter.17.cloned.1.call-start = ((), (), s32[]{:S(2)}) async-start(), calls=%async_computation.22 | async-start | bytes 5242880 | tf_op jit(solution)/shard_map/reduce_scatter | solution.py:291
  1226.4 218.5 %copy-start.22 = (f32[8,1,256]{2,1,0:T(1,128)S(1)}, f32[8,1,256]{2,1,0:T(1,128)}, u32[]{:S(2)}) copy-start(f32[8,1,256]{2,1,0:T(1,128)} %copy-done.21) | copy-start | bytes 24580
  1226.4 218.5 %copy-start.27 = (f32[256]{0:T(256)S(1)}, f32[256]{0:T(256)}, u32[]{:S(2)}) copy-start(f32[256]{0:T(256)} %copy-done.26) | copy-start | bytes 3076
  1229.5 215.4 %copy-start = (bf16[256,2048]{1,0:T(8,128)(2,1)S(1)}, bf16[256,2048]{1,0:T(8,128)(2,1)}, u32[]{:S(2)}) copy-start(bf16[256,2048]{1,0:T(8,128)(2,1)} %param.28) | copy-start | bytes 3145732
  1229.5 243.0 %copy-start.2 = (f32[256,2048]{1,0:T(8,128)S(1)}, f32[256,2048]{1,0:T(8,128)}, u32[]{:S(2)}) copy-start(f32[256,2048]{1,0:T(8,128)} %get-tuple-element.359) | copy-start | bytes 6291460
  1229.5 243.0 %copy-start.28 = (f32[256]{0:T(256)S(1)}, f32[256]{0:T(256)}, u32[]{:S(2)}) copy-start(f32[256]{0:T(256)} %get-tuple-element.398) | copy-start | bytes 3076
  (37 other events, 415.7 us)
Sparse Core Ops, SparseCore 0:
  9.9 31.5 all-gather.13
  43.6 81.0 all-gather.11
  126.6 26.7 all-gather.15
  261.1 142.9 reduce-scatter.10
  405.8 44.0 all-gather.19
  451.6 43.3 all-gather.21
  497.1 80.7 all-gather.17
  579.5 79.2 all-gather.25
  660.7 42.8 all-gather.23
  739.3 144.4 reduce-scatter.14
  886.1 77.4 reduce-scatter.12
  968.7 81.2 all-gather.27
  1053.8 57.5 reduce-scatter.28
  1114.8 86.7 reduce-scatter.26
  1205.1 33.5 reduce-scatter.20
  1242.5 33.5 reduce-scatter.22
  1279.2 41.2 reduce-scatter.24
  1324.6 41.2 reduce-scatter.18
  1368.1 76.7 reduce-scatter.16
where the time goes:
time: 1490 us; the launch traced here: 1480 us
  waiting for transfers between devices  950 us (64%)
  matrix products  282 us (19%)
  local copies, waits for them, and re-layouts  95.6 us (6%)
  other arithmetic  72.8 us (5%)
  blocking collectives  64.9 us (4%)
  between operations  15.4 us (1%)
    reduce_scatter x1, waiting for transfers between devices, body(): lax.psum_scatter(contract_cols(lax.slice_in_dim(grad_gate_up, 0, token_ro...  133 us
    reduce_scatter x1, waiting for transfers between devices, body(): lax.psum_scatter(jnp.dot(lax.slice_in_dim(mixed, 0, token_rows * lax.axis...  133 us
    reduce_scatter x1, waiting for transfers between devices, body(): lax.psum_scatter(jnp.dot(lax.slice_in_dim(hidden, 0, token_rows * lax.axi...  77.7 us
    all_gather x1, waiting for transfers between devices, body(): lax.all_gather(normed2.astype(jnp.bfloat16), 'tensor', axis=0, tiled=True)  77.3 us
    reduce_scatter x1, waiting for transfers between devices, body(): lax.psum_scatter(contract_cols(grad_qkv, w_qkv).astype(jnp.bfloat16), 'te...  77.2 us
    all_gather x1, waiting for transfers between devices, body(): lax.all_gather(normed1.astype(jnp.bfloat16), 'tensor', axis=0, tiled=True)  76 us
    dot_general x36, matrix products, contract_rows(): lax.dot_general(left, right, (((0,), (0,)), ((), ())), preferred_element_...  75.3 us
    all_gather x1, waiting for transfers between devices, body(): piece_rows = lax.all_gather(cotangent, 'tensor', axis=0, tiled=True)  62 us
  transfers between devices with their start and end apart: 19, of which 15 were waited for; matrix products, arithmetic and copies ran while one was open for 26% of the time, Pallas kernels for 0%

commit v1 on v0

v1 whole, which is shorter than its diff:
```python
import functools
import math

import jax
import jax.numpy as jnp
from jax import lax
from jax.experimental import pallas as pl
from jax.experimental.pallas import tpu as pltpu
from jax.sharding import PartitionSpec as P

HD = 64
RATIO = 8
EPSILON = 1e-05
MASKED = -1e30
BF = jnp.bfloat16
F32 = jnp.float32


def dot_nn(left, right):
    return lax.dot_general(left, right, (((1,), (0,)), ((), ())), preferred_element_type=F32)


def dot_nt(left, right):
    return lax.dot_general(left, right, (((1,), (1,)), ((), ())), preferred_element_type=F32)


def dot_tn(left, right):
    return lax.dot_general(left, right, (((0,), (0,)), ((), ())), preferred_element_type=F32)


def rms_forward(values_in, gain_row):
    factor = lax.rsqrt(jnp.mean(values_in * values_in, axis=-1, keepdims=True) + EPSILON)
    return (values_in * factor * gain_row, factor)


def rms_backward(values_in, factor, gain_row, gradient):
    scaled = gain_row * gradient
    grad_gain = jnp.sum(gradient * values_in * factor, axis=0)
    grad_input = factor * scaled - values_in * (factor * factor * factor) * jnp.mean(
        scaled * values_in, axis=-1, keepdims=True
    )
    return (grad_input, grad_gain)


def rope_t(u, cos, sin):
    half = HD // 2
    return u * cos + jnp.concatenate([-u[half:], u[:half]], 0) * sin


def rope_back_t(w, cos, sin):
    half = HD // 2
    ws = w * sin
    return w * cos + jnp.concatenate([ws[half:], -ws[:half]], 0)


def bias_of(first, row0, keys, rows):
    key = lax.broadcasted_iota(jnp.int32, (keys, rows), 0)
    row = lax.broadcasted_iota(jnp.int32, (keys, rows), 1) + row0
    return jnp.where((key <= row) & (key >= first), 0.0, MASKED).astype(F32)


def attn_forward_kernel(row0_ref, a1_ref, wq_ref, kv_ref, cos_ref, sin_ref, first_ref, o_ref, q_ref, lse_ref, bias_ref, s_ref, vt_ref):
    keys, rows = bias_ref.shape

    @pl.when(pl.program_id(0) == 0)
    def _():
        bias_ref[...] = bias_of(first_ref[...], row0_ref[0], keys, rows)

    kv = kv_ref[0]
    kvt = kv.T
    vt_ref[...] = jnp.concatenate([kvt[HD:], jnp.ones((16, keys), BF)], 0)
    qt = dot_nn(a1_ref[...], wq_ref[0]).T
    cos, sin = cos_ref[...], sin_ref[...]
    for h in range(RATIO):
        q = (rope_t(qt[h * HD : (h + 1) * HD], cos, sin) * HD ** (-0.5)).astype(BF)
        q_ref[0, h * HD : (h + 1) * HD] = q
        s_ref[...] = dot_nn(kv, jnp.concatenate([q, jnp.zeros_like(q)], 0)) + bias_ref[...]
        peak = jnp.max(s_ref[...], axis=0, keepdims=True)
        e = jnp.exp(s_ref[...] - peak).astype(BF)
        ot = dot_nn(vt_ref[...], e)
        total = ot[HD : HD + 1]
        o_ref[0, h * HD : (h + 1) * HD] = (ot[:HD] / total).astype(BF)
        lse_ref[0, h : h + 1] = peak + jnp.log(total)


def attn_backward_kernel(row0_ref, q_ref, kv_ref, do_ref, o_ref, lse_ref, cos_ref, sin_ref, first_ref, dq_ref, dkv_ref, bias_ref, acc_ref):
    keys, rows = bias_ref.shape

    @pl.when(pl.program_id(0) == 0)
    def _():
        bias_ref[...] = bias_of(first_ref[...], row0_ref[0], keys, rows)

    kv = kv_ref[0]
    kt = kv.T[:HD]
    cos, sin = cos_ref[...], sin_ref[...]
    for h in range(RATIO):
        part = slice(h * HD, (h + 1) * HD)
        q, do, o = q_ref[0, part], do_ref[0, part], o_ref[0, part]
        qz = jnp.concatenate([q, jnp.zeros_like(q)], 0)
        doz = jnp.concatenate([jnp.zeros_like(do), do], 0)
        delta = jnp.sum(do.astype(F32) * o.astype(F32), axis=0, keepdims=True)
        p = jnp.exp(dot_nn(kv, qz) + bias_ref[...] - lse_ref[0, h : h + 1])
        ds = (p * (dot_nn(kv, doz) - delta)).astype(BF)
        grad = dot_nt(ds, qz) + dot_nt(p.astype(BF), doz)
        if h == 0:
            acc_ref[...] = grad
        else:
            acc_ref[...] += grad
        dq = dot_nn(kt, ds) * HD ** (-0.5)
        dq_ref[0, part] = rope_back_t(dq, cos, sin).astype(BF)
    dkv_ref[0] = acc_ref[...]


def params():
    return pltpu.CompilerParams(vmem_limit_bytes=56 * 2**20)


def attn_forward(row0, a1, wq, kv, cos, sin, first):
    groups, width, cols = wq.shape
    rows, keys = a1.shape[0], kv.shape[1]
    whole = lambda *shape: pl.BlockSpec(shape, lambda i: (0,) * len(shape))
    part = lambda *shape: pl.BlockSpec((1,) + shape, lambda i: (i,) + (0,) * len(shape))
    return pl.pallas_call(
        attn_forward_kernel,
        grid=(groups,),
        in_specs=[pl.BlockSpec(memory_space=pltpu.SMEM), whole(rows, width), part(width, cols), part(keys, 2 * HD), whole(HD, rows), whole(HD, rows), whole(1, rows)],
        out_specs=[part(cols, rows), part(cols, rows), part(RATIO, rows)],
        out_shape=[jax.ShapeDtypeStruct((groups, cols, rows), BF), jax.ShapeDtypeStruct((groups, cols, rows), BF), jax.ShapeDtypeStruct((groups, RATIO, rows), F32)],
        scratch_shapes=[pltpu.VMEM((keys, rows), F32), pltpu.VMEM((keys, rows), F32), pltpu.VMEM((HD + 16, keys), BF)],
        compiler_params=params(),
        name="attn_forward",
    )(row0, a1, wq, kv, cos, sin, first)


def attn_backward(row0, q, kv, do, o, lse, cos, sin, first):
    groups, cols, rows = q.shape
    keys = kv.shape[1]
    whole = lambda *shape: pl.BlockSpec(shape, lambda i: (0,) * len(shape))
    part = lambda *shape: pl.BlockSpec((1,) + shape, lambda i: (i,) + (0,) * len(shape))
    return pl.pallas_call(
        attn_backward_kernel,
        grid=(groups,),
        in_specs=[pl.BlockSpec(memory_space=pltpu.SMEM), part(cols, rows), part(keys, 2 * HD), part(cols, rows), part(cols, rows), part(RATIO, rows), whole(HD, rows), whole(HD, rows), whole(1, rows)],
        out_specs=[part(cols, rows), part(keys, 2 * HD)],
        out_shape=[jax.ShapeDtypeStruct((groups, cols, rows), BF), jax.ShapeDtypeStruct((groups, keys, 2 * HD), F32)],
        scratch_shapes=[pltpu.VMEM((keys, rows), F32), pltpu.VMEM((keys, 2 * HD), F32)],
        compiler_params=params(),
        name="attn_backward",
    )(row0, q, kv, do, o, lse, cos, sin, first)


MESH = pl.DeviceIdType.MESH
ANY = pl.BlockSpec(memory_space=pl.ANY)


class Place:
    def __init__(self):
        d, self.t = lax.axis_index("dp"), lax.axis_index("tensor")
        self.c, self.p = d % 2, d // 2
        x, y = self.p % 2, self.p // 2
        self.px, self.py, self.pd = self.p + 1 - 2 * x, self.p + 2 - 4 * y, 3 - self.p
        self.across = [self.t + 1 - 2 * (self.t % 2), (self.t + 2) % 4, 3 - self.t]
        self.order = [self.t] + self.across

    def at(self, p, c, t):
        return {"dp": p * 2 + c, "tensor": t}

    def x_side(self):
        return self.at(self.px, self.c, self.t)

    def y_side(self):
        return self.at(self.py, self.c, self.t)

    def twin(self):
        return self.at(self.p, 1 - self.c, self.t)

    def line(self, t):
        return self.at(self.p, self.c, t)

    def greet(self):
        barrier = pltpu.get_barrier_semaphore()
        others = [self.x_side(), self.y_side(), self.twin()] + [self.line(t) for t in self.across]
        for other in others:
            pl.semaphore_signal(barrier, inc=1, device_id=other, device_id_type=MESH)
        pl.semaphore_wait(barrier, len(others))


def half_of(ref, part):
    rows = ref.shape[0] // 2
    return ref.at[pl.ds(part * rows, rows)]


def gather_kernel(kv, wq, wo, wg, wu, wd, kv_out, q_out, o_out, g_out, u_out, d_out, z_send, z_recv, send, recv, local):
    me = Place()
    me.greet()
    sources = [kv, wq, wo, wg, wu, wd]
    outs = [kv_out, q_out, o_out, g_out, u_out, d_out]

    def piece(k, s, p, c):
        if k == 2:
            return o_out.at[p, c, s]
        return outs[k].at[s, p, c] if k < 2 else outs[k].at[p, c]

    def pair(k, s, c):
        if k == 2:
            return o_out.at[:, c, s]
        return outs[k].at[s, :, c] if k < 2 else outs[k].at[:, c]

    def remote(src, dst, send_sem, recv_sem, to):
        copy = pltpu.make_async_remote_copy(src, dst, send_sem, recv_sem, device_id=to, device_id_type=MESH)
        copy.start()
        return copy

    lines = {}
    for k in range(3):
        for j, z in enumerate(me.across):
            lines[k, j + 1] = remote(sources[k], piece(k, me.t, me.p, me.c), z_send.at[k, j], z_recv.at[k, j], me.line(z))
    items = [(k, j) for k in range(3) for j in range(4)] + [(k, 0) for k in range(3, 6)]
    going = {}

    def push(i, kind, src, dst, to):
        going[i, kind] = remote(src, dst, send.at[i, kind], recv.at[i, kind], to)

    def first(i):
        k, j = items[i]
        s = me.order[j]
        mine = piece(k, s, me.p, me.c)
        if j == 0:
            src = sources[k]
            going[i, "local"] = pltpu.make_async_copy(src, mine, local.at[i])
            going[i, "local"].start()
        else:
            lines[k, j].wait_recv()
            src = mine
        push(i, 0, src, mine, me.x_side())
        push(i, 1, src, mine, me.y_side())

    def second(i):
        k, j = items[i]
        s = me.order[j]
        going[i, 0].wait_recv()
        part = half_of(piece(k, s, me.px, me.c), 0)
        push(i, 2, part, part, me.y_side())
        going[i, 1].wait_recv()
        part = half_of(piece(k, s, me.py, me.c), 1)
        push(i, 3, part, part, me.x_side())

    def third(i):
        k, j = items[i]
        going[i, 2].wait_recv()
        going[i, 3].wait_recv()
        if (i, "local") in going:
            going[i, "local"].wait()
        part = pair(k, me.order[j], me.c)
        push(i, 4, part, part, me.twin())

    count = len(items)
    for tick in range(count + 4):
        if tick < count:
            first(tick)
        if 0 <= tick - 1 < count:
            second(tick - 1)
        if 0 <= tick - 2 < count:
            third(tick - 2)
        if 0 <= tick - 4 < count:
            going[tick - 4, 4].wait_recv()
    for copy in lines.values():
        copy.wait_send()
    for i in range(count):
        for kind in range(5):
            going[i, kind].wait_send()


def gather_weights(kv, wq, wo, wg, wu, wd):
    dma = pltpu.SemaphoreType.DMA
    shape = lambda lead, w: jax.ShapeDtypeStruct(lead + w.shape, BF)
    return pl.pallas_call(
        gather_kernel,
        out_shape=[shape((4, 4, 2), kv), shape((4, 4, 2), wq), shape((4, 2, 4), wo), shape((4, 2), wg), shape((4, 2), wu), shape((4, 2), wd)],
        in_specs=[ANY] * 6,
        out_specs=[ANY] * 6,
        scratch_shapes=[dma((3, 3)), dma((3, 3)), dma((15, 5)), dma((15, 5)), dma((15,))],
        compiler_params=pltpu.CompilerParams(collective_id=1, has_side_effects=True, vmem_limit_bytes=48 * 2**20),
        name="gather_weights",
    )(kv, wq, wo, wg, wu, wd)


def body(tokens, segments, attn_gain, w_query, w_key, w_value, w_out, mlp_gain, w_gate, w_up, w_down, cotangent):
    rows, width = tokens.shape
    hidden = w_gate.shape[1]
    nt = lax.axis_size("tensor")
    row0 = lax.axis_index("tensor") * rows
    keys = segments.shape[0]

    own_seg = lax.dynamic_slice_in_dim(segments, row0, rows)
    first = jnp.sum((segments[:, None] < own_seg[None, :]).astype(jnp.int32), axis=0)
    index = jnp.arange(rows, dtype=jnp.int32) + row0
    freq = jnp.exp(jnp.arange(HD // 2, dtype=F32) * (-2.0 * math.log(10000.0) / HD))
    angle = freq[:, None] * (index - first).astype(F32)[None, :]
    cos, sin = jnp.cos(angle), jnp.sin(angle)
    cos, sin = jnp.concatenate([cos, cos], 0), jnp.concatenate([sin, sin], 0)
    first = first[None, :]
    row0_s = row0[None].astype(jnp.int32)

    gain1 = lax.all_gather(attn_gain, "dp", axis=0, tiled=True).astype(F32)
    gain2 = lax.all_gather(mlp_gain, "dp", axis=0, tiled=True).astype(F32)
    w_kv = jnp.concatenate([w_key, w_value], 1)
    if lax.axis_size("dp") == 8 and nt == 4:
        wkv, wq, wo, wg, wu, wd = gather_weights(w_kv, w_query, w_out, w_gate, w_up, w_down)
        wkv, wq = wkv.reshape(4, width, -1), wq.reshape(4, width, -1)
        wo = wo.reshape(8, width, -1).transpose(1, 0, 2).reshape(width, width)
        wg, wu = wg.reshape(width, -1), wu.reshape(width, -1)
        wd = wd.reshape(8, hidden, -1).transpose(1, 0, 2).reshape(hidden, width)
    else:
        full = lambda w, axis: lax.all_gather(lax.all_gather(w, "dp", axis=axis, tiled=True), "tensor", axis=0)
        wq = full(w_query, 0)
        wkv = full(w_kv, 0)
        wo = full(w_out, 1).reshape(width, width)
        wg = lax.all_gather(w_gate, "dp", axis=0, tiled=True)
        wu = lax.all_gather(w_up, "dp", axis=0, tiled=True)
        wd = lax.all_gather(w_down, "dp", axis=1, tiled=True)

    x = tokens.astype(F32)
    n1, r1 = rms_forward(x, gain1)
    a1 = n1.astype(BF)
    kv = jnp.einsum("rd,gdc->grc", a1, wkv, preferred_element_type=F32)
    cos_r, sin_r = cos.T, sin.T
    k = kv[..., :HD]
    k = k * cos_r + jnp.concatenate([-k[..., HD // 2 :], k[..., : HD // 2]], -1) * sin_r
    kv = jnp.concatenate([k, kv[..., HD:]], -1).astype(BF)
    kv = lax.all_gather(kv, "tensor", axis=1, tiled=True)
    o, q, lse = attn_forward(row0_s, a1, wq, kv, cos, sin, first)
    o2 = o.reshape(-1, rows)
    h = x + dot_tn(o2, wo)

    n2, r2 = rms_forward(h, gain2)
    a2 = lax.all_gather(n2.astype(BF), "tensor", axis=0, tiled=True)
    cot = lax.all_gather(cotangent, "tensor", axis=0, tiled=True)
    g, u = dot_nn(a2, wg), dot_nn(a2, wu)
    sig = jax.nn.sigmoid(g)
    act = g * sig
    z = (act * u).astype(BF)
    scatter = lambda v: lax.psum_scatter(v.astype(BF), "tensor", scatter_dimension=0, tiled=True).astype(F32)
    output = (h + scatter(dot_nn(z, wd))).astype(BF)
    dz = dot_nt(cot, wd)
    dg = (dz * u * (sig * (1.0 + g * (1.0 - sig)))).astype(BF)
    du = (dz * act).astype(BF)
    gd_part = dot_tn(z, cot)
    gg_part = dot_tn(a2, dg)
    gu_part = dot_tn(a2, du)
    da2 = scatter(dot_nt(dg, wg) + dot_nt(du, wu))
    dres, gain2_part = rms_backward(h, r2, gain2, da2)
    dh = cotangent.astype(F32) + dres
    dhb = dh.astype(BF)

    do = dot_nt(wo, dhb).astype(BF).reshape(o.shape)
    go_part = dot_nn(o2, dhb)
    dq, dkv = attn_backward(row0_s, q, kv, do, o, lse, cos, sin, first)
    groups = dkv.shape[0]
    dkv = lax.psum_scatter(dkv.astype(BF), "tensor", scatter_dimension=1, tiled=True).astype(F32)
    dk = dkv[..., :HD]
    ws = dk * sin_r
    dk = dk * cos_r + jnp.concatenate([ws[..., HD // 2 :], -ws[..., : HD // 2]], -1)
    dkv = jnp.concatenate([dk, dkv[..., HD:]], -1).astype(BF)
    gq_part = jnp.einsum("rd,gcr->gdc", a1, dq, preferred_element_type=F32)
    gkv_part = jnp.einsum("rd,grc->gdc", a1, dkv, preferred_element_type=F32)
    da1 = jnp.einsum("gcr,gdc->rd", dq, wq, preferred_element_type=F32) + jnp.einsum("grc,gdc->rd", dkv, wkv, preferred_element_type=F32)
    din, gain1_part = rms_backward(x, r1, gain1, da1)
    grad_tokens = dh + din

    def home(v, dim):
        v = lax.psum_scatter(v.astype(BF), "dp", scatter_dimension=dim, tiled=True)
        return v

    def home_all(v, dim):
        return lax.psum_scatter(home(v, dim + 1), "tensor", scatter_dimension=0, tiled=False).astype(F32)

    gq = home_all(gq_part, 0)
    gkv = home_all(gkv_part, 0)
    go = home_all(go_part.reshape(nt, -1, width), 1)
    gg, gu = home(gg_part, 0).astype(F32), home(gu_part, 0).astype(F32)
    gd = home(gd_part, 1).astype(F32)
    gains = lax.psum_scatter(jnp.stack([gain1_part, gain2_part]), "dp", scatter_dimension=1, tiled=True)
    gains = lax.psum(gains, "tensor")
    return (output, grad_tokens, gains[0], gq, gkv[:, :HD], gkv[:, HD:], go, gains[1], gg, gu, gd)


def solution(mesh):
    rows, block = P(("dp", "tensor"), None), P("dp", "tensor")
    turned, line = P("tensor", "dp"), P("dp")
    return jax.shard_map(
        body,
        mesh=mesh,
        in_specs=(rows, line, line, block, block, block, turned, line, block, block, turned, rows),
        out_specs=(rows, rows, line, block, block, block, turned, line, block, block, turned),
        check_vma=False,
    )
```

time: 1490 us -> 1190 us (0.80)
  waiting for transfers between devices: 950 us -> 716 us
  Pallas kernels: 0 us -> 213 us
  matrix products: 282 us -> 142 us
  local copies, waits for them, and re-layouts: 95.6 us -> 37.9 us
  other arithmetic: 72.8 us -> 29.2 us
  blocking collectives: 64.9 us -> 30.8 us
    all_gather x9 -> x3, waiting for transfers between devices: 393 us -> 142 us  [the longest x1 71 us: body(): a2 = lax.all_gather(n2.astype(BF), 'tensor', axis=0, tiled=True)]
    pallas_call x0 -> x3, Pallas kernels: none -> 213 us  [the longest x1 161 us: gather_weights(): pl.pallas_call(gather_kernel, out_shape=[shape((4, 4, 2), kv), shape((4,...]
    dot_general x124 -> x17, matrix products: 282 us -> 142 us  [the longest x4 45.3 us: dot_nt(): lax.dot_general(left, right, (((1,), (1,)), ((), ())), preferred_element_...]
    unnamed x19 -> x17, waiting for transfers between devices: 4.51 us -> 36.5 us
    another operation x19 -> x0, local copies, waits for them, and re-layouts: 26.5 us -> none
    all_gather x4 -> x2, blocking collectives: 39.2 us -> 19.1 us  [the longest x1 10.3 us: body(): gain1 = lax.all_gather(attn_gain, 'dp', axis=0, tiled=True).astype(F32)]
    reduce_scatter x10 -> x12, waiting for transfers between devices: 553 us -> 537 us  [the longest x6 307 us: home(): v = lax.psum_scatter(v.astype(BF), 'dp', scatter_dimension=dim, tiled=True)]
  transfers between devices with their start and end apart: 19 -> 16, of which waited for: 15 -> 15; matrix products, arithmetic and copies ran while one was open for 26% -> 11% of each run, Pallas kernels for 0% -> 0%
where the time goes in v1:
time: 1190 us; the launch traced here: 1180 us
  waiting for transfers between devices  716 us (60%)
  Pallas kernels  213 us (18%)
  matrix products  142 us (12%)
  local copies, waits for them, and re-layouts  37.9 us (3%)
  blocking collectives  30.8 us (3%)
  other arithmetic  29.2 us (2%)
  between operations  14.7 us (1%)
    reduce_scatter x6, waiting for transfers between devices, home(): v = lax.psum_scatter(v.astype(BF), 'dp', scatter_dimension=dim, tiled=True)  307 us
    pallas_call x1, Pallas kernels, gather_weights(): pl.pallas_call(gather_kernel, out_shape=[shape((4, 4, 2), kv), shape((4,...  161 us
    reduce_scatter x2, waiting for transfers between devices, body(): lax.psum_scatter(v.astype(BF), 'tensor', scatter_dimension=0, tiled=True)  142 us
    all_gather x1, waiting for transfers between devices, body(): a2 = lax.all_gather(n2.astype(BF), 'tensor', axis=0, tiled=True)  71 us
    reduce_scatter x3, waiting for transfers between devices, home_all(): lax.psum_scatter(home(v, dim + 1), 'tensor', scatter_dimension=0, tiled=F...  60.8 us
    all_gather x1, waiting for transfers between devices, body(): cot = lax.all_gather(cotangent, 'tensor', axis=0, tiled=True)  58.8 us
    dot_general x4, matrix products, dot_nt(): lax.dot_general(left, right, (((1,), (1,)), ((), ())), preferred_element_...  45.3 us
    dot_general x4, matrix products, dot_tn(): lax.dot_general(left, right, (((0,), (0,)), ((), ())), preferred_element_...  38.9 us
  transfers between devices with their start and end apart: 16, of which 15 were waited for; matrix products, arithmetic and copies ran while one was open for 11% of the time, Pallas kernels for 0%

profile of v1, /device:TPU:0, one launch (start us, length us, event | category | flops | bytes accessed | tf_op | source)
XLA Modules:
  0.0 1185.0 jit_solution(1286141789928459115)
XLA Ops:
  24.0 161.2 %gather_weights.1 = (bf16[4,4,2,256,128]{4,3,2,1,0:T(8,128)(2,1)S(1)}, bf16[4,4,2,256,512]{4,3,2,1,0:T(8,128)(2,1)}, bf16[4,2,4,512,256]{4,3,2,1,0:T(8,128)(2,1)...) custom-call(bf16[256,128]{1,0:T(8,128)(2,1)S(1)} %pad_maximum_fusion.2.kv,, ...), custom_call_target="tpu_custom_call" | custom-call | tf_op jit(solution)/shard_map/gather_weights/pallas_call | solution.py:277
  199.0 11.6 copy.63
  210.6 12.0 %all-gather.6.cloned.1.call-done.kv_ref = bf16[4,1024,128]{2,1,0:T(8,128)(2,1)} async-done(((bf16[4,256,128]{2,1,0:T(8,128)(2,1)}), bf16[4,1024,128]{2,1,0:T(8,128)(2,1)}) %all-gather.6.cloned.1.call-update) | async-done | bytes 1048592 | tf_op jit(solution)/shard_map/all_gather | solution.py:331
  222.6 27.1 %attn_forward.1 = (bf16[4,512,256]{2,1,0:T(8,128)(2,1)}, bf16[4,512,256]{2,1,0:T(8,128)(2,1)}, f32[4,8,256]{2,1,0:T(8,128)}) custom-call(s32[1]{0:T(128)} %bitcast.row0_ref, bf16[256,2048]{1,0:T(8,128)(2,1)} %copy-done.10, bf16[4,2048,512]{2,1,0:T(8,128)(2,1)} %bitcast.98, bf16[4,1024,128]{2,1,0:T(8,128)(2,1)} %all-gather.6.cloned.1.call-done.kv_ref, ...), custom_call_target="tpu_custom_call" | custom-call | tf_op jit(solution)/shard_map/attn_forward/pallas_call | solution.py:123
  266.6 71.0 %all-gather.8.cloned.1.call-done = bf16[1024,2048]{1,0:T(8,128)(2,1)} async-done(((bf16[256,2048]{1,0:T(8,128)(2,1)}), bf16[1024,2048]{1,0:T(8,128)(2,1)}) %all-gather.8.cloned.1.call-update) | async-done | bytes 4194320 | tf_op jit(solution)/shard_map/all_gather | solution.py:337
  337.7 11.8 fusion.40
  359.8 58.8 %all-gather.10.cloned.1.call-done = bf16[1024,2048]{1,0:T(8,128)(2,1)} async-done(((bf16[256,2048]{1,0:T(8,128)(2,1)}), bf16[1024,2048]{1,0:T(8,128)(2,1)}) %all-gather.10.cloned.1.call-update) | async-done | bytes 4194320 | tf_op jit(solution)/shard_map/all_gather | solution.py:338
  418.6 15.4 %fusion.2 = (bf16[1024,1408]{1,0:T(8,128)(2,1)S(1)}, bf16[1024,1408]{1,0:T(8,128)(2,1)S(1)}, bf16[1024,1408]{1,0:T(8,128)(2,1)}) fusion(f32[1024,1408]{1,0:T(8,128)} %fusion.39, f32[1024,1408]{1,0:T(8,128)} %fusion.40, bf16[1024,2048]{1,0:T(8,128)(2,1)} %all-gather.10.cloned.1.call-done, bf16[1408,2048]{0,1:T(8,128)(2,1)} %bitcast.104), kind=kOutput, calls=%fused_computation.9 | convolution fusion | flops 5927206912 | bytes 30146560 | tf_op jit(solution)/shard_map/dot_general | solution.py:24
  444.8 11.4 add_convert_fusion
  456.3 11.0 convolution_convert_fusion.4
  467.4 64.3 %reduce-scatter.18.cloned.1.call-done = bf16[256,2048]{1,0:T(8,128)(2,1)} async-done(((bf16[1024,2048]{1,0:T(8,128)(2,1)}), bf16[256,2048]{1,0:T(8,128)(2,1)}) %reduce-scatter.18.cloned.1.call-update) | async-done | bytes 1048592 | tf_op jit(solution)/shard_map/reduce_scatter | solution.py:343
  533.6 77.7 %reduce-scatter.16.cloned.1.call-done = bf16[256,2048]{1,0:T(8,128)(2,1)} async-done(((bf16[1024,2048]{1,0:T(8,128)(2,1)}), bf16[256,2048]{1,0:T(8,128)(2,1)}) %reduce-scatter.16.cloned.1.call-update) | async-done | bytes 1048592 | tf_op jit(solution)/shard_map/reduce_scatter | solution.py:343
  622.2 25.0 %attn_backward.1 = (bf16[4,512,256]{2,1,0:T(8,128)(2,1)}, f32[4,1024,128]{2,1,0:T(8,128)}) custom-call(s32[1]{0:T(128)} %bitcast.row0_ref, bf16[4,512,256]{2,1,0:T(8,128)(2,1)} %get-tuple-element.29.q_ref, bf16[4,1024,128]{2,1,0:T(8,128)(2,1)} %all-gather.6.cloned.1.call-done.kv_ref, bf16[4,512,256]{2,1,0:T(8,128)(2,1)} %bitcast.107, ...), custom_call_target="tpu_custom_call" | custom-call | tf_op jit(solution)/shard_map/attn_backward/pallas_call | solution.py:140
  650.0 27.7 %reduce-scatter.20.cloned.1.call-done = bf16[4,256,128]{2,1,0:T(8,128)(2,1)} async-done(((bf16[4,1024,128]{2,1,0:T(8,128)(2,1)}), bf16[4,256,128]{2,1,0:T(8,128)(2,1)}) %reduce-scatter.20.cloned.1.call-update) | async-done | bytes 262160 | tf_op jit(solution)/shard_map/reduce_scatter | solution.py:360
  696.8 10.9 convolution_convert_fusion
  747.7 48.7 %reduce-scatter.22.cloned.1.call-done = bf16[4,256,512]{1,2,0:T(8,128)(2,1)} async-done(((bf16[4,2048,512]{1,2,0:T(8,128)(2,1)}), bf16[4,256,512]{1,2,0:T(8,128)(2,1)}) %reduce-scatter.22.cloned.1.call-update) | async-done | bytes 1048592 | tf_op jit(solution)/shard_map/reduce_scatter | solution.py:372
  796.5 75.1 %reduce-scatter.30.cloned.1.call-done = bf16[4,512,256]{2,1,0:T(8,128)(2,1)} async-done(((bf16[4,512,2048]{2,1,0:T(8,128)(2,1)}), bf16[4,512,256]{2,1,0:T(8,128)(2,1)}) %reduce-scatter.30.cloned.1.call-update) | async-done | bytes 1048592 | tf_op jit(solution)/shard_map/reduce_scatter | solution.py:372
  871.7 62.3 %reduce-scatter.38.cloned.1.call-done = bf16[1408,256]{1,0:T(8,128)(2,1)} async-done(((bf16[1408,2048]{1,0:T(8,128)(2,1)}), bf16[1408,256]{1,0:T(8,128)(2,1)}) %reduce-scatter.38.cloned.1.call-update) | async-done | bytes 720912 | tf_op jit(solution)/shard_map/reduce_scatter | solution.py:372
  936.3 60.6 %reduce-scatter.36.cloned.1.call-done = bf16[256,1408]{1,0:T(8,128)(2,1)} async-done(((bf16[2048,1408]{1,0:T(8,128)(2,1)}), bf16[256,1408]{1,0:T(8,128)(2,1)}) %reduce-scatter.36.cloned.1.call-update) | async-done | bytes 720912 | tf_op jit(solution)/shard_map/reduce_scatter | solution.py:372
  999.2 60.1 %reduce-scatter.34.cloned.1.call-done = bf16[256,1408]{1,0:T(8,128)(2,1)} async-done(((bf16[2048,1408]{1,0:T(8,128)(2,1)}), bf16[256,1408]{1,0:T(8,128)(2,1)}) %reduce-scatter.34.cloned.1.call-update) | async-done | bytes 720912 | tf_op jit(solution)/shard_map/reduce_scatter | solution.py:372
  1063.7 35.1 %reduce-scatter.40.cloned.1.call-done = f32[256,2]{1,0:T(8,128)} async-done(((f32[2048,2]{1,0:T(8,128)}), f32[256,2]{1,0:T(8,128)}) %reduce-scatter.40.cloned.1.call-update) | async-done | bytes 2064
  1099.8 11.7 psum.7
  1122.2 26.1 %reduce-scatter.24.cloned.1.call-done = bf16[1,256,512]{1,2,0:T(8,128)(2,1)} async-done(((bf16[4,256,512]{1,2,0:T(8,128)(2,1)}), bf16[1,256,512]{1,2,0:T(8,128)(2,1)}) %reduce-scatter.24.cloned.1.call-update) | async-done | bytes 262160 | tf_op jit(solution)/shard_map/reduce_scatter | solution.py:376
  1150.3 26.1 %reduce-scatter.32.cloned.1.call-done = bf16[1,512,256]{2,1,0:T(8,128)(2,1)} async-done(((bf16[4,512,256]{2,1,0:T(8,128)(2,1)}), bf16[1,512,256]{2,1,0:T(8,128)(2,1)}) %reduce-scatter.32.cloned.1.call-update) | async-done | bytes 262160 | tf_op jit(solution)/shard_map/reduce_scatter | solution.py:376
  (165 shorter events, 167.2 us)
Async XLA Ops:
  7.2 215.3 %all-gather.6.cloned.1.call-start = ((), (), s32[]{:S(2)}) async-start(), calls=%async_computation.13 | async-start | bytes 1310720 | tf_op jit(solution)/shard_map/all_gather | solution.py:331
  10.2 177.1 %copy-start.24 = (f32[256]{0:T(256)}, f32[256]{0:T(256)S(1)}, u32[]{:S(2)}) copy-start(f32[256]{0:T(256)S(1)} %get-tuple-element.101) | copy-start | bytes 3076
  20.5 166.7 %copy-start.21 = (f32[8,1,256]{2,1,0:T(1,128)}, f32[8,1,256]{2,1,0:T(1,128)S(1)}, u32[]{:S(2)}) copy-start(f32[8,1,256]{2,1,0:T(1,128)S(1)} %convert_element_type.154) | copy-start | bytes 24580
  24.0 163.3 %copy-start.10 = (bf16[256,2048]{1,0:T(8,128)(2,1)}, bf16[256,2048]{1,0:T(8,128)(2,1)S(1)}, u32[]{:S(2)}) copy-start(bf16[256,2048]{1,0:T(8,128)(2,1)S(1)} %fusion.15.a1_ref) | copy-start | bytes 3145732
  190.2 147.5 %all-gather.8.cloned.1.call-start = ((), (), s32[]{:S(2)}) async-start(), calls=%async_computation.14 | async-start | bytes 5242880 | tf_op jit(solution)/shard_map/all_gather | solution.py:337
  222.6 27.1 %copy-start.12 = (bf16[256,2048]{1,0:T(8,128)(2,1)S(1)}, bf16[256,2048]{1,0:T(8,128)(2,1)}, u32[]{:S(2)}) copy-start(bf16[256,2048]{1,0:T(8,128)(2,1)} %param.12) | copy-start | bytes 3145732
  257.2 161.3 %all-gather.10.cloned.1.call-start = ((), (), s32[]{:S(2)}) async-start(), calls=%async_computation.16 | async-start | bytes 5242880 | tf_op jit(solution)/shard_map/all_gather | solution.py:338
  258.0 273.7 %reduce-scatter.18.cloned.1.call-start = ((), (), s32[]{:S(2)}) async-start(), calls=%async_computation.17 | async-start | bytes 5242880 | tf_op jit(solution)/shard_map/reduce_scatter | solution.py:343
  456.2 155.0 %reduce-scatter.16.cloned.1.call-start = ((), (), s32[]{:S(2)}) async-start(), calls=%async_computation.15 | async-start | bytes 5242880 | tf_op jit(solution)/shard_map/reduce_scatter | solution.py:343
  467.3 144.0 %copy-start.17 = (bf16[256,2048]{1,0:T(8,128)(2,1)S(1)}, bf16[256,2048]{1,0:T(8,128)(2,1)}, u32[]{:S(2)}) copy-start(bf16[256,2048]{1,0:T(8,128)(2,1)} %param.23) | copy-start | bytes 3145732
  467.3 210.4 %reduce-scatter.20.cloned.1.call-start = ((), (), s32[]{:S(2)}) async-start(), calls=%async_computation.18 | async-start | bytes 1310720 | tf_op jit(solution)/shard_map/reduce_scatter | solution.py:360
  649.9 29.4 %copy-start.11 = (bf16[256,2048]{1,0:T(8,128)(2,1)S(1)}, bf16[256,2048]{1,0:T(8,128)(2,1)}, u32[]{:S(2)}) copy-start(bf16[256,2048]{1,0:T(8,128)(2,1)} %copy-done.10) | copy-start | bytes 3145732
  649.9 97.2 %reduce-scatter.26.cloned.1.call-start = ((), (), s32[]{:S(2)}) async-start(), calls=%async_computation.21 | async-start | bytes 2359296 | tf_op jit(solution)/shard_map/reduce_scatter | solution.py:372
  681.6 114.8 %reduce-scatter.22.cloned.1.call-start = ((), (), s32[]{:S(2)}) async-start(), calls=%async_computation.19 | async-start | bytes 9437184 | tf_op jit(solution)/shard_map/reduce_scatter | solution.py:372
  687.3 184.3 %reduce-scatter.30.cloned.1.call-start = ((), (), s32[]{:S(2)}) async-start(), calls=%async_computation.23 | async-start | bytes 9437184 | tf_op jit(solution)/shard_map/reduce_scatter | solution.py:372
  695.0 239.0 %reduce-scatter.38.cloned.1.call-start = ((), (), s32[]{:S(2)}) async-start(), calls=%async_computation.27 | async-start | bytes 6488064 | tf_op jit(solution)/shard_map/reduce_scatter | solution.py:372
  707.7 289.2 %reduce-scatter.36.cloned.1.call-start = ((), (), s32[]{:S(2)}) async-start(), calls=%async_computation.26 | async-start | bytes 6488064 | tf_op jit(solution)/shard_map/reduce_scatter | solution.py:372
  720.4 338.9 %reduce-scatter.34.cloned.1.call-start = ((), (), s32[]{:S(2)}) async-start(), calls=%async_computation.25 | async-start | bytes 6488064 | tf_op jit(solution)/shard_map/reduce_scatter | solution.py:372
  733.1 365.7 %reduce-scatter.40.cloned.1.call-start = ((), (), s32[]{:S(2)}) async-start(), calls=%async_computation.28 | async-start | bytes 1179648
  747.1 373.6 %reduce-scatter.28.cloned.1.call-start = ((), (), s32[]{:S(2)}) async-start(), calls=%async_computation.22 | async-start | bytes 327680 | tf_op jit(solution)/shard_map/reduce_scatter | solution.py:376
  747.7 400.6 %reduce-scatter.24.cloned.1.call-start = ((), (), s32[]{:S(2)}) async-start(), calls=%async_computation.20 | async-start | bytes 1310720 | tf_op jit(solution)/shard_map/reduce_scatter | solution.py:376
  796.5 379.9 %reduce-scatter.32.cloned.1.call-start = ((), (), s32[]{:S(2)}) async-start(), calls=%async_computation.24 | async-start | bytes 1310720 | tf_op jit(solution)/shard_map/reduce_scatter | solution.py:376
  871.6 190.1 %copy-start.9 = (f32[256,2048]{1,0:T(8,128)S(1)}, f32[256,2048]{1,0:T(8,128)}, u32[]{:S(2)}) copy-start(f32[256,2048]{1,0:T(8,128)} %copy-done.7) | copy-start | bytes 6291460
  871.7 190.1 %copy-start.27 = (f32[256]{0:T(256)S(1)}, f32[256]{0:T(256)}, u32[]{:S(2)}) copy-start(f32[256]{0:T(256)} %get-tuple-element.100) | copy-start | bytes 3076
  (27 other events, 185.6 us)
Sparse Core Ops, SparseCore 0:
  190.3 32.2 all-gather.5
  257.4 80.2 all-gather.7
  339.2 79.2 all-gather.9
  456.4 75.2 reduce-scatter.17
  533.9 77.2 reduce-scatter.15
  650.0 27.6 reduce-scatter.19
  681.7 39.8 reduce-scatter.25
  725.1 71.2 reduce-scatter.21
  800.3 71.2 reduce-scatter.29
  874.9 59.0 reduce-scatter.37
  937.8 59.0 reduce-scatter.35
  1000.2 59.0 reduce-scatter.33
  1062.8 35.9 reduce-scatter.39
  1101.0 19.5 reduce-scatter.27
  1122.8 25.4 reduce-scatter.23
  1150.5 25.8 reduce-scatter.31

commit v2 on v1

--- a/solution.py
+++ b/solution.py
@@ -285,6 +285,246 @@
     )(kv, wq, wo, wg, wu, wd)
 
 
+def xor4(a, m):
+    return (a // 2 + m // 2) % 2 * 2 + (a % 2 + m % 2) % 2
+
+
+def copy_to(src, dst, send_sem, recv_sem, to):
+    return pltpu.make_async_remote_copy(src, dst, send_sem, recv_sem, device_id=to, device_id_type=MESH)
+
+
+def add_low(left, right):
+    return (left.astype(F32) + right.astype(F32)).astype(BF)
+
+
+def mlp_kernel(a2_in, ct_in, wg_in, wu_in, wd_in, da2_out, mo_out, gg_out, gu_out, gd_out, twin_g, twin_u, twin_d, wg, wu, wd, a2_buf, ct_buf, mo_buf, a2_col, ct_col, zt, dg, du, out_buf, in_buf, diag_gu, x_gu, y_gu, diag_d, x_d, y_d, stage_gu, stage_d, load, store, line_send, line_recv, twin_send, twin_recv, send, recv, stage_sem):
+    me = Place()
+    rows, width = da2_out.shape
+    hidden = wg.shape[1]
+    cols = width // 8
+    weights = [pltpu.make_async_copy(wg_in, wg, load.at[4]), pltpu.make_async_copy(wu_in, wu, load.at[5])]
+    weights += [pltpu.make_async_copy(wd_in.at[d], wd.at[:, pl.ds(d * cols, cols)], load.at[6 + d]) for d in range(8)]
+    for copy in weights:
+        copy.start()
+
+    def chunk_load(j, slot):
+        s = xor4(me.t, 3 - j)
+        return pltpu.make_async_copy(a2_in.at[s], a2_buf.at[slot], load.at[slot]), pltpu.make_async_copy(ct_in.at[s], ct_buf.at[slot], load.at[2 + slot])
+
+    def chunk_send(j):
+        return copy_to(out_buf.at[j], in_buf.at[2 - j], line_send.at[j], line_recv.at[2 - j], me.line(xor4(me.t, 3 - j)))
+
+    def mo_store(j, slot):
+        return pltpu.make_async_copy(mo_buf.at[slot], mo_out.at[xor4(me.t, 3 - j)], store.at[slot])
+
+    for copy in chunk_load(0, 0):
+        copy.start()
+    me.greet()
+    for copy in weights:
+        copy.wait()
+
+    def chunk(j, _):
+        slot = j % 2
+
+        @pl.when(j < 3)
+        def _():
+            for copy in chunk_load(j + 1, 1 - slot):
+                copy.start()
+
+        for copy in chunk_load(j, slot):
+            copy.wait()
+        where = pl.multiple_of(xor4(me.t, 3 - j) * rows, rows)
+        g, u = dot_nn(a2_buf[slot], wg[...]), dot_nn(a2_buf[slot], wu[...])
+        dz = dot_nt(ct_buf[slot], wd[...])
+        sig = 1.0 / (1.0 + jnp.exp(-g))
+        act = g * sig
+        z = (act * u).astype(BF)
+        zt[:, pl.ds(where, rows)] = z.T
+        dg_now = (dz * u * (sig * (1.0 + g * (1.0 - sig)))).astype(BF)
+        du_now = (dz * act).astype(BF)
+        dg[pl.ds(where, rows)] = dg_now
+        du[pl.ds(where, rows)] = du_now
+        part = dot_nt(dg_now, wg[...]) + dot_nt(du_now, wu[...])
+
+        @pl.when(j < 3)
+        def _():
+            out_buf[j] = part.astype(BF)
+            chunk_send(j).start()
+
+        @pl.when(j == 3)
+        def _():
+            da2_out[...] = part
+
+        @pl.when(j >= 2)
+        def _():
+            mo_store(j - 2, slot).wait()
+
+        mo_buf[slot] = dot_nn(z, wd[...]).astype(BF)
+        mo_store(j, slot).start()
+        return 0
+
+    lax.fori_loop(0, 4, chunk, 0)
+    mo_store(2, 0).wait()
+    mo_store(3, 1).wait()
+
+    def owner(i):
+        return xor4(me.p, 3 - i % 4) * 2 + (1 - me.c + i // 4) % 2
+
+    def tile_load(i, slot):
+        at = pl.ds(pl.multiple_of(owner(i) * cols, cols), cols)
+        return pltpu.make_async_copy(a2_in.at[:, :, at], a2_col.at[slot], load.at[slot]), pltpu.make_async_copy(ct_in.at[:, :, at], ct_col.at[slot], load.at[2 + slot])
+
+    def piece(k, p, c):
+        at = pl.ds(pl.multiple_of((p * 2 + c) * cols, cols), cols)
+        return (wg, wu)[k].at[at] if k < 2 else wd.at[:, at]
+
+    twins = [twin_g, twin_u, twin_d]
+
+    def twin_push(k, i):
+        p = xor4(me.p, 3 - i)
+        return copy_to(piece(k, p, 1 - me.c), twins[k].at[p], twin_send.at[k, i], twin_recv.at[k, i], me.twin())
+
+    for copy in tile_load(0, 0):
+        copy.start()
+
+    def tile(i, _):
+        slot = i % 2
+
+        @pl.when(i < 7)
+        def _():
+            for copy in tile_load(i + 1, 1 - slot):
+                copy.start()
+
+        for copy in tile_load(i, slot):
+            copy.wait()
+        at = pl.ds(pl.multiple_of(owner(i) * cols, cols), cols)
+        a2t = a2_col[slot].reshape(4 * rows, cols).T
+        wg[at] = dot_nn(a2t, dg[...]).astype(BF)
+        wu[at] = dot_nn(a2t, du[...]).astype(BF)
+        wd[:, at] = dot_nn(zt[...], ct_col[slot].reshape(4 * rows, cols)).astype(BF)
+
+        @pl.when(i < 4)
+        def _():
+            for k in range(3):
+                twin_push(k, i).start()
+
+        return 0
+
+    lax.fori_loop(0, 8, tile, 0)
+
+    diag = [diag_gu.at[0], diag_gu.at[1], diag_d]
+    from_x = [x_gu.at[0], x_gu.at[1], x_d]
+    from_y = [y_gu.at[0], y_gu.at[1], y_d]
+    stage = [stage_gu.at[0], stage_gu.at[1], stage_d]
+
+    def side(k, kind):
+        if kind < 2:
+            src, dst = half_of(piece(k, me.pd, me.c), kind), half_of(diag[k], kind)
+        else:
+            src, dst = (piece(k, me.px, me.c), from_x[k]) if kind == 2 else (piece(k, me.py, me.c), from_y[k])
+        return copy_to(src, dst, send.at[k, kind], recv.at[k, kind], me.x_side() if kind % 2 == 0 else me.y_side())
+
+    steps = [(k, i) for i in range(4) for k in range(3)]
+
+    def fetch(n):
+        k, i = steps[n]
+        twin_push(k, i).wait_recv()
+        copy = pltpu.make_async_copy(twins[k].at[xor4(me.p, 3 - i)], stage[k], stage_sem.at[k])
+        copy.start()
+        return copy
+
+    def add_twin(n, copy):
+        k, i = steps[n]
+        copy.wait()
+        mine = piece(k, xor4(me.p, 3 - i), me.c)
+        mine[...] = add_low(mine[...], stage[k][...])
+        if i == 0:
+            side(k, 0).start()
+            side(k, 1).start()
+
+    ahead = fetch(0)
+    for n in range(12):
+        now = ahead
+        if n + 1 < 12:
+            ahead = fetch(n + 1)
+        add_twin(n, now)
+    for k in range(3):
+        side(k, 1).wait_recv()
+        part, extra = half_of(piece(k, me.px, me.c), 1), half_of(diag[k], 1)
+        part[...] = add_low(part[...], extra[...])
+        side(k, 2).start()
+        side(k, 0).wait_recv()
+        part, extra = half_of(piece(k, me.py, me.c), 0), half_of(diag[k], 0)
+        part[...] = add_low(part[...], extra[...])
+        side(k, 3).start()
+    results = []
+    for k in range(3):
+        side(k, 2).wait_recv()
+        side(k, 3).wait_recv()
+        mine = piece(k, me.p, me.c)
+        mine[...] = (mine[...].astype(F32) + from_x[k][...].astype(F32) + from_y[k][...].astype(F32)).astype(BF)
+        results.append(pltpu.make_async_copy(mine, (gg_out, gu_out, gd_out)[k], stage_sem.at[k]))
+        results[-1].start()
+    for j in range(3):
+        chunk_send(j).wait_recv()
+    da2_out[...] += in_buf[0].astype(F32) + in_buf[1].astype(F32) + in_buf[2].astype(F32)
+    for copy in results:
+        copy.wait()
+    for j in range(3):
+        chunk_send(j).wait_send()
+    for k in range(3):
+        for i in range(4):
+            twin_push(k, i).wait_send()
+            side(k, i).wait_send()
+
+
+def mlp(a2, ct, wg, wu, wd):
+    chunks, rows, width = a2.shape
+    hidden, cols = wg.shape[1], width // 8
+    dma, vmem = pltpu.SemaphoreType.DMA, lambda *shape: pltpu.VMEM(shape, BF)
+    shape = lambda *dims: jax.ShapeDtypeStruct(dims, BF)
+    return pl.pallas_call(
+        mlp_kernel,
+        out_shape=[jax.ShapeDtypeStruct((rows, width), F32), shape(4, rows, width), shape(cols, hidden), shape(cols, hidden), shape(hidden, cols), shape(4, cols, hidden), shape(4, cols, hidden), shape(4, hidden, cols)],
+        in_specs=[ANY] * 5,
+        out_specs=[pl.BlockSpec(memory_space=pltpu.VMEM)] + [ANY] * 7,
+        scratch_shapes=[
+            vmem(width, hidden), vmem(width, hidden), vmem(hidden, width),
+            vmem(2, rows, width), vmem(2, rows, width), vmem(2, rows, width),
+            vmem(2, 4, rows, cols), vmem(2, 4, rows, cols),
+            vmem(hidden, 4 * rows), vmem(4 * rows, hidden), vmem(4 * rows, hidden),
+            vmem(3, rows, width), vmem(3, rows, width),
+            vmem(2, cols, hidden), vmem(2, cols, hidden), vmem(2, cols, hidden),
+            vmem(hidden, cols), vmem(hidden, cols), vmem(hidden, cols),
+            vmem(2, cols, hidden), vmem(hidden, cols),
+            dma((14,)), dma((2,)), dma((3,)), dma((3,)), dma((3, 4)), dma((3, 4)), dma((3, 4)), dma((3, 4)), dma((3,)),
+        ],
+        compiler_params=pltpu.CompilerParams(collective_id=2, has_side_effects=True, vmem_limit_bytes=62 * 2**20),
+        name="mlp",
+    )(a2, ct, wg, wu, wd)[:5]
+
+
+def home(v, dim):
+    return lax.psum_scatter(v.astype(BF), "dp", scatter_dimension=dim, tiled=True)
+
+
+def mlp_plain(h, a2, cot, wg, wu, wd):
+    g, u = dot_nn(a2, wg), dot_nn(a2, wu)
+    sig = jax.nn.sigmoid(g)
+    act = g * sig
+    z = (act * u).astype(BF)
+    scatter = lambda v: lax.psum_scatter(v.astype(BF), "tensor", scatter_dimension=0, tiled=True).astype(F32)
+    output = (h + scatter(dot_nn(z, wd))).astype(BF)
+    dz = dot_nt(cot, wd)
+    dg = (dz * u * (sig * (1.0 + g * (1.0 - sig)))).astype(BF)
+    du = (dz * act).astype(BF)
+    gd = home(dot_tn(z, cot), 1).astype(F32)
+    gg = home(dot_tn(a2, dg), 0).astype(F32)
+    gu = home(dot_tn(a2, du), 0).astype(F32)
+    da2 = scatter(dot_nt(dg, wg) + dot_nt(du, wu))
+    return output, da2, gg, gu, gd
+
+
 def body(tokens, segments, attn_gain, w_query, w_key, w_value, w_out, mlp_gain, w_gate, w_up, w_down, cotangent):
     rows, width = tokens.shape
     hidden = w_gate.shape[1]
@@ -310,7 +550,7 @@
         wkv, wq = wkv.reshape(4, width, -1), wq.reshape(4, width, -1)
         wo = wo.reshape(8, width, -1).transpose(1, 0, 2).reshape(width, width)
         wg, wu = wg.reshape(width, -1), wu.reshape(width, -1)
-        wd = wd.reshape(8, hidden, -1).transpose(1, 0, 2).reshape(hidden, width)
+        wd8 = wd.reshape(8, hidden, -1)
     else:
         full = lambda w, axis: lax.all_gather(lax.all_gather(w, "dp", axis=axis, tiled=True), "tensor", axis=0)
         wq = full(w_query, 0)
@@ -336,19 +576,12 @@
     n2, r2 = rms_forward(h, gain2)
     a2 = lax.all_gather(n2.astype(BF), "tensor", axis=0, tiled=True)
     cot = lax.all_gather(cotangent, "tensor", axis=0, tiled=True)
-    g, u = dot_nn(a2, wg), dot_nn(a2, wu)
-    sig = jax.nn.sigmoid(g)
-    act = g * sig
-    z = (act * u).astype(BF)
-    scatter = lambda v: lax.psum_scatter(v.astype(BF), "tensor", scatter_dimension=0, tiled=True).astype(F32)
-    output = (h + scatter(dot_nn(z, wd))).astype(BF)
-    dz = dot_nt(cot, wd)
-    dg = (dz * u * (sig * (1.0 + g * (1.0 - sig)))).astype(BF)
-    du = (dz * act).astype(BF)
-    gd_part = dot_tn(z, cot)
-    gg_part = dot_tn(a2, dg)
-    gu_part = dot_tn(a2, du)
-    da2 = scatter(dot_nt(dg, wg) + dot_nt(du, wu))
+    if lax.axis_size("dp") == 8 and nt == 4:
+        da2, mo, gg, gu, gd = mlp(a2.reshape(4, rows, width), cot.reshape(4, rows, width), wg, wu, wd8)
+        output = (h + lax.psum_scatter(mo.reshape(4 * rows, width), "tensor", scatter_dimension=0, tiled=True).astype(F32)).astype(BF)
+        gg, gu, gd = gg.astype(F32), gu.astype(F32), gd.astype(F32)
+    else:
+        output, da2, gg, gu, gd = mlp_plain(h, a2, cot, wg, wu, wd)
     dres, gain2_part = rms_backward(h, r2, gain2, da2)
     dh = cotangent.astype(F32) + dres
     dhb = dh.astype(BF)
@@ -368,18 +601,12 @@
     din, gain1_part = rms_backward(x, r1, gain1, da1)
     grad_tokens = dh + din
 
-    def home(v, dim):
-        v = lax.psum_scatter(v.astype(BF), "dp", scatter_dimension=dim, tiled=True)
-        return v
-
     def home_all(v, dim):
         return lax.psum_scatter(home(v, dim + 1), "tensor", scatter_dimension=0, tiled=False).astype(F32)
 
     gq = home_all(gq_part, 0)
     gkv = home_all(gkv_part, 0)
     go = home_all(go_part.reshape(nt, -1, width), 1)
-    gg, gu = home(gg_part, 0).astype(F32), home(gu_part, 0).astype(F32)
-    gd = home(gd_part, 1).astype(F32)
     gains = lax.psum_scatter(jnp.stack([gain1_part, gain2_part]), "dp", scatter_dimension=1, tiled=True)
     gains = lax.psum(gains, "tensor")
     return (output, grad_tokens, gains[0], gq, gkv[:, :HD], gkv[:, HD:], go, gains[1], gg, gu, gd)

time: 1190 us -> 1000 us (0.84)
  waiting for transfers between devices: 716 us -> 496 us
  Pallas kernels: 213 us -> 362 us
  matrix products: 142 us -> 37.9 us
    reduce_scatter x8 -> x4, waiting for transfers between devices: 449 us -> 235 us  [the longest x3 164 us: home(): lax.psum_scatter(v.astype(BF), 'dp', scatter_dimension=dim, tiled=True)]
    pallas_call x0 -> x1, Pallas kernels: none -> 148 us  [mlp(): pl.pallas_call(mlp_kernel, out_shape=[jax.ShapeDtypeStruct((rows, width),...]
    dot_general x4 -> x1, matrix products: 45.3 us -> 7.73 us  [dot_nt(): lax.dot_general(left, right, (((1,), (1,)), ((), ())), preferred_element_...]
    dot_general x4 -> x1, matrix products: 38.9 us -> 6.3 us  [dot_tn(): lax.dot_general(left, right, (((0,), (0,)), ((), ())), preferred_element_...]
    dot_general x4 -> x1, matrix products: 38.7 us -> 6.91 us  [dot_nn(): lax.dot_general(left, right, (((1,), (0,)), ((), ())), preferred_element_...]
    all_gather x1, waiting for transfers between devices: 58.8 us -> 45.5 us  [body(): cot = lax.all_gather(cotangent, 'tensor', axis=0, tiled=True)]
    unnamed x17 -> x13, waiting for transfers between devices: 36.5 us -> 33.6 us
  transfers between devices with their start and end apart: 16 -> 12, of which waited for: 15 -> 12; matrix products, arithmetic and copies ran while one was open for 11% -> 6% of each run, Pallas kernels for 0% -> 3%
where the time goes in v2:
time: 1000 us; the launch traced here: 996 us
  waiting for transfers between devices  496 us (50%)
  Pallas kernels  362 us (36%)
  matrix products  37.9 us (4%)
  blocking collectives  30.8 us (3%)
  other arithmetic  27.9 us (3%)
  local copies, waits for them, and re-layouts  26.1 us (3%)
  between operations  14.9 us (1%)
    reduce_scatter x3, waiting for transfers between devices, home(): lax.psum_scatter(v.astype(BF), 'dp', scatter_dimension=dim, tiled=True)  164 us
    pallas_call x1, Pallas kernels, gather_weights(): pl.pallas_call(gather_kernel, out_shape=[shape((4, 4, 2), kv), shape((4,...  161 us
    pallas_call x1, Pallas kernels, mlp(): pl.pallas_call(mlp_kernel, out_shape=[jax.ShapeDtypeStruct((rows, width),...  148 us
    all_gather x1, waiting for transfers between devices, body(): a2 = lax.all_gather(n2.astype(BF), 'tensor', axis=0, tiled=True)  81.5 us
    reduce_scatter x1, waiting for transfers between devices, body(): lax.psum_scatter(mo.reshape(4 * rows, width), 'tensor', scatter_dimension...  70.9 us
    reduce_scatter x3, waiting for transfers between devices, home_all(): lax.psum_scatter(home(v, dim + 1), 'tensor', scatter_dimension=0, tiled=F...  60.9 us
    all_gather x1, waiting for transfers between devices, body(): cot = lax.all_gather(cotangent, 'tensor', axis=0, tiled=True)  45.5 us
    unnamed x13, waiting for transfers between devices  33.6 us
  transfers between devices with their start and end apart: 12, of which 12 were waited for; matrix products, arithmetic and copies ran while one was open for 6% of the time, Pallas kernels for 3%

profile of v2, /device:TPU:0, one launch (start us, length us, event | category | flops | bytes accessed | tf_op | source)
XLA Modules:
  0.0 996.0 jit_solution(16116417969833711107)
XLA Ops:
  10.2 10.3 %all-gather = bf16[8,1,256]{2,1,0:T(2,128)(2,1)S(1)} all-gather(bf16[1,1,256]{2,1,0:T(2,128)(2,1)S(1)} %reshape.137), channel_id=1, replica_groups=mesh['dp'=8,'tensor'=4] {'dp'}, dimensions={0}, use_global_device_ids=true | all-gather | bytes 4608 | tf_op jit(solution)/shard_map/all_gather | solution.py:545
  24.0 161.2 %gather_weights.1 = (bf16[4,4,2,256,128]{4,3,2,1,0:T(8,128)(2,1)S(1)}, bf16[4,4,2,256,512]{4,3,2,1,0:T(8,128)(2,1)}, bf16[4,2,4,512,256]{4,3,2,1,0:T(8,128)(2,1)...) custom-call(bf16[256,128]{1,0:T(8,128)(2,1)S(1)} %pad_maximum_fusion.2.kv,, ...), custom_call_target="tpu_custom_call" | custom-call | tf_op jit(solution)/shard_map/gather_weights/pallas_call | solution.py:277
  190.1 8.8 all-gather.1
  198.9 11.5 %copy.58 = bf16[8,2048,256]{1,2,0:T(8,128)(2,1)} copy(bf16[8,2048,256]{2,1,0:T(8,128)(2,1)} %bitcast.75) | data formatting | bytes 16777216 | tf_op jit(solution)/shard_map/reshape | solution.py:551
  210.4 11.3 %all-gather.6.cloned.1.call-done.kv_ref = bf16[4,1024,128]{2,1,0:T(8,128)(2,1)} async-done(((bf16[4,256,128]{2,1,0:T(8,128)(2,1)}), bf16[4,1024,128]{2,1,0:T(8,128)(2,1)}) %all-gather.6.cloned.1.call-update) | async-done | bytes 1048592 | tf_op jit(solution)/shard_map/all_gather | solution.py:571
  221.7 27.1 %attn_forward.1 = (bf16[4,512,256]{2,1,0:T(8,128)(2,1)}, bf16[4,512,256]{2,1,0:T(8,128)(2,1)}, f32[4,8,256]{2,1,0:T(8,128)}) custom-call(s32[1]{0:T(128)} %bitcast.row0_ref, bf16[256,2048]{1,0:T(8,128)(2,1)} %copy-done.12, bf16[4,2048,512]{2,1,0:T(8,128)(2,1)} %bitcast.71, bf16[4,1024,128]{2,1,0:T(8,128)(2,1)} %all-gather.6.cloned.1.call-done.kv_ref, ...), custom_call_target="tpu_custom_call" | custom-call | tf_op jit(solution)/shard_map/attn_forward/pallas_call | solution.py:123
  248.8 6.3 multiply_reduce_fusion.2
  258.0 45.5 %all-gather.10.cloned.1.call-done = bf16[1024,2048]{1,0:T(8,128)(2,1)} async-done(((bf16[256,2048]{1,0:T(8,128)(2,1)}), bf16[1024,2048]{1,0:T(8,128)(2,1)}) %all-gather.10.cloned.1.call-update) | async-done | bytes 4194320 | tf_op jit(solution)/shard_map/all_gather | solution.py:578
  303.6 81.5 %all-gather.8.cloned.1.call-done = bf16[1024,2048]{1,0:T(8,128)(2,1)} async-done(((bf16[256,2048]{1,0:T(8,128)(2,1)}), bf16[1024,2048]{1,0:T(8,128)(2,1)}) %all-gather.8.cloned.1.call-update) | async-done | bytes 4194320 | tf_op jit(solution)/shard_map/all_gather | solution.py:577
  385.0 148.4 %mlp.1 = (f32[256,2048]{1,0:T(8,128)}, bf16[4,256,2048]{2,1,0:T(8,128)(2,1)}, bf16[256,1408]{1,0:T(8,128)(2,1)}, bf16[256,1408]{1,0:T(8,128)(2,1)}, bf16[1408,25...) custom-call(bf16[4,256,2048]{2,1,0:T(8,128)(2,1)} %bitcast.80, ...), custom_call_target="tpu_custom_call" | custom-call | tf_op jit(solution)/shard_map/mlp/pallas_call | solution.py:486
  537.2 70.9 %reduce-scatter.12.cloned.1.call-done = bf16[256,2048]{1,0:T(8,128)(2,1)} async-done(((bf16[1024,2048]{1,0:T(8,128)(2,1)}), bf16[256,2048]{1,0:T(8,128)(2,1)}) %reduce-scatter.12.cloned.1.call-update) | async-done | bytes 1048592 | tf_op jit(solution)/shard_map/reduce_scatter | solution.py:581
  612.0 7.7 convolution_convert_fusion.2
  619.7 25.0 %attn_backward.1 = (bf16[4,512,256]{2,1,0:T(8,128)(2,1)}, f32[4,1024,128]{2,1,0:T(8,128)}) custom-call(s32[1]{0:T(128)} %bitcast.row0_ref, bf16[4,512,256]{2,1,0:T(8,128)(2,1)} %get-tuple-element.36.q_ref, bf16[4,1024,128]{2,1,0:T(8,128)(2,1)} %all-gather.6.cloned.1.call-done.kv_ref, bf16[4,512,256]{2,1,0:T(8,128)(2,1)} %bitcast.83, ...), custom_call_target="tpu_custom_call" | custom-call | tf_op jit(solution)/shard_map/attn_backward/pallas_call | solution.py:140
  647.5 27.7 %reduce-scatter.14.cloned.1.call-done = bf16[4,256,128]{2,1,0:T(8,128)(2,1)} async-done(((bf16[4,1024,128]{2,1,0:T(8,128)(2,1)}), bf16[4,256,128]{2,1,0:T(8,128)(2,1)}) %reduce-scatter.14.cloned.1.call-update) | async-done | bytes 262160 | tf_op jit(solution)/shard_map/reduce_scatter | solution.py:593
  687.3 6.9 convolution_convert_fusion
  697.6 6.6 fusion.10
  705.7 14.3 %reduce-scatter.20.cloned.1.call-done = bf16[4,256,128]{1,2,0:T(8,128)(2,1)} async-done(((bf16[4,2048,128]{1,2,0:T(8,128)(2,1)}), bf16[4,256,128]{1,2,0:T(8,128)(2,1)}) %reduce-scatter.20.cloned.1.call-update) | async-done | bytes 262160 | tf_op jit(solution)/shard_map/reduce_scatter | solution.py:508
  720.1 75.1 %reduce-scatter.16.cloned.1.call-done = bf16[4,256,512]{1,2,0:T(8,128)(2,1)} async-done(((bf16[4,2048,512]{1,2,0:T(8,128)(2,1)}), bf16[4,256,512]{1,2,0:T(8,128)(2,1)}) %reduce-scatter.16.cloned.1.call-update) | async-done | bytes 1048592 | tf_op jit(solution)/shard_map/reduce_scatter | solution.py:508
  795.2 74.7 %reduce-scatter.24.cloned.1.call-done = bf16[4,512,256]{2,1,0:T(8,128)(2,1)} async-done(((bf16[4,512,2048]{2,1,0:T(8,128)(2,1)}), bf16[4,512,256]{2,1,0:T(8,128)(2,1)}) %reduce-scatter.24.cloned.1.call-update) | async-done | bytes 1048592 | tf_op jit(solution)/shard_map/reduce_scatter | solution.py:508
  876.7 32.7 %reduce-scatter.28.cloned.1.call-done = f32[256,2]{1,0:T(8,128)} async-done(((f32[2048,2]{1,0:T(8,128)}), f32[256,2]{1,0:T(8,128)}) %reduce-scatter.28.cloned.1.call-update) | async-done | bytes 2064
  910.5 11.7 %psum.7 = f32[2,256]{1,0:T(2,128)S(1)} all-reduce(f32[2,256]{1,0:T(2,128)S(1)} %copy.67), channel_id=1, replica_groups=mesh['dp'=8,'tensor'=4] {'tensor'}, use_global_device_ids=true, to_apply=%region_10.0 | all-reduce | flops 512 | bytes 4096 | tf_op jit(solution)/shard_map/psum | solution.py:611
  922.8 8.6 reduce-scatter.22.cloned.1.call-done
  932.8 26.2 %reduce-scatter.18.cloned.1.call-done = bf16[1,256,512]{1,2,0:T(8,128)(2,1)} async-done(((bf16[4,256,512]{1,2,0:T(8,128)(2,1)}), bf16[1,256,512]{1,2,0:T(8,128)(2,1)}) %reduce-scatter.18.cloned.1.call-update) | async-done | bytes 262160 | tf_op jit(solution)/shard_map/reduce_scatter | solution.py:605
  961.0 26.1 %reduce-scatter.26.cloned.1.call-done = bf16[1,512,256]{2,1,0:T(8,128)(2,1)} async-done(((bf16[4,512,256]{2,1,0:T(8,128)(2,1)}), bf16[1,512,256]{2,1,0:T(8,128)(2,1)}) %reduce-scatter.26.cloned.1.call-update) | async-done | bytes 262160 | tf_op jit(solution)/shard_map/reduce_scatter | solution.py:605
  (128 shorter events, 54.7 us)
Async XLA Ops:
  7.2 16.8 %copy-start.4 = (bf16[1408,256]{1,0:T(8,128)(2,1)S(1)}, bf16[1408,256]{1,0:T(8,128)(2,1)}, u32[]{:S(2)}) copy-start(bf16[1408,256]{1,0:T(8,128)(2,1)} %wd.1) | copy-start | bytes 2162692
  7.2 16.8 %copy-start.3 = (bf16[256,1408]{1,0:T(8,128)(2,1)S(1)}, bf16[256,1408]{1,0:T(8,128)(2,1)}, u32[]{:S(2)}) copy-start(bf16[256,1408]{1,0:T(8,128)(2,1)} %wu.1) | copy-start | bytes 2162692
  7.2 16.8 %copy-start.2 = (bf16[256,1408]{1,0:T(8,128)(2,1)S(1)}, bf16[256,1408]{1,0:T(8,128)(2,1)}, u32[]{:S(2)}) copy-start(bf16[256,1408]{1,0:T(8,128)(2,1)} %wg.1) | copy-start | bytes 2162692
  7.2 16.8 %copy-start.6 = (bf16[512,256]{1,0:T(8,128)(2,1)S(1)}, bf16[512,256]{1,0:T(8,128)(2,1)}, u32[]{:S(2)}) copy-start(bf16[512,256]{1,0:T(8,128)(2,1)} %wo.1) | copy-start | bytes 786436
  7.2 16.8 %copy-start.5 = (bf16[256,512]{1,0:T(8,128)(2,1)S(1)}, bf16[256,512]{1,0:T(8,128)(2,1)}, u32[]{:S(2)}) copy-start(bf16[256,512]{1,0:T(8,128)(2,1)} %wq.1) | copy-start | bytes 786436
  7.2 214.5 %all-gather.6.cloned.1.call-start = ((), (), s32[]{:S(2)}) async-start(), calls=%async_computation.9 | async-start | bytes 1310720 | tf_op jit(solution)/shard_map/all_gather | solution.py:571
  10.2 175.0 %copy-start.22 = (f32[256]{0:T(256)}, f32[256]{0:T(256)S(1)}, u32[]{:S(2)}) copy-start(f32[256]{0:T(256)S(1)} %get-tuple-element.108) | copy-start | bytes 3076
  24.0 162.0 %copy-start.12 = (bf16[256,2048]{1,0:T(8,128)(2,1)}, bf16[256,2048]{1,0:T(8,128)(2,1)S(1)}, u32[]{:S(2)}) copy-start(bf16[256,2048]{1,0:T(8,128)(2,1)S(1)} %fusion.4.a1_ref) | copy-start | bytes 3145732
  187.1 3.0 copy-start.21
  189.3 114.3 %all-gather.10.cloned.1.call-start = ((), (), s32[]{:S(2)}) async-start(), calls=%async_computation.11 | async-start | bytes 5242880 | tf_op jit(solution)/shard_map/all_gather | solution.py:578
  190.1 195.0 %all-gather.8.cloned.1.call-start = ((), (), s32[]{:S(2)}) async-start(), calls=%async_computation.10 | async-start | bytes 5242880 | tf_op jit(solution)/shard_map/all_gather | solution.py:577
  221.7 27.1 %copy-start.14 = (bf16[256,2048]{1,0:T(8,128)(2,1)S(1)}, bf16[256,2048]{1,0:T(8,128)(2,1)}, u32[]{:S(2)}) copy-start(bf16[256,2048]{1,0:T(8,128)(2,1)} %param.12) | copy-start | bytes 3145732
  257.7 350.4 %reduce-scatter.12.cloned.1.call-start = ((), (), s32[]{:S(2)}) async-start(), calls=%async_computation.12 | async-start | bytes 5242880 | tf_op jit(solution)/shard_map/reduce_scatter | solution.py:581
  533.5 141.8 %reduce-scatter.14.cloned.1.call-start = ((), (), s32[]{:S(2)}) async-start(), calls=%async_computation.13 | async-start | bytes 1310720 | tf_op jit(solution)/shard_map/reduce_scatter | solution.py:593
  612.0 7.7 copy-start.9
  647.5 72.5 %reduce-scatter.20.cloned.1.call-start = ((), (), s32[]{:S(2)}) async-start(), calls=%async_computation.16 | async-start | bytes 2359296 | tf_op jit(solution)/shard_map/reduce_scatter | solution.py:508
  679.9 115.3 %reduce-scatter.16.cloned.1.call-start = ((), (), s32[]{:S(2)}) async-start(), calls=%async_computation.14 | async-start | bytes 9437184 | tf_op jit(solution)/shard_map/reduce_scatter | solution.py:508
  685.6 184.4 %reduce-scatter.24.cloned.1.call-start = ((), (), s32[]{:S(2)}) async-start(), calls=%async_computation.18 | async-start | bytes 9437184 | tf_op jit(solution)/shard_map/reduce_scatter | solution.py:508
  694.2 3.4 copy-start.23
  694.2 215.3 %reduce-scatter.28.cloned.1.call-start = ((), (), s32[]{:S(2)}) async-start(), calls=%async_computation.20 | async-start | bytes 1179648
  705.7 225.7 %reduce-scatter.22.cloned.1.call-start = ((), (), s32[]{:S(2)}) async-start(), calls=%async_computation.17 | async-start | bytes 327680 | tf_op jit(solution)/shard_map/reduce_scatter | solution.py:605
  720.0 239.0 %reduce-scatter.18.cloned.1.call-start = ((), (), s32[]{:S(2)}) async-start(), calls=%async_computation.15 | async-start | bytes 1310720 | tf_op jit(solution)/shard_map/reduce_scatter | solution.py:605
  795.2 191.9 %reduce-scatter.26.cloned.1.call-start = ((), (), s32[]{:S(2)}) async-start(), calls=%async_computation.19 | async-start | bytes 1310720 | tf_op jit(solution)/shard_map/reduce_scatter | solution.py:605
  870.0 3.6 copy-start.19
  (15 other events, 25.0 us)
Sparse Core Ops, SparseCore 0:
  189.4 32.2 all-gather.5
  223.3 80.2 all-gather.9
  305.7 79.2 all-gather.7
  533.6 74.4 reduce-scatter.11
  647.6 27.6 reduce-scatter.13
  680.0 39.9 reduce-scatter.19
  723.8 71.2 reduce-scatter.15
  798.6 71.2 reduce-scatter.23
  873.4 35.9 reduce-scatter.27
  911.7 19.5 reduce-scatter.21
  933.6 25.3 reduce-scatter.17
  961.3 25.7 reduce-scatter.25

commit v3 on v2

--- a/solution.py
+++ b/solution.py
@@ -297,7 +297,7 @@
     return (left.astype(F32) + right.astype(F32)).astype(BF)
 
 
-def mlp_kernel(a2_in, ct_in, wg_in, wu_in, wd_in, da2_out, mo_out, gg_out, gu_out, gd_out, twin_g, twin_u, twin_d, wg, wu, wd, a2_buf, ct_buf, mo_buf, a2_col, ct_col, zt, dg, du, out_buf, in_buf, diag_gu, x_gu, y_gu, diag_d, x_d, y_d, stage_gu, stage_d, load, store, line_send, line_recv, twin_send, twin_recv, send, recv, stage_sem):
+def mlp_kernel(a2_in, ct_in, wg_in, wu_in, wd_in, da2_out, mo_out, mo_got, gg_out, gu_out, gd_out, twin_g, twin_u, twin_d, wg, wu, wd, a2_buf, ct_buf, mo_buf, a2_col, ct_col, zt, dg, du, out_buf, in_buf, diag_gu, x_gu, y_gu, diag_d, x_d, y_d, stage_gu, stage_d, load, store, line_send, line_recv, mo_send, mo_recv, twin_send, twin_recv, send, recv, stage_sem):
     me = Place()
     rows, width = da2_out.shape
     hidden = wg.shape[1]
@@ -366,6 +366,12 @@
     lax.fori_loop(0, 4, chunk, 0)
     mo_store(2, 0).wait()
     mo_store(3, 1).wait()
+
+    def mo_push(m):
+        return copy_to(mo_out.at[xor4(me.t, m)], mo_got.at[m - 1], mo_send.at[m - 1], mo_recv.at[m - 1], me.line(xor4(me.t, m)))
+
+    for m in (1, 2):
+        mo_push(m).start()
 
     def owner(i):
         return xor4(me.p, 3 - i % 4) * 2 + (1 - me.c + i // 4) % 2
@@ -470,6 +476,8 @@
     da2_out[...] += in_buf[0].astype(F32) + in_buf[1].astype(F32) + in_buf[2].astype(F32)
     for copy in results:
         copy.wait()
+    for m in (1, 2):
+        mo_push(m).wait()
     for j in range(3):
         chunk_send(j).wait_send()
     for k in range(3):
@@ -485,9 +493,9 @@
     shape = lambda *dims: jax.ShapeDtypeStruct(dims, BF)
     return pl.pallas_call(
         mlp_kernel,
-        out_shape=[jax.ShapeDtypeStruct((rows, width), F32), shape(4, rows, width), shape(cols, hidden), shape(cols, hidden), shape(hidden, cols), shape(4, cols, hidden), shape(4, cols, hidden), shape(4, hidden, cols)],
+        out_shape=[jax.ShapeDtypeStruct((rows, width), F32), shape(4, rows, width), shape(2, rows, width), shape(cols, hidden), shape(cols, hidden), shape(hidden, cols), shape(4, cols, hidden), shape(4, cols, hidden), shape(4, hidden, cols)],
         in_specs=[ANY] * 5,
-        out_specs=[pl.BlockSpec(memory_space=pltpu.VMEM)] + [ANY] * 7,
+        out_specs=[pl.BlockSpec(memory_space=pltpu.VMEM)] + [ANY] * 8,
         scratch_shapes=[
             vmem(width, hidden), vmem(width, hidden), vmem(hidden, width),
             vmem(2, rows, width), vmem(2, rows, width), vmem(2, rows, width),
@@ -497,11 +505,11 @@
             vmem(2, cols, hidden), vmem(2, cols, hidden), vmem(2, cols, hidden),
             vmem(hidden, cols), vmem(hidden, cols), vmem(hidden, cols),
             vmem(2, cols, hidden), vmem(hidden, cols),
-            dma((14,)), dma((2,)), dma((3,)), dma((3,)), dma((3, 4)), dma((3, 4)), dma((3, 4)), dma((3, 4)), dma((3,)),
+            dma((14,)), dma((2,)), dma((3,)), dma((3,)), dma((2,)), dma((2,)), dma((3, 4)), dma((3, 4)), dma((3, 4)), dma((3, 4)), dma((3,)),
         ],
         compiler_params=pltpu.CompilerParams(collective_id=2, has_side_effects=True, vmem_limit_bytes=62 * 2**20),
         name="mlp",
-    )(a2, ct, wg, wu, wd)[:5]
+    )(a2, ct, wg, wu, wd)[:6]
 
 
 def home(v, dim):
@@ -525,6 +533,235 @@
     return output, da2, gg, gu, gd
 
 
+def attn_back_kernel(wo_in, wq_in, wkv_in, mo_in, q_ref, o_ref, kv_ref, lse_ref, dh_ref, a1_ref, x_ref, r1_ref, gain2_ref, cos_ref, sin_ref, first_ref, da1_ref, go_ref, gq_ref, gkv_ref, mo_got, twin_o, twin_q, twin_kv, grad_o, grad_q, grad_kv, diag_o, diag_q, diag_kv, x_o, x_q, x_kv, y_o, y_q, y_kv, z_o, z_q, z_kv, stage_o, stage_q, stage_kv, wo, wq, wkv, a1t, do_ref, bias_ref, acc_ref, dqt_ref, dkv_own, dkv_out, dkv_got, load, mo_sem, dkv_send, dkv_recv, twin_send, twin_recv, send, recv, line_send, line_recv):
+    me = Place()
+    rows, width = dh_ref.shape
+    keys, cols = kv_ref.shape[1], width // 8
+    head_of = [xor4(me.t, 3 - j) for j in range(4)]
+
+    def wo_load(j):
+        return pltpu.make_async_copy(wo_in.at[:, head_of[j]], wo.at[j % 2], load.at[j % 2])
+
+    def wq_load(j):
+        return pltpu.make_async_copy(wq_in.at[head_of[j]], wq, load.at[2])
+
+    wkv_load = pltpu.make_async_copy(wkv_in, wkv, load.at[3])
+    mo_push = copy_to(mo_in.at[xor4(me.t, 3)], mo_got, mo_sem.at[0], mo_sem.at[1], me.line(xor4(me.t, 3)))
+    wo_load(0).start()
+    wo_load(1).start()
+    wq_load(0).start()
+    wkv_load.start()
+    me.greet()
+    mo_push.start()
+    a1t[...] = a1_ref[...].T
+    bias_ref[...] = bias_of(first_ref[...], me.t * rows, keys, rows)
+
+    grads, twins, diags = [grad_o, grad_q, grad_kv], [twin_o, twin_q, twin_kv], [diag_o, diag_q, diag_kv]
+    from_x, from_y, from_z = [x_o, x_q, x_kv], [y_o, y_q, y_kv], [z_o, z_q, z_kv]
+    stages = [stage_o, stage_q, stage_kv]
+
+    def twin_push(k, j):
+        i = k * 4 + j
+        return copy_to(grads[k].at[j, :, 1 - me.c], twins[k].at[j], twin_send.at[i], twin_recv.at[i], me.twin())
+
+    def side(k, j, kind):
+        i = k * 4 + j
+        piece = lambda p: grads[k].at[j, p, me.c]
+        if kind < 2:
+            src, dst = half_of(piece(me.pd), kind), half_of(diags[k].at[j], kind)
+        else:
+            src, dst = (piece(me.px), from_x[k].at[j]) if kind == 2 else (piece(me.py), from_y[k].at[j])
+        return copy_to(src, dst, send.at[i, kind], recv.at[i, kind], me.x_side() if kind % 2 == 0 else me.y_side())
+
+    def line_push(k, j):
+        return copy_to(grads[k].at[j, me.p, me.c], from_z[k].at[2 - j], line_send.at[k, j], line_recv.at[k, 2 - j], me.line(head_of[j]))
+
+    def first(k, j):
+        twin_push(k, j).wait_recv()
+        copy = pltpu.make_async_copy(twins[k].at[j], stages[k], load.at[4])
+        copy.start()
+        copy.wait()
+        for p in (me.pd, me.px, me.py, me.p):
+            mine = grads[k].at[j, p, me.c]
+            mine[...] = add_low(mine[...], stages[k][p])
+            if p is me.pd:
+                side(k, j, 0).start()
+                side(k, j, 1).start()
+
+    def second(k, j):
+        for kind, p, to in ((1, me.px, 2), (0, me.py, 3)):
+            side(k, j, kind).wait_recv()
+            part, extra = half_of(grads[k].at[j, p, me.c], kind), half_of(diags[k].at[j], kind)
+            part[...] = add_low(part[...], extra[...])
+            side(k, j, to).start()
+
+    def third(k, j):
+        side(k, j, 2).wait_recv()
+        side(k, j, 3).wait_recv()
+        mine = grads[k].at[j, me.p, me.c]
+        total = mine[...].astype(F32) + from_x[k][j].astype(F32) + from_y[k][j].astype(F32)
+        if j < 3:
+            mine[...] = total.astype(BF)
+            line_push(k, j).start()
+        else:
+            (go_ref, gq_ref, gkv_ref)[k][...] = total
+
+    def out_group(j):
+        g = head_of[j]
+        wo_load(j).wait()
+        do = jnp.zeros((wo.shape[2], rows), F32)
+        for d in range(8):
+            part = slice(d * cols, (d + 1) * cols)
+            do += dot_nt(wo[j % 2, d], dh_ref[:, part])
+            grad_o[j, d // 2, d % 2] = dot_nn(o_ref[g], dh_ref[:, part]).astype(BF)
+        twin_push(0, j).start()
+        do_ref[j] = do.astype(BF)
+        if j + 2 < 4:
+            wo_load(j + 2).start()
+
+    def dkv_push(j, m):
+        z = xor4(me.t, m)
+        there = 3 - ((3 - j) ^ m)
+        src = dkv_out.at[j, pl.ds(pl.multiple_of(z * rows, rows), rows)]
+        return copy_to(src, dkv_got.at[m - 1, there], dkv_send.at[m - 1, j], dkv_recv.at[m - 1, there], me.line(z))
+
+    def back_group(j):
+        g = head_of[j]
+        kv = kv_ref[g]
+        kt = kv.T[:HD]
+        cos, sin = cos_ref[...], sin_ref[...]
+
+        def head(h, _):
+            part = pl.ds(pl.multiple_of(h * HD, HD), HD)
+            q, do, o = q_ref[g, part], do_ref[j, part], o_ref[g, part]
+            qz = jnp.concatenate([q, jnp.zeros_like(q)], 0)
+            doz = jnp.concatenate([jnp.zeros_like(do), do], 0)
+            delta = jnp.sum(do.astype(F32) * o.astype(F32), axis=0, keepdims=True)
+            p = jnp.exp(dot_nn(kv, qz) + bias_ref[...] - lse_ref[g, pl.ds(h, 1)])
+            ds = (p * (dot_nn(kv, doz) - delta)).astype(BF)
+            acc_ref[...] += dot_nt(ds, qz) + dot_nt(p.astype(BF), doz)
+            dqt_ref[part] = rope_back_t(dot_nn(kt, ds) * HD ** (-0.5), cos, sin).astype(BF)
+            return 0
+
+        acc_ref[...] = jnp.zeros_like(acc_ref)
+        lax.fori_loop(0, RATIO, head, 0, unroll=2)
+        dkv_out[j] = acc_ref[...].astype(BF)
+        dkv_own[j] = acc_ref[pl.ds(pl.multiple_of(me.t * rows, rows), rows)]
+        for m in (3, 2, 1):
+            dkv_push(j, m).start()
+        for d in range(8):
+            grad_q[j, d // 2, d % 2] = dot_nt(a1t[d * cols : (d + 1) * cols], dqt_ref[...]).astype(BF)
+        twin_push(1, j).start()
+        wq_load(j).wait()
+        part = dot_nt(dqt_ref[...].T, wq[...])
+        if j == 0:
+            da1_ref[...] = part
+        else:
+            da1_ref[...] += part
+        if j < 3:
+            wq_load(j + 1).start()
+
+    def keys_back():
+        wkv_load.wait()
+        turned = []
+        for j in range(4):
+            total = dkv_own[j]
+            for m in (3, 2, 1):
+                dkv_push(3 - ((3 - j) ^ m), m).wait_recv()
+                total += dkv_got[m - 1, j].astype(F32)
+            total = total.T
+            dkvt = jnp.concatenate([rope_back_t(total[:HD], cos_ref[...], sin_ref[...]), total[HD:]], 0)
+            turned.append(dkvt.astype(BF))
+            da1_ref[...] += dot_nt(dkvt.T.astype(BF), wkv[head_of[j]])
+        gain1 = jnp.sum(da1_ref[...] * (x_ref[...].astype(F32) * r1_ref[...]), axis=0, keepdims=True)
+        gain2 = gain2_ref[...]
+        for j in range(4):
+            for d in range(8):
+                at = d * cols
+                grad_kv[j, d // 2, d % 2, :cols] = dot_nt(a1t[at : at + cols], turned[j]).astype(BF)
+                extra = [gain1[:, at : at + 128], gain1[:, at + 128 : at + 256], gain2[:, at : at + 128], gain2[:, at + 128 : at + 256], jnp.zeros((28, 128), F32)]
+                grad_kv[j, d // 2, d % 2, cols:] = jnp.concatenate(extra, 0).astype(BF)
+            twin_push(2, j).start()
+
+    for j in range(4):
+        out_group(j)
+    for j in range(4):
+        first(0, j)
+    second(0, 0)
+    second(0, 1)
+    back_group(0)
+    second(0, 2)
+    second(0, 3)
+    first(1, 0)
+    back_group(1)
+    third(0, 0)
+    third(0, 1)
+    second(1, 0)
+    first(1, 1)
+    back_group(2)
+    third(0, 2)
+    third(0, 3)
+    second(1, 1)
+    first(1, 2)
+    third(1, 0)
+    back_group(3)
+    second(1, 2)
+    first(1, 3)
+    third(1, 1)
+    keys_back()
+    second(1, 3)
+    third(1, 2)
+    for j in range(4):
+        first(2, j)
+    third(1, 3)
+    for j in range(4):
+        second(2, j)
+    for j in range(4):
+        third(2, j)
+    for k in range(3):
+        for j in range(3):
+            line_push(k, j).wait()
+        total = (go_ref, gq_ref, gkv_ref)[k]
+        total[...] += from_z[k][0].astype(F32) + from_z[k][1].astype(F32) + from_z[k][2].astype(F32)
+    mo_push.wait()
+    for j in range(4):
+        for m in (1, 2, 3):
+            dkv_push(j, m).wait_send()
+        for k in range(3):
+            twin_push(k, j).wait_send()
+            for kind in range(4):
+                side(k, j, kind).wait_send()
+
+
+def attn_back(wo, wq, wkv, mo, q, o, kv, lse, dh, a1, x, r1, gain2, cos, sin, first):
+    rows, width = dh.shape
+    groups, heads, _ = q.shape
+    keys, cols = kv.shape[1], width // 8
+    dma, vmem = pltpu.SemaphoreType.DMA, lambda *shape: pltpu.VMEM(shape, BF)
+    low = lambda *dims: jax.ShapeDtypeStruct(dims, BF)
+    full = lambda *dims: jax.ShapeDtypeStruct(dims, F32)
+    inside = pl.BlockSpec(memory_space=pltpu.VMEM)
+    pieces = ((heads, cols), (cols, heads), (cols + 32, 2 * HD))
+    return pl.pallas_call(
+        attn_back_kernel,
+        out_shape=[full(rows, width)] + [full(*p) for p in pieces] + [low(rows, width)] + [low(4, 4, *p) for p in pieces],
+        in_specs=[ANY] * 4 + [inside] * 12,
+        out_specs=[inside] * 4 + [ANY] * 4,
+        scratch_shapes=[vmem(4, 4, 2, *p) for p in pieces]
+        + [vmem(4, *p) for _ in range(3) for p in pieces]
+        + [vmem(3, *p) for p in pieces]
+        + [vmem(4, *p) for p in pieces]
+        + [
+            vmem(2, 8, heads, cols), vmem(width, heads), vmem(4, width, 2 * HD), vmem(width, rows), vmem(4, heads, rows),
+            pltpu.VMEM((keys, rows), F32), pltpu.VMEM((keys, 2 * HD), F32), vmem(heads, rows),
+            pltpu.VMEM((4, rows, 2 * HD), F32), vmem(4, keys, 2 * HD), vmem(3, 4, rows, 2 * HD),
+            dma((5,)), dma((2,)), dma((3, 4)), dma((3, 4)), dma((12,)), dma((12,)), dma((12, 4)), dma((12, 4)), dma((3, 3)), dma((3, 3)),
+        ],
+        compiler_params=pltpu.CompilerParams(collective_id=3, has_side_effects=True, vmem_limit_bytes=63 * 2**20),
+        name="attn_back",
+    )(wo, wq, wkv, mo, q, o, kv, lse, dh, a1, x, r1, gain2, cos, sin, first)[:5]
+
+
 def body(tokens, segments, attn_gain, w_query, w_key, w_value, w_out, mlp_gain, w_gate, w_up, w_down, cotangent):
     rows, width = tokens.shape
     hidden = w_gate.shape[1]
@@ -548,6 +785,7 @@
     if lax.axis_size("dp") == 8 and nt == 4:
         wkv, wq, wo, wg, wu, wd = gather_weights(w_kv, w_query, w_out, w_gate, w_up, w_down)
         wkv, wq = wkv.reshape(4, width, -1), wq.reshape(4, width, -1)
+        wo_raw = wo.reshape(8, 4, -1, width // 8)
         wo = wo.reshape(8, width, -1).transpose(1, 0, 2).reshape(width, width)
         wg, wu = wg.reshape(width, -1), wu.reshape(width, -1)
         wd8 = wd.reshape(8, hidden, -1)
@@ -577,14 +815,24 @@
     a2 = lax.all_gather(n2.astype(BF), "tensor", axis=0, tiled=True)
     cot = lax.all_gather(cotangent, "tensor", axis=0, tiled=True)
     if lax.axis_size("dp") == 8 and nt == 4:
-        da2, mo, gg, gu, gd = mlp(a2.reshape(4, rows, width), cot.reshape(4, rows, width), wg, wu, wd8)
-        output = (h + lax.psum_scatter(mo.reshape(4 * rows, width), "tensor", scatter_dimension=0, tiled=True).astype(F32)).astype(BF)
+        da2, mo, mo_near, gg, gu, gd = mlp(a2.reshape(4, rows, width), cot.reshape(4, rows, width), wg, wu, wd8)
         gg, gu, gd = gg.astype(F32), gu.astype(F32), gd.astype(F32)
     else:
         output, da2, gg, gu, gd = mlp_plain(h, a2, cot, wg, wu, wd)
     dres, gain2_part = rms_backward(h, r2, gain2, da2)
     dh = cotangent.astype(F32) + dres
     dhb = dh.astype(BF)
+
+    if lax.axis_size("dp") == 8 and nt == 4:
+        da1, go, gq, gkv, mo_far = attn_back(wo_raw, wq, wkv, mo, q, o, kv, lse, dhb, a1, tokens, r1, gain2_part[None, :], cos, sin, first)
+        mo_own = lax.dynamic_index_in_dim(mo, lax.axis_index("tensor"), 0, keepdims=False)
+        output = (h + mo_own.astype(F32) + mo_near[0].astype(F32) + mo_near[1].astype(F32) + mo_far.astype(F32)).astype(BF)
+        din, _ = rms_backward(x, r1, gain1, da1)
+        grad_tokens = dh + din
+        cols = w_key.shape[0]
+        gains = gkv[cols : cols + 4].reshape(2, -1)
+        gkv = gkv[:cols]
+        return (output, grad_tokens, gains[0], gq, gkv[:, :HD], gkv[:, HD:], go, gains[1], gg, gu, gd)
 
     do = dot_nt(wo, dhb).astype(BF).reshape(o.shape)
     go_part = dot_nn(o2, dhb)

time: 1000 us -> 713 us (0.71)
  waiting for transfers between devices: 496 us -> 138 us
  Pallas kernels: 362 us -> 480 us
  matrix products: 37.9 us -> 7 us
  blocking collectives: 30.8 us -> 19.2 us
    reduce_scatter x8 -> x0, waiting for transfers between devices: 324 us -> none  [the longest x3 164 us: home(): lax.psum_scatter(v.astype(BF), 'dp', scatter_dimension=dim, tiled=True)]
    pallas_call x1, Pallas kernels: 25 us -> 138 us  [attn_back(): pl.pallas_call(attn_back_kernel, out_shape=[full(rows, width)] + [full(*p...]
    unnamed x13 -> x3, waiting for transfers between devices: 33.6 us -> 0.73 us
    dot_general x6 -> x0, matrix products: 30.9 us -> none  [the longest x1 7.73 us: dot_nt(): lax.dot_general(left, right, (((1,), (1,)), ((), ())), preferred_element_...]
    psum x1 -> x0, blocking collectives: 11.7 us -> none  [body(): gains = lax.psum(gains, 'tensor')]
  transfers between devices with their start and end apart: 12 -> 3, of which waited for: 12 -> 3; matrix products, arithmetic and copies ran while one was open for 6% -> 3% of each run, Pallas kernels for 3% -> 4%
where the time goes in v3:
time: 713 us; the launch traced here: 708 us
  Pallas kernels  480 us (67%)
  waiting for transfers between devices  138 us (19%)
  local copies, waits for them, and re-layouts  24.6 us (3%)
  other arithmetic  23.7 us (3%)
  blocking collectives  19.2 us (3%)
  between operations  14.5 us (2%)
    pallas_call x1, Pallas kernels, gather_weights(): pl.pallas_call(gather_kernel, out_shape=[shape((4, 4, 2), kv), shape((4,...  161 us
    pallas_call x1, Pallas kernels, mlp(): pl.pallas_call(mlp_kernel, out_shape=[jax.ShapeDtypeStruct((rows, width),...  154 us
    pallas_call x1, Pallas kernels, attn_back(): pl.pallas_call(attn_back_kernel, out_shape=[full(rows, width)] + [full(*p...  138 us
    all_gather x1, waiting for transfers between devices, body(): a2 = lax.all_gather(n2.astype(BF), 'tensor', axis=0, tiled=True)  81.5 us
    all_gather x1, waiting for transfers between devices, body(): cot = lax.all_gather(cotangent, 'tensor', axis=0, tiled=True)  45 us
    pallas_call x1, Pallas kernels, attn_forward(): pl.pallas_call(attn_forward_kernel, grid=(groups,), in_specs=[pl.BlockSpe...  27.1 us
  transfers between devices with their start and end apart: 3, of which 3 were waited for; matrix products, arithmetic and copies ran while one was open for 3% of the time, Pallas kernels for 4%

profile of v3, /device:TPU:0, one launch (start us, length us, event | category | flops | bytes accessed | tf_op | source)
XLA Modules:
  0.0 708.0 jit_solution(6988430349950942035)
XLA Ops:
  7.3 1.7 fusion
  9.6 10.3 %all-gather = bf16[8,1,256]{2,1,0:T(2,128)(2,1)S(1)} all-gather(bf16[1,1,256]{2,1,0:T(2,128)(2,1)S(1)} %reshape.148), channel_id=1, replica_groups=mesh['dp'=8,'tensor'=4] {'dp'}, dimensions={0}, use_global_device_ids=true | all-gather | bytes 4608 | tf_op jit(solution)/shard_map/all_gather | solution.py:782
  21.7 1.5 fusion.2.a1_ref
  23.4 161.2 %gather_weights.1 = (bf16[4,4,2,256,128]{4,3,2,1,0:T(8,128)(2,1)S(1)}, bf16[4,4,2,256,512]{4,3,2,1,0:T(8,128)(2,1)}, bf16[4,2,4,512,256]{4,3,2,1,0:T(8,128)(2,1)...) custom-call(bf16[256,128]{1,0:T(8,128)(2,1)S(1)} %pad_maximum_fusion.1.kv,, ...), custom_call_target="tpu_custom_call" | custom-call | tf_op jit(solution)/shard_map/gather_weights/pallas_call | solution.py:277
  189.5 11.5 %copy.57 = bf16[8,2048,256]{1,2,0:T(8,128)(2,1)} copy(bf16[8,2048,256]{2,1,0:T(8,128)(2,1)} %bitcast.48) | data formatting | bytes 16777216 | tf_op jit(solution)/shard_map/reshape | solution.py:789
  201.0 8.8 %all-gather.1 = bf16[8,1,256]{2,1,0:T(2,128)(2,1)S(1)} all-gather(bf16[1,1,256]{2,1,0:T(2,128)(2,1)S(1)} %reshape.150), channel_id=1, replica_groups=mesh['dp'=8,'tensor'=4] {'dp'}, dimensions={0}, use_global_device_ids=true | all-gather | bytes 4608 | tf_op jit(solution)/shard_map/all_gather | solution.py:783
  209.8 11.2 %all-gather.6.cloned.1.call-done.kv_ref = bf16[4,1024,128]{2,1,0:T(8,128)(2,1)} async-done(((bf16[4,256,128]{2,1,0:T(8,128)(2,1)}), bf16[4,1024,128]{2,1,0:T(8,128)(2,1)}) %all-gather.6.cloned.1.call-update) | async-done | bytes 1048592 | tf_op jit(solution)/shard_map/all_gather | solution.py:809
  221.0 27.1 %attn_forward.1 = (bf16[4,512,256]{2,1,0:T(8,128)(2,1)}, bf16[4,512,256]{2,1,0:T(8,128)(2,1)}, f32[4,8,256]{2,1,0:T(8,128)}) custom-call(s32[1]{0:T(128)} %bitcast.row0_ref, bf16[256,2048]{1,0:T(8,128)(2,1)} %copy-done.11, bf16[4,2048,512]{2,1,0:T(8,128)(2,1)} %bitcast.46, bf16[4,1024,128]{2,1,0:T(8,128)(2,1)} %all-gather.6.cloned.1.call-done.kv_ref, ...), custom_call_target="tpu_custom_call" | custom-call | tf_op jit(solution)/shard_map/attn_forward/pallas_call | solution.py:123
  248.2 6.3 multiply_reduce_fusion.2
  254.5 1.3 copy-done.6
  255.8 1.2 multiply_convert_fusion
  257.9 45.0 %all-gather.10.cloned.1.call-done = bf16[1024,2048]{1,0:T(8,128)(2,1)} async-done(((bf16[256,2048]{1,0:T(8,128)(2,1)}), bf16[1024,2048]{1,0:T(8,128)(2,1)}) %all-gather.10.cloned.1.call-update) | async-done | bytes 4194320 | tf_op jit(solution)/shard_map/all_gather | solution.py:816
  302.9 81.5 %all-gather.8.cloned.1.call-done = bf16[1024,2048]{1,0:T(8,128)(2,1)} async-done(((bf16[256,2048]{1,0:T(8,128)(2,1)}), bf16[1024,2048]{1,0:T(8,128)(2,1)}) %all-gather.8.cloned.1.call-update) | async-done | bytes 4194320 | tf_op jit(solution)/shard_map/all_gather | solution.py:815
  384.4 153.7 %mlp.1 = (f32[256,2048]{1,0:T(8,128)}, bf16[4,256,2048]{2,1,0:T(8,128)(2,1)}, bf16[2,256,2048]{2,1,0:T(8,128)(2,1)}, bf16[256,1408]{1,0:T(8,128)(2,1)}, bf16[256...) custom-call(bf16[4,256,2048]{2,1,0:T(8,128)(2,1)} %bitcast.55, ...), custom_call_target="tpu_custom_call" | custom-call | tf_op jit(solution)/shard_map/mlp/pallas_call | solution.py:494
  538.1 3.5 multiply_reduce_fusion
  541.7 2.3 fusion.14
  544.0 138.4 %attn_back.1 = (f32[256,2048]{1,0:T(8,128)}, f32[512,256]{1,0:T(8,128)}, f32[256,512]{1,0:T(8,128)}, f32[288,128]{1,0:T(8,128)}, bf16[256,2048]{1,0:T(8,128)(2,1...) custom-call(bf16[8,4,512,256]{3,2,1,0:T(8,128)(2,1)} %bitcast.49, ...), custom_call_target="tpu_custom_call" | custom-call | tf_op jit(solution)/shard_map/attn_back/pallas_call | solution.py:745
  683.5 1.3 slice_bitcast_fusion
  684.8 2.3 fusion.6
  688.6 1.2 convert_element_type.82
  689.8 1.2 convert_element_type.83
  691.0 1.2 convert_element_type.84
  693.1 1.9 fusion.5
  696.3 3.1 fusion.8
  (87 shorter events, 14.5 us)
Async XLA Ops:
  7.2 16.2 %copy-start.4 = (bf16[256,512]{1,0:T(8,128)(2,1)S(1)}, bf16[256,512]{1,0:T(8,128)(2,1)}, u32[]{:S(2)}) copy-start(bf16[256,512]{1,0:T(8,128)(2,1)} %wq.1) | copy-start | bytes 786436
  7.2 16.2 %copy-start.5 = (bf16[512,256]{1,0:T(8,128)(2,1)S(1)}, bf16[512,256]{1,0:T(8,128)(2,1)}, u32[]{:S(2)}) copy-start(bf16[512,256]{1,0:T(8,128)(2,1)} %wo.1) | copy-start | bytes 786436
  7.2 16.2 %copy-start.1 = (bf16[256,1408]{1,0:T(8,128)(2,1)S(1)}, bf16[256,1408]{1,0:T(8,128)(2,1)}, u32[]{:S(2)}) copy-start(bf16[256,1408]{1,0:T(8,128)(2,1)} %wg.1) | copy-start | bytes 2162692
  7.2 16.2 %copy-start.2 = (bf16[256,1408]{1,0:T(8,128)(2,1)S(1)}, bf16[256,1408]{1,0:T(8,128)(2,1)}, u32[]{:S(2)}) copy-start(bf16[256,1408]{1,0:T(8,128)(2,1)} %wu.1) | copy-start | bytes 2162692
  7.2 16.2 %copy-start.3 = (bf16[1408,256]{1,0:T(8,128)(2,1)S(1)}, bf16[1408,256]{1,0:T(8,128)(2,1)}, u32[]{:S(2)}) copy-start(bf16[1408,256]{1,0:T(8,128)(2,1)} %wd.1) | copy-start | bytes 2162692
  7.2 213.8 %all-gather.6.cloned.1.call-start = ((), (), s32[]{:S(2)}) async-start(), calls=%async_computation | async-start | bytes 1310720 | tf_op jit(solution)/shard_map/all_gather | solution.py:809
  23.3 162.1 %copy-start.11 = (bf16[256,2048]{1,0:T(8,128)(2,1)}, bf16[256,2048]{1,0:T(8,128)(2,1)S(1)}, u32[]{:S(2)}) copy-start(bf16[256,2048]{1,0:T(8,128)(2,1)S(1)} %fusion.2.a1_ref) | copy-start | bytes 3145732
  186.4 2.9 copy-start.23
  188.6 114.3 %all-gather.10.cloned.1.call-start = ((), (), s32[]{:S(2)}) async-start(), calls=%async_computation.2 | async-start | bytes 5242880 | tf_op jit(solution)/shard_map/all_gather | solution.py:816
  189.4 195.0 %all-gather.8.cloned.1.call-start = ((), (), s32[]{:S(2)}) async-start(), calls=%async_computation.1 | async-start | bytes 5242880 | tf_op jit(solution)/shard_map/all_gather | solution.py:815
  189.4 11.5 %copy-start.25 = (bf16[256]{0:T(256)(128)(2,1)S(1)}, bf16[256]{0:T(256)(128)(2,1)}, u32[]{:S(2)}) copy-start(bf16[256]{0:T(256)(128)(2,1)} %param.19) | copy-start | bytes 1540
  221.0 27.1 %copy-start.9 = (bf16[256,2048]{1,0:T(8,128)(2,1)S(1)}, bf16[256,2048]{1,0:T(8,128)(2,1)}, u32[]{:S(2)}) copy-start(bf16[256,2048]{1,0:T(8,128)(2,1)} %x_ref.1) | copy-start | bytes 3145732
  384.4 157.3 %copy-start.15 = (bf16[256,2048]{1,0:T(8,128)(2,1)S(1)}, bf16[256,2048]{1,0:T(8,128)(2,1)}, u32[]{:S(2)}) copy-start(bf16[256,2048]{1,0:T(8,128)(2,1)} %param.23) | copy-start | bytes 3145732
  538.1 3.5 copy-start.7
  538.1 3.5 copy-start.14
  682.4 6.2 copy-start.20
  684.8 5.0 copy-start.19
  688.6 3.6 copy-start.13
  689.8 2.4 copy-start.10
  689.8 3.3 copy-start.12
  693.1 3.0 copy-start.16
  693.1 3.2 copy-start.17
  696.3 3.1 copy-start.22
  696.3 3.9 copy-start.21
  (5 other events, 7.7 us)
Sparse Core Ops, SparseCore 0:
  188.8 32.2 all-gather.5
  222.6 80.2 all-gather.9
  305.1 79.2 all-gather.7

commit v4 on v3

--- a/solution.py
+++ b/solution.py
@@ -190,10 +190,12 @@
     return ref.at[pl.ds(part * rows, rows)]
 
 
-def gather_kernel(kv, wq, wo, wg, wu, wd, kv_out, q_out, o_out, g_out, u_out, d_out, z_send, z_recv, send, recv, local):
+def attn_gather_kernel(kv_in, wq_in, wo_in, wg_in, wu_in, wd_in, ct_in, x_ref, cos_ref, sin_ref, first_ref, h_ref, a1_ref, r1_ref, r2_ref, gains_ref, q_ref, o_ref, lse_ref, kv_ref, kv_out, q_out, o_out, g_out, u_out, d_out, a2_all, ct_all, wkv, wq, wo, rows_kv, bias_ref, s_ref, vt_ref, qt_ref, o_rows, a2_ref, z_send, z_recv, send, recv, local, load, kv_send, kv_recv, line_send, line_recv):
     me = Place()
+    rows, width = x_ref.shape
+    keys, cols = kv_ref.shape[1], width // 8
     me.greet()
-    sources = [kv, wq, wo, wg, wu, wd]
+    sources = [kv_in, wq_in, wo_in, wg_in, wu_in, wd_in]
     outs = [kv_out, q_out, o_out, g_out, u_out, d_out]
 
     def piece(k, s, p, c):
@@ -206,83 +208,272 @@
             return o_out.at[:, c, s]
         return outs[k].at[s, :, c] if k < 2 else outs[k].at[:, c]
 
-    def remote(src, dst, send_sem, recv_sem, to):
-        copy = pltpu.make_async_remote_copy(src, dst, send_sem, recv_sem, device_id=to, device_id_type=MESH)
-        copy.start()
-        return copy
-
-    lines = {}
-    for k in range(3):
-        for j, z in enumerate(me.across):
-            lines[k, j + 1] = remote(sources[k], piece(k, me.t, me.p, me.c), z_send.at[k, j], z_recv.at[k, j], me.line(z))
-    items = [(k, j) for k in range(3) for j in range(4)] + [(k, 0) for k in range(3, 6)]
-    going = {}
-
-    def push(i, kind, src, dst, to):
-        going[i, kind] = remote(src, dst, send.at[i, kind], recv.at[i, kind], to)
-
-    def first(i):
-        k, j = items[i]
+    def line_push(k, j):
+        return copy_to(sources[k], piece(k, me.t, me.p, me.c), z_send.at[k, j - 1], z_recv.at[k, j - 1], me.line(me.order[j]))
+
+    def push(k, j, kind):
+        s, i = me.order[j], k * 4 + j if k < 3 else k + 9
+        if kind < 2:
+            dst = piece(k, s, me.p, me.c)
+            src = sources[k] if j == 0 else dst
+        elif kind < 4:
+            src = dst = half_of(piece(k, s, me.px if kind == 2 else me.py, me.c), kind - 2)
+        else:
+            src = dst = pair(k, s, me.c)
+        to = [me.x_side, me.y_side, me.y_side, me.x_side, me.twin][kind]()
+        return copy_to(src, dst, send.at[i, kind], recv.at[i, kind], to)
+
+    def keep(k):
+        return pltpu.make_async_copy(sources[k], piece(k, me.t, me.p, me.c), local.at[k])
+
+    def first(k, j):
+        if j == 0:
+            keep(k).start()
+        else:
+            line_push(k, j).wait_recv()
+        push(k, j, 0).start()
+        push(k, j, 1).start()
+
+    def second(k, j):
+        push(k, j, 0).wait_recv()
+        push(k, j, 2).start()
+        push(k, j, 1).wait_recv()
+        push(k, j, 3).start()
+
+    def third(k, j):
+        push(k, j, 2).wait_recv()
+        push(k, j, 3).wait_recv()
+        if j == 0:
+            keep(k).wait()
+        push(k, j, 4).start()
+
+    def last(k, j):
+        push(k, j, 4).wait_recv()
+
+    def step(n, k, action):
+        t, out, own = me.t, (ct_all, a2_all)[n], (ct_in, a2_ref)[n]
+        for way, chunk, can in ((0, t - k + 1, (t < 3) & (t - k + 1 >= 0)), (1, t + k - 1, (t > 0) & (t + k - 1 <= 3))):
+
+            @pl.when(can)
+            def _():
+                src = own if k == 1 else out.at[chunk]
+                copy = copy_to(src, out.at[chunk], line_send.at[n, way, k - 1], line_recv.at[n, way, k - 1], me.line(t + 1 - 2 * way))
+                copy.start() if action == "start" else copy.wait_send()
+
+    def got(n, k):
+        t, out = me.t, (ct_all, a2_all)[n]
+        for way, chunk, can in ((0, t - k, t - k >= 0), (1, t + k, t + k <= 3)):
+
+            @pl.when(can)
+            def _():
+                copy_to(out.at[chunk], out.at[chunk], line_send.at[n, way, k - 1], line_recv.at[n, way, k - 1], me.line(t + 1 - 2 * way)).wait_recv()
+
+    def own_rows(n):
+        return pltpu.make_async_copy((ct_in, a2_ref)[n], (ct_all, a2_all)[n].at[me.t], local.at[6 + n])
+
+    kv_load = pltpu.make_async_copy(kv_out, wkv, load.at[0])
+    kv_keep = pltpu.make_async_copy(rows_kv, kv_ref, load.at[1])
+
+    def wq_load(j):
+        return pltpu.make_async_copy(q_out.at[me.order[j]], wq.at[j % 2], load.at[2 + j % 2])
+
+    def wo_load(j):
         s = me.order[j]
-        mine = piece(k, s, me.p, me.c)
-        if j == 0:
-            src = sources[k]
-            going[i, "local"] = pltpu.make_async_copy(src, mine, local.at[i])
-            going[i, "local"].start()
-        else:
-            lines[k, j].wait_recv()
-            src = mine
-        push(i, 0, src, mine, me.x_side())
-        push(i, 1, src, mine, me.y_side())
-
-    def second(i):
-        k, j = items[i]
-        s = me.order[j]
-        going[i, 0].wait_recv()
-        part = half_of(piece(k, s, me.px, me.c), 0)
-        push(i, 2, part, part, me.y_side())
-        going[i, 1].wait_recv()
-        part = half_of(piece(k, s, me.py, me.c), 1)
-        push(i, 3, part, part, me.x_side())
-
-    def third(i):
-        k, j = items[i]
-        going[i, 2].wait_recv()
-        going[i, 3].wait_recv()
-        if (i, "local") in going:
-            going[i, "local"].wait()
-        part = pair(k, me.order[j], me.c)
-        push(i, 4, part, part, me.twin())
-
-    count = len(items)
-    for tick in range(count + 4):
-        if tick < count:
-            first(tick)
-        if 0 <= tick - 1 < count:
-            second(tick - 1)
-        if 0 <= tick - 2 < count:
-            third(tick - 2)
-        if 0 <= tick - 4 < count:
-            going[tick - 4, 4].wait_recv()
-    for copy in lines.values():
-        copy.wait_send()
-    for i in range(count):
-        for kind in range(5):
-            going[i, kind].wait_send()
-
-
-def gather_weights(kv, wq, wo, wg, wu, wd):
-    dma = pltpu.SemaphoreType.DMA
-    shape = lambda lead, w: jax.ShapeDtypeStruct(lead + w.shape, BF)
+        return pltpu.make_async_copy(o_out.at[:, :, s], wo.at[:, :, pl.ds(pl.multiple_of(s * 2 * cols, cols), 2 * cols)], load.at[4 + j])
+
+    own = pl.ds(pl.multiple_of(me.t * rows, rows), rows)
+
+    def kv_push(j):
+        part = rows_kv.at[:, own]
+        return copy_to(part, part, kv_send.at[j - 1], kv_recv.at[j - 1], me.line(me.order[j]))
+
+    def gain(n):
+        parts = [wkv[0, d // 2, d % 2, cols + 2 * n + e : cols + 2 * n + e + 1] for d in range(8) for e in range(2)]
+        return jnp.concatenate(parts, 1).astype(F32)
+
+    def norm(value):
+        return lax.rsqrt(jnp.mean(value * value, axis=-1, keepdims=True) + EPSILON)
+
+    def project_keys():
+        x = x_ref[...].astype(F32)
+        r1_ref[...] = norm(x)
+        gains_ref[0:1] = gain(0)
+        gains_ref[1:2] = gain(1)
+        a1_ref[...] = (x * r1_ref[...] * gains_ref[0:1]).astype(BF)
+        for s in range(4):
+            weights = wkv[s, :, :, :cols].reshape(width, 2 * HD)
+            kvt = dot_nn(a1_ref[...], weights).T
+            kvt = jnp.concatenate([rope_t(kvt[:HD], cos_ref[...], sin_ref[...]), kvt[HD:]], 0).astype(BF)
+            rows_kv[s, own] = kvt.T
+
+    def attend(j):
+        g = me.order[j]
+        qt_ref[...] = dot_nn(a1_ref[...], wq[j % 2].reshape(width, -1)).T
+        kv = rows_kv[g]
+        vt_ref[...] = jnp.concatenate([kv.T[HD:], jnp.ones((16, keys), BF)], 0)
+        cos, sin = cos_ref[...], sin_ref[...]
+
+        def head(h, _):
+            part = pl.ds(pl.multiple_of(h * HD, HD), HD)
+            q = (rope_t(qt_ref[part], cos, sin) * HD ** (-0.5)).astype(BF)
+            q_ref[g, part] = q
+            s_ref[...] = dot_nn(kv, jnp.concatenate([q, jnp.zeros_like(q)], 0)) + bias_ref[...]
+            peak = jnp.max(s_ref[...], axis=0, keepdims=True)
+            e = jnp.exp(s_ref[...] - peak).astype(BF)
+            ot = dot_nn(vt_ref[...], e)
+            total = ot[HD : HD + 1]
+            o_ref[g, part] = (ot[:HD] / total).astype(BF)
+            lse_ref[g, pl.ds(h, 1)] = peak + jnp.log(total)
+            return 0
+
+        lax.fori_loop(0, RATIO, head, 0, unroll=2)
+        o_rows[:, pl.ds(pl.multiple_of(g * 2 * cols, cols), 2 * cols)] = o_ref[g].T
+
+    def mix():
+        for d in range(8):
+            part = slice(d * cols, (d + 1) * cols)
+            h_ref[:, part] = x_ref[:, part].astype(F32) + dot_nn(o_rows[...], wo[d // 2, d % 2])
+        h = h_ref[...]
+        r2_ref[...] = norm(h)
+        a2_ref[...] = (h * r2_ref[...] * gains_ref[1:2]).astype(BF)
+
+    KV, Q, O, G, U, D = range(6)
+    for k in (KV, Q, O):
+        for j in (1, 2, 3):
+            line_push(k, j).start()
+    own_rows(0).start()
+    first(KV, 0)
+    first(Q, 0)
+    bias_ref[...] = bias_of(first_ref[...], me.t * rows, keys, rows)
+    for j in (1, 2, 3):
+        first(KV, j)
+    for j in range(4):
+        second(KV, j)
+    first(Q, 1)
+    for j in range(4):
+        third(KV, j)
+    second(Q, 0)
+    for j in range(4):
+        last(KV, j)
+    kv_load.start()
+    kv_load.wait()
+    project_keys()
+    for j in (1, 2, 3):
+        kv_push(j).start()
+    step(0, 1, "start")
+    first(Q, 2)
+    second(Q, 1)
+    third(Q, 0)
+    first(Q, 3)
+    second(Q, 2)
+    third(Q, 1)
+    last(Q, 0)
+    wq_load(0).start()
+    first(O, 0)
+    for j in (1, 2, 3):
+        kv_push(j).wait_recv()
+    kv_keep.start()
+    wq_load(0).wait()
+    attend(0)
+    second(Q, 3)
+    third(Q, 2)
+    first(O, 1)
+    last(Q, 1)
+    wq_load(1).start()
+    second(O, 0)
+    got(0, 1)
+    step(0, 2, "start")
+    wq_load(1).wait()
+    attend(1)
+    third(Q, 3)
+    first(O, 2)
+    last(Q, 2)
+    wq_load(2).start()
+    second(O, 1)
+    third(O, 0)
+    wq_load(2).wait()
+    attend(2)
+    first(O, 3)
+    last(Q, 3)
+    wq_load(3).start()
+    second(O, 2)
+    third(O, 1)
+    got(0, 2)
+    step(0, 3, "start")
+    wq_load(3).wait()
+    attend(3)
+    first(G, 0)
+    second(O, 3)
+    third(O, 2)
+    last(O, 0)
+    wo_load(0).start()
+    last(O, 1)
+    wo_load(1).start()
+    third(O, 3)
+    first(U, 0)
+    last(O, 2)
+    wo_load(2).start()
+    last(O, 3)
+    wo_load(3).start()
+    for j in range(4):
+        wo_load(j).wait()
+    mix()
+    own_rows(1).start()
+    step(1, 1, "start")
+    second(G, 0)
+    first(D, 0)
+    third(G, 0)
+    second(U, 0)
+    got(1, 1)
+    step(1, 2, "start")
+    third(U, 0)
+    second(D, 0)
+    got(1, 2)
+    step(1, 3, "start")
+    third(D, 0)
+    for k in (G, U, D):
+        last(k, 0)
+    got(0, 3)
+    got(1, 3)
+    kv_keep.wait()
+    for n in range(2):
+        own_rows(n).wait()
+        for k in (1, 2, 3):
+            step(n, k, "wait")
+    for j in (1, 2, 3):
+        kv_push(j).wait_send()
+        for k in (KV, Q, O):
+            line_push(k, j).wait_send()
+    for k in range(6):
+        for j in range(4 if k < 3 else 1):
+            for kind in range(5):
+                push(k, j, kind).wait_send()
+
+
+def attn_gather(kv, wq, wo, wg, wu, wd, ct, x, cos, sin, first):
+    rows, width = x.shape
+    heads, cols, keys = wq.shape[1], wq.shape[0], 4 * rows
+    dma, vmem = pltpu.SemaphoreType.DMA, lambda *shape: pltpu.VMEM(shape, BF)
+    low = lambda *dims: jax.ShapeDtypeStruct(dims, BF)
+    full = lambda *dims: jax.ShapeDtypeStruct(dims, F32)
+    inside = pl.BlockSpec(memory_space=pltpu.VMEM)
     return pl.pallas_call(
-        gather_kernel,
-        out_shape=[shape((4, 4, 2), kv), shape((4, 4, 2), wq), shape((4, 2, 4), wo), shape((4, 2), wg), shape((4, 2), wu), shape((4, 2), wd)],
-        in_specs=[ANY] * 6,
-        out_specs=[ANY] * 6,
-        scratch_shapes=[dma((3, 3)), dma((3, 3)), dma((15, 5)), dma((15, 5)), dma((15,))],
-        compiler_params=pltpu.CompilerParams(collective_id=1, has_side_effects=True, vmem_limit_bytes=48 * 2**20),
-        name="gather_weights",
-    )(kv, wq, wo, wg, wu, wd)
+        attn_gather_kernel,
+        out_shape=[
+            full(rows, width), low(rows, width), full(rows, 1), full(rows, 1), full(2, width), low(4, heads, rows), low(4, heads, rows), full(4, RATIO, rows),
+            low(4, keys, 2 * HD), low(4, 4, 2, *kv.shape), low(4, 4, 2, *wq.shape), low(4, 2, 4, *wo.shape),
+            low(4, 2, *wg.shape), low(4, 2, *wu.shape), low(4, 2, *wd.shape), low(4, rows, width), low(4, rows, width),
+        ],
+        in_specs=[ANY] * 7 + [inside] * 4,
+        out_specs=[inside] * 8 + [ANY] * 9,
+        scratch_shapes=[
+            vmem(4, 4, 2, *kv.shape), vmem(2, 4, 2, cols, heads), vmem(4, 2, width, cols), vmem(4, keys, 2 * HD),
+            pltpu.VMEM((keys, rows), F32), pltpu.VMEM((keys, rows), F32), vmem(HD + 16, keys), pltpu.VMEM((heads, rows), F32), vmem(rows, width), vmem(rows, width),
+            dma((3, 3)), dma((3, 3)), dma((15, 5)), dma((15, 5)), dma((8,)), dma((8,)), dma((3,)), dma((3,)), dma((2, 2, 3)), dma((2, 2, 3)),
+        ],
+        compiler_params=pltpu.CompilerParams(collective_id=1, has_side_effects=True, vmem_limit_bytes=56 * 2**20),
+        name="attn_gather",
+    )(kv, wq, wo, wg, wu, wd, ct, x, cos, sin, first)
 
 
 def xor4(a, m):
@@ -672,7 +863,7 @@
             total = total.T
             dkvt = jnp.concatenate([rope_back_t(total[:HD], cos_ref[...], sin_ref[...]), total[HD:]], 0)
             turned.append(dkvt.astype(BF))
-            da1_ref[...] += dot_nt(dkvt.T.astype(BF), wkv[head_of[j]])
+            da1_ref[...] += dot_nt(dkvt.T.astype(BF), wkv[head_of[j], :, :cols].reshape(width, 2 * HD))
         gain1 = jnp.sum(da1_ref[...] * (x_ref[...].astype(F32) * r1_ref[...]), axis=0, keepdims=True)
         gain2 = gain2_ref[...]
         for j in range(4):
@@ -752,7 +943,7 @@
         + [vmem(3, *p) for p in pieces]
         + [vmem(4, *p) for p in pieces]
         + [
-            vmem(2, 8, heads, cols), vmem(width, heads), vmem(4, width, 2 * HD), vmem(width, rows), vmem(4, heads, rows),
+            vmem(2, 8, heads, cols), vmem(width, heads), vmem(4, 8, cols + 32, 2 * HD), vmem(width, rows), vmem(4, heads, rows),
             pltpu.VMEM((keys, rows), F32), pltpu.VMEM((keys, 2 * HD), F32), vmem(heads, rows),
             pltpu.VMEM((4, rows, 2 * HD), F32), vmem(4, keys, 2 * HD), vmem(3, 4, rows, 2 * HD),
             dma((5,)), dma((2,)), dma((3, 4)), dma((3, 4)), dma((12,)), dma((12,)), dma((12, 4)), dma((12, 4)), dma((3, 3)), dma((3, 3)),
@@ -762,41 +953,56 @@
     )(wo, wq, wkv, mo, q, o, kv, lse, dh, a1, x, r1, gain2, cos, sin, first)[:5]
 
 
+def rope_tables(segments, rows, row0):
+    own = lax.dynamic_slice_in_dim(segments, row0, rows)
+    first = jnp.sum((segments[:, None] < own[None, :]).astype(jnp.int32), axis=0)
+    index = jnp.arange(rows, dtype=jnp.int32) + row0
+    freq = jnp.exp(jnp.arange(HD // 2, dtype=F32) * (-2.0 * math.log(10000.0) / HD))
+    angle = freq[:, None] * (index - first).astype(F32)[None, :]
+    cos, sin = jnp.cos(angle), jnp.sin(angle)
+    return jnp.concatenate([cos, cos], 0), jnp.concatenate([sin, sin], 0), first[None, :]
+
+
 def body(tokens, segments, attn_gain, w_query, w_key, w_value, w_out, mlp_gain, w_gate, w_up, w_down, cotangent):
+    rows, width = tokens.shape
+    cols, hidden = w_gate.shape
+    t = lax.axis_index("tensor")
+    cos, sin, first = rope_tables(segments, rows, t * rows)
+    extra = jnp.concatenate([attn_gain.reshape(2, -1), mlp_gain.reshape(2, -1), jnp.zeros((28, 2 * HD), BF)], 0)
+    w_kv = jnp.concatenate([jnp.concatenate([w_key, w_value], 1), extra], 0)
+    h, a1, r1, r2, gains, q, o, lse, kv, wkv, wq, wo, wg, wu, wd, a2, ct = attn_gather(w_kv, w_query, w_out, w_gate, w_up, w_down, cotangent, tokens, cos, sin, first)
+    wkv, wq, wo = wkv.reshape(4, 8, -1, 2 * HD), wq.reshape(4, width, -1), wo.reshape(8, 4, -1, cols)
+    da2, mo, mo_near, gg, gu, gd = mlp(a2, ct, wg.reshape(width, -1), wu.reshape(width, -1), wd.reshape(8, hidden, -1))
+    dres, gain2_part = rms_backward(h, r2, gains[1:2], da2)
+    dh = cotangent.astype(F32) + dres
+    da1, go, gq, gkv, mo_far = attn_back(wo, wq, wkv, mo, q, o, kv, lse, dh.astype(BF), a1, tokens, r1, gain2_part[None, :], cos, sin, first)
+    mo_own = lax.dynamic_index_in_dim(mo, t, 0, keepdims=False)
+    output = (h + mo_own.astype(F32) + mo_near[0].astype(F32) + mo_near[1].astype(F32) + mo_far.astype(F32)).astype(BF)
+    din, _ = rms_backward(tokens.astype(F32), r1, gains[0:1], da1)
+    grad_tokens = dh + din
+    gain_grads = gkv[cols : cols + 4].reshape(2, -1)
+    gkv = gkv[:cols]
+    return (output, grad_tokens, gain_grads[0], gq, gkv[:, :HD], gkv[:, HD:], go, gain_grads[1], gg.astype(F32), gu.astype(F32), gd.astype(F32))
+
+
+def body_plain(tokens, segments, attn_gain, w_query, w_key, w_value, w_out, mlp_gain, w_gate, w_up, w_down, cotangent):
     rows, width = tokens.shape
     hidden = w_gate.shape[1]
     nt = lax.axis_size("tensor")
     row0 = lax.axis_index("tensor") * rows
-    keys = segments.shape[0]
-
-    own_seg = lax.dynamic_slice_in_dim(segments, row0, rows)
-    first = jnp.sum((segments[:, None] < own_seg[None, :]).astype(jnp.int32), axis=0)
-    index = jnp.arange(rows, dtype=jnp.int32) + row0
-    freq = jnp.exp(jnp.arange(HD // 2, dtype=F32) * (-2.0 * math.log(10000.0) / HD))
-    angle = freq[:, None] * (index - first).astype(F32)[None, :]
-    cos, sin = jnp.cos(angle), jnp.sin(angle)
-    cos, sin = jnp.concatenate([cos, cos], 0), jnp.concatenate([sin, sin], 0)
-    first = first[None, :]
+    cos, sin, first = rope_tables(segments, rows, row0)
     row0_s = row0[None].astype(jnp.int32)
 
     gain1 = lax.all_gather(attn_gain, "dp", axis=0, tiled=True).astype(F32)
     gain2 = lax.all_gather(mlp_gain, "dp", axis=0, tiled=True).astype(F32)
     w_kv = jnp.concatenate([w_key, w_value], 1)
-    if lax.axis_size("dp") == 8 and nt == 4:
-        wkv, wq, wo, wg, wu, wd = gather_weights(w_kv, w_query, w_out, w_gate, w_up, w_down)
-        wkv, wq = wkv.reshape(4, width, -1), wq.reshape(4, width, -1)
-        wo_raw = wo.reshape(8, 4, -1, width // 8)
-        wo = wo.reshape(8, width, -1).transpose(1, 0, 2).reshape(width, width)
-        wg, wu = wg.reshape(width, -1), wu.reshape(width, -1)
-        wd8 = wd.reshape(8, hidden, -1)
-    else:
-        full = lambda w, axis: lax.all_gather(lax.all_gather(w, "dp", axis=axis, tiled=True), "tensor", axis=0)
-        wq = full(w_query, 0)
-        wkv = full(w_kv, 0)
-        wo = full(w_out, 1).reshape(width, width)
-        wg = lax.all_gather(w_gate, "dp", axis=0, tiled=True)
-        wu = lax.all_gather(w_up, "dp", axis=0, tiled=True)
-        wd = lax.all_gather(w_down, "dp", axis=1, tiled=True)
+    full = lambda w, axis: lax.all_gather(lax.all_gather(w, "dp", axis=axis, tiled=True), "tensor", axis=0)
+    wq = full(w_query, 0)
+    wkv = full(w_kv, 0)
+    wo = full(w_out, 1).reshape(width, width)
+    wg = lax.all_gather(w_gate, "dp", axis=0, tiled=True)
+    wu = lax.all_gather(w_up, "dp", axis=0, tiled=True)
+    wd = lax.all_gather(w_down, "dp", axis=1, tiled=True)
 
     x = tokens.astype(F32)
     n1, r1 = rms_forward(x, gain1)
@@ -814,25 +1020,10 @@
     n2, r2 = rms_forward(h, gain2)
     a2 = lax.all_gather(n2.astype(BF), "tensor", axis=0, tiled=True)
     cot = lax.all_gather(cotangent, "tensor", axis=0, tiled=True)
-    if lax.axis_size("dp") == 8 and nt == 4:
-        da2, mo, mo_near, gg, gu, gd = mlp(a2.reshape(4, rows, width), cot.reshape(4, rows, width), wg, wu, wd8)
-        gg, gu, gd = gg.astype(F32), gu.astype(F32), gd.astype(F32)
-    else:
-        output, da2, gg, gu, gd = mlp_plain(h, a2, cot, wg, wu, wd)
+    output, da2, gg, gu, gd = mlp_plain(h, a2, cot, wg, wu, wd)
     dres, gain2_part = rms_backward(h, r2, gain2, da2)
     dh = cotangent.astype(F32) + dres
     dhb = dh.astype(BF)
-
-    if lax.axis_size("dp") == 8 and nt == 4:
-        da1, go, gq, gkv, mo_far = attn_back(wo_raw, wq, wkv, mo, q, o, kv, lse, dhb, a1, tokens, r1, gain2_part[None, :], cos, sin, first)
-        mo_own = lax.dynamic_index_in_dim(mo, lax.axis_index("tensor"), 0, keepdims=False)
-        output = (h + mo_own.astype(F32) + mo_near[0].astype(F32) + mo_near[1].astype(F32) + mo_far.astype(F32)).astype(BF)
-        din, _ = rms_backward(x, r1, gain1, da1)
-        grad_tokens = dh + din
-        cols = w_key.shape[0]
-        gains = gkv[cols : cols + 4].reshape(2, -1)
-        gkv = gkv[:cols]
-        return (output, grad_tokens, gains[0], gq, gkv[:, :HD], gkv[:, HD:], go, gains[1], gg, gu, gd)
 
     do = dot_nt(wo, dhb).astype(BF).reshape(o.shape)
     go_part = dot_nn(o2, dhb)
@@ -864,7 +1055,7 @@
     rows, block = P(("dp", "tensor"), None), P("dp", "tensor")
     turned, line = P("tensor", "dp"), P("dp")
     return jax.shard_map(
-        body,
+        body if (mesh.shape["dp"], mesh.shape["tensor"]) == (8, 4) else body_plain,
         mesh=mesh,
         in_specs=(rows, line, line, block, block, block, turned, line, block, block, turned, rows),
         out_specs=(rows, rows, line, block, block, block, turned, line, block, block, turned),

time: 713 us -> 561 us (0.79)
  waiting for transfers between devices: 138 us -> 0 us
  Pallas kernels: 480 us -> 528 us
  blocking collectives: 19.2 us -> 0 us
  local copies, waits for them, and re-layouts: 24.6 us -> 7.57 us
  between operations: 14.5 us -> 1.27 us
    all_gather x3 -> x0, waiting for transfers between devices: 138 us -> none  [the longest x1 81.5 us: body(): a2 = lax.all_gather(n2.astype(BF), 'tensor', axis=0, tiled=True)]
    pallas_call x2 -> x1, Pallas kernels: 188 us -> 235 us  [attn_gather(): pl.pallas_call(attn_gather_kernel, out_shape=[full(rows, width), low(rows...]
    all_gather x2 -> x0, blocking collectives: 19.2 us -> none  [the longest x1 10.3 us: body(): gain1 = lax.all_gather(attn_gain, 'dp', axis=0, tiled=True).astype(F32)]
    reshape x1 -> x0, local copies, waits for them, and re-layouts: 11.5 us -> none  [body(): wo = wo.reshape(8, width, -1).transpose(1, 0, 2).reshape(width, width)]
  transfers between devices with their start and end apart: 3 -> 0, of which waited for: 3 -> 0; matrix products, arithmetic and copies ran while one was open for 3% -> 0% of each run, Pallas kernels for 4% -> 0%
where the time goes in v4:
time: 561 us; the launch traced here: 557 us
  Pallas kernels  528 us (94%)
  other arithmetic  20 us (4%)
  local copies, waits for them, and re-layouts  7.57 us (1%)
    pallas_call x1, Pallas kernels, attn_gather(): pl.pallas_call(attn_gather_kernel, out_shape=[full(rows, width), low(rows...  235 us
    pallas_call x1, Pallas kernels, mlp(): pl.pallas_call(mlp_kernel, out_shape=[jax.ShapeDtypeStruct((rows, width),...  153 us
    pallas_call x1, Pallas kernels, attn_back(): pl.pallas_call(attn_back_kernel, out_shape=[full(rows, width)] + [full(*p...  140 us

profile of v4, /device:TPU:0, one launch (start us, length us, event | category | flops | bytes accessed | tf_op | source)
XLA Modules:
  0.0 556.7 jit_solution(12511021457782725904)
XLA Ops:
  0.6 0.8 dynamic_slice.7
  1.4 0.9 convert_reduce_fusion
  2.4 0.2 multiply_sine_fusion
  2.6 0.9 copy.31
  3.5 0.9 copy.32
  4.4 1.4 maximum_maximum_fusion.kv_in
  5.8 0.7 pad_maximum_fusion
  6.5 234.9 %attn_gather.1 = (f32[256,2048]{1,0:T(8,128)}, bf16[256,2048]{1,0:T(8,128)(2,1)}, f32[256,1]{1,0:T(8,128)}, f32[256,1]{1,0:T(8,128)}, f32[2,2048]{1,0:T(2,128)},...) custom-call(bf16[288,128]{1,0:T(8,128)(2,1)} %maximum_maximum_fusion, ...), custom_call_target="tpu_custom_call" | custom-call | tf_op jit(solution)/shard_map/attn_gather/pallas_call | solution.py:460
  241.4 153.3 %mlp.1 = (f32[256,2048]{1,0:T(8,128)}, bf16[4,256,2048]{2,1,0:T(8,128)(2,1)}, bf16[2,256,2048]{2,1,0:T(8,128)(2,1)}, bf16[256,1408]{1,0:T(8,128)(2,1)}, bf16[256...) custom-call(bf16[4,256,2048]{2,1,0:T(8,128)(2,1)} %get-tuple-element, ...), custom_call_target="tpu_custom_call" | custom-call | tf_op jit(solution)/shard_map/mlp/pallas_call | solution.py:685
  395.1 3.5 multiply_reduce_fusion
  398.7 2.3 fusion.10
  401.0 139.7 %attn_back.1 = (f32[256,2048]{1,0:T(8,128)}, f32[512,256]{1,0:T(8,128)}, f32[256,512]{1,0:T(8,128)}, f32[288,128]{1,0:T(8,128)}, bf16[256,2048]{1,0:T(8,128)(2,1...) custom-call(bf16[8,4,512,256]{3,2,1,0:T(8,128)(2,1)} %bitcast.26, ...), custom_call_target="tpu_custom_call" | custom-call | tf_op jit(solution)/shard_map/attn_back/pallas_call | solution.py:936
  540.7 4.8 fusion.5
  545.5 0.4 fusion.3
  545.9 1.2 copy-done.3
  547.1 1.9 fusion.2
  549.0 0.6 slice_bitcast_fusion
  549.7 0.7 copy.34
  550.4 0.7 copy.33
  551.1 1.2 convert_element_type.65
  552.3 1.2 convert_element_type.66
  553.5 1.2 convert_element_type.67
  554.7 0.8 copy.37
  555.5 0.8 copy.38
  (41 shorter events, 0.6 us)
Async XLA Ops:
  2.3 4.2 copy-start.15
  241.4 153.4 %copy-start.13 = (f32[256,1]{1,0:T(8,128)S(1)}, f32[256,1]{1,0:T(8,128)}, u32[]{:S(2)}) copy-start(f32[256,1]{1,0:T(8,128)} %get-tuple-element.54) | copy-start | bytes 3076
  241.4 153.5 %copy-start.9 = (f32[256,1]{1,0:T(8,128)S(1)}, f32[256,1]{1,0:T(8,128)}, u32[]{:S(2)}) copy-start(f32[256,1]{1,0:T(8,128)} %get-tuple-element.58.r1_ref) | copy-start | bytes 3076
  241.4 153.7 %copy-start.14 = (f32[2,2048]{1,0:T(2,128)S(1)}, f32[2,2048]{1,0:T(2,128)}, u32[]{:S(2)}) copy-start(f32[2,2048]{1,0:T(2,128)} %get-tuple-element.55) | copy-start | bytes 49156
  241.4 157.2 %copy-start.5 = (bf16[256,2048]{1,0:T(8,128)(2,1)S(1)}, bf16[256,2048]{1,0:T(8,128)(2,1)}, u32[]{:S(2)}) copy-start(bf16[256,2048]{1,0:T(8,128)(2,1)} %ct_in.1) | copy-start | bytes 3145732
  395.1 3.5 copy-start
  395.1 3.5 copy-start.4
  540.7 4.8 copy-start.1
  540.7 4.8 copy-start.2
  545.5 1.6 copy-start.3
  547.1 1.9 copy-start.12
  547.1 4.0 copy-start.8
  549.0 3.3 copy-start.7
  551.1 2.4 copy-start.6
  552.3 2.4 copy-start.11
  553.5 2.0 copy-start.10

commit v5 on v4

--- a/solution.py
+++ b/solution.py
@@ -160,7 +160,12 @@
         x, y = self.p % 2, self.p // 2
         self.px, self.py, self.pd = self.p + 1 - 2 * x, self.p + 2 - 4 * y, 3 - self.p
         self.across = [self.t + 1 - 2 * (self.t % 2), (self.t + 2) % 4, 3 - self.t]
-        self.order = [self.t] + self.across
+        self.inner = (self.t == 1) | (self.t == 2)
+        self.outer = (self.t == 0) | (self.t == 3)
+        inner = self.t * (3 - self.t) // 2
+        self.order = [self.t, self.across[0], 2 - self.t // 2, 3 - self.t // 2 * 3]
+        self.far = [0, 1, 2 - inner, 3 - inner]
+        self.way = [0, 1 - self.t % 2, 1 - self.t // 2, 1 - self.t // 2]
 
     def at(self, p, c, t):
         return {"dp": p * 2 + c, "tensor": t}
@@ -206,18 +211,40 @@
     def pair(k, s, c):
         if k == 2:
             return o_out.at[:, c, s]
-        return outs[k].at[s, :, c] if k < 2 else outs[k].at[:, c]
-
-    def line_push(k, j):
-        return copy_to(sources[k], piece(k, me.t, me.p, me.c), z_send.at[k, j - 1], z_recv.at[k, j - 1], me.line(me.order[j]))
+        if k == 0:
+            return kv_out.at[:, :, c]
+        return q_out.at[s, :, c] if k == 1 else outs[k].at[:, c]
+
+    def line_copy(k, chunk, way, step, own=False):
+        dst = piece(k, chunk, me.p, me.c)
+        src = sources[k] if own else dst
+        at = (k, way, step - 1)
+        return copy_to(src, dst, z_send.at[at], z_recv.at[at], me.line(me.t + 1 - 2 * way))
+
+    def line_first(k, action):
+        for way in range(2):
+
+            @pl.when(me.t < 3 if way == 0 else me.t > 0)
+            def _():
+                copy = line_copy(k, me.t, way, 1, True)
+                copy.start() if action == "start" else copy.wait_send()
+
+    def line_next(k, j, action):
+        target = me.t + 1 - 2 * me.way[j]
+
+        @pl.when((target >= 0) & (target <= 3))
+        def _():
+            copy = line_copy(k, me.order[j], me.way[j], me.far[j] + 1)
+            copy.start() if action == "start" else copy.wait_send()
 
     def push(k, j, kind):
-        s, i = me.order[j], k * 4 + j if k < 3 else k + 9
+        s, i = me.order[j], (0, 1 + j, 5 + j, 9, 10, 11)[k]
+        part = (lambda p: kv_out.at[:, p, me.c]) if k == 0 else (lambda p: piece(k, s, p, me.c))
         if kind < 2:
-            dst = piece(k, s, me.p, me.c)
-            src = sources[k] if j == 0 else dst
+            dst = part(me.p)
+            src = sources[k] if j == 0 and k > 0 else dst
         elif kind < 4:
-            src = dst = half_of(piece(k, s, me.px if kind == 2 else me.py, me.c), kind - 2)
+            src = dst = half_of(part(me.px if kind == 2 else me.py), kind - 2)
         else:
             src = dst = pair(k, s, me.c)
         to = [me.x_side, me.y_side, me.y_side, me.x_side, me.twin][kind]()
@@ -226,11 +253,15 @@
     def keep(k):
         return pltpu.make_async_copy(sources[k], piece(k, me.t, me.p, me.c), local.at[k])
 
+    def arrive(k, j):
+        line_copy(k, me.order[j], me.way[j], me.far[j]).wait_recv()
+        line_next(k, j, "start")
+
     def first(k, j):
-        if j == 0:
+        if k == 0:
+            keep(k).wait()
+        elif j == 0:
             keep(k).start()
-        else:
-            line_push(k, j).wait_recv()
         push(k, j, 0).start()
         push(k, j, 1).start()
 
@@ -243,7 +274,7 @@
     def third(k, j):
         push(k, j, 2).wait_recv()
         push(k, j, 3).wait_recv()
-        if j == 0:
+        if j == 0 and k > 0:
             keep(k).wait()
         push(k, j, 4).start()
 
@@ -285,7 +316,7 @@
 
     def kv_push(j):
         part = rows_kv.at[:, own]
-        return copy_to(part, part, kv_send.at[j - 1], kv_recv.at[j - 1], me.line(me.order[j]))
+        return copy_to(part, part, kv_send.at[j - 1], kv_recv.at[j - 1], me.line(me.across[j - 1]))
 
     def gain(n):
         parts = [wkv[0, d // 2, d % 2, cols + 2 * n + e : cols + 2 * n + e + 1] for d in range(8) for e in range(2)]
@@ -338,77 +369,79 @@
         a2_ref[...] = (h * r2_ref[...] * gains_ref[1:2]).astype(BF)
 
     KV, Q, O, G, U, D = range(6)
-    for k in (KV, Q, O):
-        for j in (1, 2, 3):
-            line_push(k, j).start()
+    keep(KV).start()
+    line_first(KV, "start")
+    line_first(Q, "start")
+    first(Q, 0)
+    first(O, 0)
     own_rows(0).start()
+    for j in (1, 2, 3):
+        arrive(KV, j)
     first(KV, 0)
-    first(Q, 0)
     bias_ref[...] = bias_of(first_ref[...], me.t * rows, keys, rows)
-    for j in (1, 2, 3):
-        first(KV, j)
-    for j in range(4):
-        second(KV, j)
+    second(Q, 0)
+    arrive(Q, 1)
     first(Q, 1)
-    for j in range(4):
-        third(KV, j)
-    second(Q, 0)
-    for j in range(4):
-        last(KV, j)
+    line_first(O, "start")
+    second(KV, 0)
+    second(O, 0)
+    arrive(Q, 2)
+    first(Q, 2)
+    third(KV, 0)
+    third(Q, 0)
+    arrive(Q, 3)
+    second(Q, 1)
+    last(KV, 0)
     kv_load.start()
+    last(Q, 0)
+    wq_load(0).start()
+    first(Q, 3)
     kv_load.wait()
     project_keys()
     for j in (1, 2, 3):
         kv_push(j).start()
+    arrive(O, 1)
+    third(Q, 1)
+    second(Q, 2)
     step(0, 1, "start")
-    first(Q, 2)
-    second(Q, 1)
-    third(Q, 0)
-    first(Q, 3)
-    second(Q, 2)
-    third(Q, 1)
-    last(Q, 0)
-    wq_load(0).start()
-    first(O, 0)
+    first(O, 1)
+    arrive(O, 2)
+    second(Q, 3)
+    third(Q, 2)
+    first(O, 2)
+    last(Q, 1)
+    wq_load(1).start()
+    arrive(O, 3)
     for j in (1, 2, 3):
         kv_push(j).wait_recv()
     kv_keep.start()
     wq_load(0).wait()
     attend(0)
-    second(Q, 3)
-    third(Q, 2)
-    first(O, 1)
-    last(Q, 1)
-    wq_load(1).start()
-    second(O, 0)
+    first(O, 3)
+    third(Q, 3)
+    second(O, 1)
+    third(O, 0)
     got(0, 1)
     step(0, 2, "start")
     wq_load(1).wait()
     attend(1)
-    third(Q, 3)
-    first(O, 2)
     last(Q, 2)
     wq_load(2).start()
-    second(O, 1)
-    third(O, 0)
+    second(O, 2)
+    third(O, 1)
+    first(G, 0)
     wq_load(2).wait()
     attend(2)
-    first(O, 3)
     last(Q, 3)
     wq_load(3).start()
-    second(O, 2)
-    third(O, 1)
-    got(0, 2)
-    step(0, 3, "start")
-    wq_load(3).wait()
-    attend(3)
-    first(G, 0)
     second(O, 3)
     third(O, 2)
     last(O, 0)
     wo_load(0).start()
     last(O, 1)
     wo_load(1).start()
+    wq_load(3).wait()
+    attend(3)
     third(O, 3)
     first(U, 0)
     last(O, 2)
@@ -433,19 +466,21 @@
     third(D, 0)
     for k in (G, U, D):
         last(k, 0)
-    got(0, 3)
+    got(0, 2)
     got(1, 3)
     kv_keep.wait()
     for n in range(2):
         own_rows(n).wait()
-        for k in (1, 2, 3):
+        for k in (1, 2, 3)[: 2 + n]:
             step(n, k, "wait")
     for j in (1, 2, 3):
         kv_push(j).wait_send()
         for k in (KV, Q, O):
-            line_push(k, j).wait_send()
+            line_next(k, j, "wait")
+    for k in (KV, Q, O):
+        line_first(k, "wait")
     for k in range(6):
-        for j in range(4 if k < 3 else 1):
+        for j in range(4 if k in (Q, O) else 1):
             for kind in range(5):
                 push(k, j, kind).wait_send()
 
@@ -469,7 +504,7 @@
         scratch_shapes=[
             vmem(4, 4, 2, *kv.shape), vmem(2, 4, 2, cols, heads), vmem(4, 2, width, cols), vmem(4, keys, 2 * HD),
             pltpu.VMEM((keys, rows), F32), pltpu.VMEM((keys, rows), F32), vmem(HD + 16, keys), pltpu.VMEM((heads, rows), F32), vmem(rows, width), vmem(rows, width),
-            dma((3, 3)), dma((3, 3)), dma((15, 5)), dma((15, 5)), dma((8,)), dma((8,)), dma((3,)), dma((3,)), dma((2, 2, 3)), dma((2, 2, 3)),
+            dma((3, 2, 3)), dma((3, 2, 3)), dma((12, 5)), dma((12, 5)), dma((8,)), dma((8,)), dma((3,)), dma((3,)), dma((2, 2, 3)), dma((2, 2, 3)),
         ],
         compiler_params=pltpu.CompilerParams(collective_id=1, has_side_effects=True, vmem_limit_bytes=56 * 2**20),
         name="attn_gather",
@@ -488,7 +523,7 @@
     return (left.astype(F32) + right.astype(F32)).astype(BF)
 
 
-def mlp_kernel(a2_in, ct_in, wg_in, wu_in, wd_in, da2_out, mo_out, mo_got, gg_out, gu_out, gd_out, twin_g, twin_u, twin_d, wg, wu, wd, a2_buf, ct_buf, mo_buf, a2_col, ct_col, zt, dg, du, out_buf, in_buf, diag_gu, x_gu, y_gu, diag_d, x_d, y_d, stage_gu, stage_d, load, store, line_send, line_recv, mo_send, mo_recv, twin_send, twin_recv, send, recv, stage_sem):
+def mlp_kernel(a2_in, ct_old, wg_in, wu_in, wd_in, ct_in, da2_out, mo_out, mo_got, gg_out, gu_out, gd_out, twin_g, twin_u, twin_d, wg, wu, wd, a2_buf, ct_buf, mo_buf, a2_col, ct_col, zt, dg, du, out_buf, in_buf, diag_gu, x_gu, y_gu, diag_d, x_d, y_d, stage_gu, stage_d, load, store, line_send, line_recv, ct_send, ct_recv, mo_send, mo_recv, twin_send, twin_recv, send, recv, stage_sem):
     me = Place()
     rows, width = da2_out.shape
     hidden = wg.shape[1]
@@ -498,34 +533,63 @@
     for copy in weights:
         copy.start()
 
+    def away(j):
+        return 2 * (1 - j % 2) + (j % 2 + j // 2) % 2
+
+    ct_push = copy_to(ct_in.at[xor4(me.t, 2)], ct_in.at[xor4(me.t, 2)], ct_send.at[0], ct_recv.at[0], me.line(xor4(me.t, 1)))
+
     def chunk_load(j, slot):
-        s = xor4(me.t, 3 - j)
+        s = xor4(me.t, away(j))
         return pltpu.make_async_copy(a2_in.at[s], a2_buf.at[slot], load.at[slot]), pltpu.make_async_copy(ct_in.at[s], ct_buf.at[slot], load.at[2 + slot])
 
-    def chunk_send(j):
-        return copy_to(out_buf.at[j], in_buf.at[2 - j], line_send.at[j], line_recv.at[2 - j], me.line(xor4(me.t, 3 - j)))
+    near, cross, both = in_buf.at[0], in_buf.at[1], in_buf.at[pl.ds(2, 2)]
+
+    def near_send():
+        return copy_to(out_buf.at[0], near, line_send.at[0], line_recv.at[0], me.line(xor4(me.t, 1)))
+
+    def both_send(m):
+        s = xor4(me.t, m)
+        return copy_to(out_buf.at[m - 1], both.at[s % 2], line_send.at[m - 1], line_recv.at[2 + s % 2], me.line(xor4(me.t, 1)))
+
+    def cross_send(m):
+        return copy_to(out_buf.at[m - 1], cross, line_send.at[m - 1], line_recv.at[1], me.line(xor4(me.t, m)))
+
+    def cross_add(m):
+        s = xor4(me.t, m)
+        copy_to(both.at[s % 2], both.at[s % 2], line_send.at[0], line_recv.at[2 + s % 2], me.line(xor4(me.t, 1))).wait_recv()
+        out_buf[m - 1] = add_low(out_buf[m - 1], both[s % 2])
+        cross_send(m).start()
 
     def mo_store(j, slot):
-        return pltpu.make_async_copy(mo_buf.at[slot], mo_out.at[xor4(me.t, 3 - j)], store.at[slot])
+        return pltpu.make_async_copy(mo_buf.at[slot], mo_out.at[xor4(me.t, away(j))], store.at[slot])
 
     for copy in chunk_load(0, 0):
         copy.start()
     me.greet()
-    for copy in weights:
-        copy.wait()
+
+    @pl.when(me.inner)
+    def _():
+        ct_push.start()
 
     def chunk(j, _):
         slot = j % 2
 
-        @pl.when(j < 3)
-        def _():
-            for copy in chunk_load(j + 1, 1 - slot):
-                copy.start()
-
         for copy in chunk_load(j, slot):
             copy.wait()
-        where = pl.multiple_of(xor4(me.t, 3 - j) * rows, rows)
-        g, u = dot_nn(a2_buf[slot], wg[...]), dot_nn(a2_buf[slot], wu[...])
+        where = pl.multiple_of(xor4(me.t, away(j)) * rows, rows)
+
+        @pl.when(j == 0)
+        def _():
+            weights[0].wait()
+
+        g = dot_nn(a2_buf[slot], wg[...])
+
+        @pl.when(j == 0)
+        def _():
+            for copy in weights[1:]:
+                copy.wait()
+
+        u = dot_nn(a2_buf[slot], wu[...])
         dz = dot_nt(ct_buf[slot], wd[...])
         sig = 1.0 / (1.0 + jnp.exp(-g))
         act = g * sig
@@ -539,12 +603,30 @@
 
         @pl.when(j < 3)
         def _():
-            out_buf[j] = part.astype(BF)
-            chunk_send(j).start()
+            out_buf[away(j) - 1] = part.astype(BF)
+
+        @pl.when((j == 1) & me.inner)
+        def _():
+            near_send().start()
+
+        for at, m in ((0, 2), (2, 3)):
+
+            @pl.when((j == at) & me.outer)
+            def _():
+                both_send(m).start()
 
         @pl.when(j == 3)
         def _():
             da2_out[...] = part
+
+        @pl.when((j == 1) & me.outer)
+        def _():
+            ct_push.wait_recv()
+
+        @pl.when(j < 3)
+        def _():
+            for copy in chunk_load(j + 1, 1 - slot):
+                copy.start()
 
         @pl.when(j >= 2)
         def _():
@@ -561,8 +643,9 @@
     def mo_push(m):
         return copy_to(mo_out.at[xor4(me.t, m)], mo_got.at[m - 1], mo_send.at[m - 1], mo_recv.at[m - 1], me.line(xor4(me.t, m)))
 
-    for m in (1, 2):
-        mo_push(m).start()
+    @pl.when(me.inner)
+    def _():
+        cross_add(3)
 
     def owner(i):
         return xor4(me.p, 3 - i % 4) * 2 + (1 - me.c + i // 4) % 2
@@ -580,6 +663,21 @@
     def twin_push(k, i):
         p = xor4(me.p, 3 - i)
         return copy_to(piece(k, p, 1 - me.c), twins[k].at[p], twin_send.at[k, i], twin_recv.at[k, i], me.twin())
+
+    diag = [diag_gu.at[0], diag_gu.at[1], diag_d]
+    from_x = [x_gu.at[0], x_gu.at[1], x_d]
+    from_y = [y_gu.at[0], y_gu.at[1], y_d]
+    stage = [stage_gu.at[0], stage_gu.at[1], stage_d]
+
+    def side(k, kind):
+        if kind < 2:
+            src, dst = half_of(piece(k, me.pd, me.c), kind), half_of(diag[k], kind)
+        else:
+            src, dst = (piece(k, me.px, me.c), from_x[k]) if kind == 2 else (piece(k, me.py, me.c), from_y[k])
+        return copy_to(src, dst, send.at[k, kind], recv.at[k, kind], me.x_side() if kind % 2 == 0 else me.y_side())
+
+    def fetch(k, p):
+        return pltpu.make_async_copy(twins[k].at[p], stage[k], stage_sem.at[k])
 
     for copy in tile_load(0, 0):
         copy.start()
@@ -605,46 +703,39 @@
             for k in range(3):
                 twin_push(k, i).start()
 
+        @pl.when(i >= 4)
+        def _():
+            p = xor4(me.p, 7 - i)
+            for k in range(3):
+                twin_push(k, i - 4).wait_recv()
+                fetch(k, p).start()
+            for k in range(3):
+                fetch(k, p).wait()
+                mine = piece(k, p, me.c)
+                mine[...] = add_low(mine[...], stage[k][...])
+
+        @pl.when(i == 4)
+        def _():
+            for k in range(3):
+                side(k, 0).start()
+                side(k, 1).start()
+
+        @pl.when((i == 5) & me.inner)
+        def _():
+            cross_add(2)
+
+        @pl.when((i == 5) & me.outer)
+        def _():
+            near_send().start()
+
+        @pl.when(i == 5)
+        def _():
+            for m in (1, 2):
+                mo_push(m).start()
+
         return 0
 
     lax.fori_loop(0, 8, tile, 0)
-
-    diag = [diag_gu.at[0], diag_gu.at[1], diag_d]
-    from_x = [x_gu.at[0], x_gu.at[1], x_d]
-    from_y = [y_gu.at[0], y_gu.at[1], y_d]
-    stage = [stage_gu.at[0], stage_gu.at[1], stage_d]
-
-    def side(k, kind):
-        if kind < 2:
-            src, dst = half_of(piece(k, me.pd, me.c), kind), half_of(diag[k], kind)
-        else:
-            src, dst = (piece(k, me.px, me.c), from_x[k]) if kind == 2 else (piece(k, me.py, me.c), from_y[k])
-        return copy_to(src, dst, send.at[k, kind], recv.at[k, kind], me.x_side() if kind % 2 == 0 else me.y_side())
-
-    steps = [(k, i) for i in range(4) for k in range(3)]
-
-    def fetch(n):
-        k, i = steps[n]
-        twin_push(k, i).wait_recv()
-        copy = pltpu.make_async_copy(twins[k].at[xor4(me.p, 3 - i)], stage[k], stage_sem.at[k])
-        copy.start()
-        return copy
-
-    def add_twin(n, copy):
-        k, i = steps[n]
-        copy.wait()
-        mine = piece(k, xor4(me.p, 3 - i), me.c)
-        mine[...] = add_low(mine[...], stage[k][...])
-        if i == 0:
-            side(k, 0).start()
-            side(k, 1).start()
-
-    ahead = fetch(0)
-    for n in range(12):
-        now = ahead
-        if n + 1 < 12:
-            ahead = fetch(n + 1)
-        add_twin(n, now)
     for k in range(3):
         side(k, 1).wait_recv()
         part, extra = half_of(piece(k, me.px, me.c), 1), half_of(diag[k], 1)
@@ -662,15 +753,21 @@
         mine[...] = (mine[...].astype(F32) + from_x[k][...].astype(F32) + from_y[k][...].astype(F32)).astype(BF)
         results.append(pltpu.make_async_copy(mine, (gg_out, gu_out, gd_out)[k], stage_sem.at[k]))
         results[-1].start()
-    for j in range(3):
-        chunk_send(j).wait_recv()
-    da2_out[...] += in_buf[0].astype(F32) + in_buf[1].astype(F32) + in_buf[2].astype(F32)
+    near_send().wait_recv()
+    cross_send(2).wait_recv()
+    da2_out[...] += in_buf[0].astype(F32) + in_buf[1].astype(F32)
     for copy in results:
         copy.wait()
     for m in (1, 2):
         mo_push(m).wait()
-    for j in range(3):
-        chunk_send(j).wait_send()
+
+    @pl.when(me.inner)
+    def _():
+        ct_push.wait_send()
+
+    near_send().wait_send()
+    for m in (2, 3):
+        cross_send(m).wait_send()
     for k in range(3):
         for i in range(4):
             twin_push(k, i).wait_send()
@@ -684,23 +781,24 @@
     shape = lambda *dims: jax.ShapeDtypeStruct(dims, BF)
     return pl.pallas_call(
         mlp_kernel,
-        out_shape=[jax.ShapeDtypeStruct((rows, width), F32), shape(4, rows, width), shape(2, rows, width), shape(cols, hidden), shape(cols, hidden), shape(hidden, cols), shape(4, cols, hidden), shape(4, cols, hidden), shape(4, hidden, cols)],
+        out_shape=[shape(4, rows, width), jax.ShapeDtypeStruct((rows, width), F32), shape(4, rows, width), shape(2, rows, width), shape(cols, hidden), shape(cols, hidden), shape(hidden, cols), shape(4, cols, hidden), shape(4, cols, hidden), shape(4, hidden, cols)],
         in_specs=[ANY] * 5,
-        out_specs=[pl.BlockSpec(memory_space=pltpu.VMEM)] + [ANY] * 8,
+        out_specs=[ANY, pl.BlockSpec(memory_space=pltpu.VMEM)] + [ANY] * 8,
+        input_output_aliases={1: 0},
         scratch_shapes=[
             vmem(width, hidden), vmem(width, hidden), vmem(hidden, width),
             vmem(2, rows, width), vmem(2, rows, width), vmem(2, rows, width),
             vmem(2, 4, rows, cols), vmem(2, 4, rows, cols),
             vmem(hidden, 4 * rows), vmem(4 * rows, hidden), vmem(4 * rows, hidden),
-            vmem(3, rows, width), vmem(3, rows, width),
+            vmem(3, rows, width), vmem(4, rows, width),
             vmem(2, cols, hidden), vmem(2, cols, hidden), vmem(2, cols, hidden),
             vmem(hidden, cols), vmem(hidden, cols), vmem(hidden, cols),
             vmem(2, cols, hidden), vmem(hidden, cols),
-            dma((14,)), dma((2,)), dma((3,)), dma((3,)), dma((2,)), dma((2,)), dma((3, 4)), dma((3, 4)), dma((3, 4)), dma((3, 4)), dma((3,)),
+            dma((14,)), dma((2,)), dma((3,)), dma((4,)), dma((1,)), dma((1,)), dma((2,)), dma((2,)), dma((3, 4)), dma((3, 4)), dma((3, 4)), dma((3, 4)), dma((3,)),
         ],
         compiler_params=pltpu.CompilerParams(collective_id=2, has_side_effects=True, vmem_limit_bytes=62 * 2**20),
         name="mlp",
-    )(a2, ct, wg, wu, wd)[:6]
+    )(a2, ct, wg, wu, wd)[1:7]
 
 
 def home(v, dim):
@@ -728,7 +826,7 @@
     me = Place()
     rows, width = dh_ref.shape
     keys, cols = kv_ref.shape[1], width // 8
-    head_of = [xor4(me.t, 3 - j) for j in range(4)]
+    head_of = [3 - me.t // 2 * 3, 2 - me.t // 2, xor4(me.t, 1), me.t]
 
     def wo_load(j):
         return pltpu.make_async_copy(wo_in.at[:, head_of[j]], wo.at[j % 2], load.at[j % 2])
@@ -764,8 +862,17 @@
             src, dst = (piece(me.px), from_x[k].at[j]) if kind == 2 else (piece(me.py), from_y[k].at[j])
         return copy_to(src, dst, send.at[i, kind], recv.at[i, kind], me.x_side() if kind % 2 == 0 else me.y_side())
 
-    def line_push(k, j):
-        return copy_to(grads[k].at[j, me.p, me.c], from_z[k].at[2 - j], line_send.at[k, j], line_recv.at[k, 2 - j], me.line(head_of[j]))
+    def line_push(k, j, slot):
+        to = xor4(me.t, 1) if slot != 1 else head_of[j]
+        return copy_to(grads[k].at[j, me.p, me.c], from_z[k].at[slot], line_send.at[k, j], line_recv.at[k, slot], me.line(to))
+
+    def fourth(k, j):
+        @pl.when(me.inner)
+        def _():
+            line_push(k, j, 2 + j).wait_recv()
+            mine = grads[k].at[j, me.p, me.c]
+            mine[...] = add_low(mine[...], from_z[k][2 + j])
+            line_push(k, j, 1).start()
 
     def first(k, j):
         twin_push(k, j).wait_recv()
@@ -793,7 +900,13 @@
         total = mine[...].astype(F32) + from_x[k][j].astype(F32) + from_y[k][j].astype(F32)
         if j < 3:
             mine[...] = total.astype(BF)
-            line_push(k, j).start()
+            if j == 2:
+                line_push(k, j, 0).start()
+            else:
+
+                @pl.when(me.outer)
+                def _():
+                    line_push(k, j, 2 + j).start()
         else:
             (go_ref, gq_ref, gkv_ref)[k][...] = total
 
@@ -811,10 +924,9 @@
             wo_load(j + 2).start()
 
     def dkv_push(j, m):
-        z = xor4(me.t, m)
-        there = 3 - ((3 - j) ^ m)
+        z, s = xor4(me.t, m), head_of[j]
         src = dkv_out.at[j, pl.ds(pl.multiple_of(z * rows, rows), rows)]
-        return copy_to(src, dkv_got.at[m - 1, there], dkv_send.at[m - 1, j], dkv_recv.at[m - 1, there], me.line(z))
+        return copy_to(src, dkv_got.at[m - 1, s], dkv_send.at[m - 1, j], dkv_recv.at[m - 1, s], me.line(z))
 
     def back_group(j):
         g = head_of[j]
@@ -858,8 +970,8 @@
         for j in range(4):
             total = dkv_own[j]
             for m in (3, 2, 1):
-                dkv_push(3 - ((3 - j) ^ m), m).wait_recv()
-                total += dkv_got[m - 1, j].astype(F32)
+                dkv_push(j, m).wait_recv()
+                total += dkv_got[m - 1, head_of[j]].astype(F32)
             total = total.T
             dkvt = jnp.concatenate([rope_back_t(total[:HD], cos_ref[...], sin_ref[...]), total[HD:]], 0)
             turned.append(dkvt.astype(BF))
@@ -874,46 +986,54 @@
                 grad_kv[j, d // 2, d % 2, cols:] = jnp.concatenate(extra, 0).astype(BF)
             twin_push(2, j).start()
 
+    O, Q, KV = range(3)
     for j in range(4):
         out_group(j)
     for j in range(4):
-        first(0, j)
-    second(0, 0)
-    second(0, 1)
+        first(O, j)
+    second(O, 0)
+    second(O, 1)
     back_group(0)
-    second(0, 2)
-    second(0, 3)
-    first(1, 0)
+    second(O, 2)
+    second(O, 3)
+    first(Q, 0)
+    third(O, 0)
     back_group(1)
-    third(0, 0)
-    third(0, 1)
-    second(1, 0)
-    first(1, 1)
+    third(O, 1)
+    second(Q, 0)
+    first(Q, 1)
+    third(O, 2)
+    fourth(O, 0)
     back_group(2)
-    third(0, 2)
-    third(0, 3)
-    second(1, 1)
-    first(1, 2)
-    third(1, 0)
+    third(O, 3)
+    second(Q, 1)
+    first(Q, 2)
+    third(Q, 0)
+    fourth(O, 1)
     back_group(3)
-    second(1, 2)
-    first(1, 3)
-    third(1, 1)
+    second(Q, 2)
+    first(Q, 3)
+    third(Q, 1)
+    fourth(Q, 0)
     keys_back()
-    second(1, 3)
-    third(1, 2)
+    second(Q, 3)
+    third(Q, 2)
+    fourth(Q, 1)
     for j in range(4):
-        first(2, j)
-    third(1, 3)
+        first(KV, j)
+    third(Q, 3)
     for j in range(4):
-        second(2, j)
+        second(KV, j)
     for j in range(4):
-        third(2, j)
+        third(KV, j)
+    for j in range(2):
+        fourth(KV, j)
     for k in range(3):
-        for j in range(3):
-            line_push(k, j).wait()
+        line_push(k, 2, 0).wait()
+        line_push(k, 0, 1).wait()
+        line_push(k, 1, 1).wait_send()
         total = (go_ref, gq_ref, gkv_ref)[k]
-        total[...] += from_z[k][0].astype(F32) + from_z[k][1].astype(F32) + from_z[k][2].astype(F32)
+        total[...] += from_z[k][0].astype(F32) + from_z[k][1].astype(F32)
     mo_push.wait()
     for j in range(4):
         for m in (1, 2, 3):
@@ -940,13 +1060,13 @@
         out_specs=[inside] * 4 + [ANY] * 4,
         scratch_shapes=[vmem(4, 4, 2, *p) for p in pieces]
         + [vmem(4, *p) for _ in range(3) for p in pieces]
-        + [vmem(3, *p) for p in pieces]
+        + [vmem(4, *p) for p in pieces]
         + [vmem(4, *p) for p in pieces]
         + [
             vmem(2, 8, heads, cols), vmem(width, heads), vmem(4, 8, cols + 32, 2 * HD), vmem(width, rows), vmem(4, heads, rows),
             pltpu.VMEM((keys, rows), F32), pltpu.VMEM((keys, 2 * HD), F32), vmem(heads, rows),
             pltpu.VMEM((4, rows, 2 * HD), F32), vmem(4, keys, 2 * HD), vmem(3, 4, rows, 2 * HD),
-            dma((5,)), dma((2,)), dma((3, 4)), dma((3, 4)), dma((12,)), dma((12,)), dma((12, 4)), dma((12, 4)), dma((3, 3)), dma((3, 3)),
+            dma((5,)), dma((2,)), dma((3, 4)), dma((3, 4)), dma((12,)), dma((12,)), dma((12, 4)), dma((12, 4)), dma((3, 3)), dma((3, 4)),
         ],
         compiler_params=pltpu.CompilerParams(collective_id=3, has_side_effects=True, vmem_limit_bytes=63 * 2**20),
         name="attn_back",

time: 561 us -> 505 us (0.900)
  Pallas kernels: 528 us -> 472 us
    pallas_call x1, Pallas kernels: 140 us -> 114 us  [attn_back(): pl.pallas_call(attn_back_kernel, out_shape=[full(rows, width)] + [full(*p...]
    pallas_call x1, Pallas kernels: 235 us -> 218 us  [attn_gather(): pl.pallas_call(attn_gather_kernel, out_shape=[full(rows, width), low(rows...]
    pallas_call x1, Pallas kernels: 153 us -> 141 us  [mlp(): pl.pallas_call(mlp_kernel, out_shape=[shape(4, rows, width), jax.ShapeDty...]
where the time goes in v5:
time: 505 us; the launch traced here: 501 us
  Pallas kernels  472 us (93%)
  other arithmetic  20 us (4%)
  local copies, waits for them, and re-layouts  7.57 us (1%)
    pallas_call x1, Pallas kernels, attn_gather(): pl.pallas_call(attn_gather_kernel, out_shape=[full(rows, width), low(rows...  218 us
    pallas_call x1, Pallas kernels, mlp(): pl.pallas_call(mlp_kernel, out_shape=[shape(4, rows, width), jax.ShapeDty...  141 us
    pallas_call x1, Pallas kernels, attn_back(): pl.pallas_call(attn_back_kernel, out_shape=[full(rows, width)] + [full(*p...  114 us

profile of v5, /device:TPU:0, one launch (start us, length us, event | category | flops | bytes accessed | tf_op | source)
XLA Modules:
  0.0 501.1 jit_solution(551883446042595401)
XLA Ops:
  0.6 0.8 dynamic_slice.7
  1.4 0.9 convert_reduce_fusion
  2.4 0.2 multiply_sine_fusion
  2.6 0.9 copy.32
  3.5 0.9 copy.33
  4.4 1.4 maximum_maximum_fusion.kv_in
  5.8 0.7 pad_maximum_fusion
  6.5 218.1 %attn_gather.1 = (f32[256,2048]{1,0:T(8,128)}, bf16[256,2048]{1,0:T(8,128)(2,1)}, f32[256,1]{1,0:T(8,128)}, f32[256,1]{1,0:T(8,128)}, f32[2,2048]{1,0:T(2,128)},...) custom-call(bf16[288,128]{1,0:T(8,128)(2,1)} %maximum_maximum_fusion, ...), custom_call_target="tpu_custom_call" | custom-call | tf_op jit(solution)/shard_map/attn_gather/pallas_call | solution.py:495
  224.6 140.8 %mlp.1 = (bf16[4,256,2048]{2,1,0:T(8,128)(2,1)}, f32[256,2048]{1,0:T(8,128)}, bf16[4,256,2048]{2,1,0:T(8,128)(2,1)}, bf16[2,256,2048]{2,1,0:T(8,128)(2,1)}, bf16...) custom-call(bf16[4,256,2048]{2,1,0:T(8,128)(2,1)} %get-tuple-element, ...), custom_call_target="tpu_custom_call", output_to_operand_aliasing={{0}: (1, {})} | custom-call | tf_op jit(solution)/shard_map/mlp/pallas_call | solution.py:782
  365.8 3.5 multiply_reduce_fusion
  369.3 2.3 fusion.10
  371.6 113.5 %attn_back.1 = (f32[256,2048]{1,0:T(8,128)}, f32[512,256]{1,0:T(8,128)}, f32[256,512]{1,0:T(8,128)}, f32[288,128]{1,0:T(8,128)}, bf16[256,2048]{1,0:T(8,128)(2,1...) custom-call(bf16[8,4,512,256]{3,2,1,0:T(8,128)(2,1)} %bitcast.26, ...), custom_call_target="tpu_custom_call" | custom-call | tf_op jit(solution)/shard_map/attn_back/pallas_call | solution.py:1056
  485.2 4.8 fusion.5
  490.0 0.4 fusion.3
  490.4 1.2 copy-done.3
  491.6 1.9 fusion.2
  493.5 0.6 slice_bitcast_fusion
  494.1 0.7 copy.35
  494.9 0.7 copy.34
  495.6 1.2 convert_element_type.65
  496.8 1.2 convert_element_type.66
  498.0 1.2 convert_element_type.67
  499.2 0.8 copy.39
  500.0 0.8 copy.40
  (41 shorter events, 0.6 us)
Async XLA Ops:
  2.3 4.2 copy-start.15
  224.6 140.8 %copy-start.13 = (f32[256,1]{1,0:T(8,128)S(1)}, f32[256,1]{1,0:T(8,128)}, u32[]{:S(2)}) copy-start(f32[256,1]{1,0:T(8,128)} %get-tuple-element.54) | copy-start | bytes 3076
  224.6 141.0 %copy-start.9 = (f32[256,1]{1,0:T(8,128)S(1)}, f32[256,1]{1,0:T(8,128)}, u32[]{:S(2)}) copy-start(f32[256,1]{1,0:T(8,128)} %get-tuple-element.58.r1_ref) | copy-start | bytes 3076
  224.6 141.1 %copy-start.14 = (f32[2,2048]{1,0:T(2,128)S(1)}, f32[2,2048]{1,0:T(2,128)}, u32[]{:S(2)}) copy-start(f32[2,2048]{1,0:T(2,128)} %get-tuple-element.55) | copy-start | bytes 49156
  224.6 144.7 %copy-start.5 = (bf16[256,2048]{1,0:T(8,128)(2,1)S(1)}, bf16[256,2048]{1,0:T(8,128)(2,1)}, u32[]{:S(2)}) copy-start(bf16[256,2048]{1,0:T(8,128)(2,1)} %ct_in.1) | copy-start | bytes 3145732
  365.7 3.5 copy-start
  365.7 3.5 copy-start.4
  485.2 4.8 copy-start.1
  485.2 4.8 copy-start.2
  490.0 1.6 copy-start.3
  491.6 1.9 copy-start.12
  491.6 4.0 copy-start.8
  493.5 3.3 copy-start.7
  495.6 2.4 copy-start.6
  496.8 2.4 copy-start.11
  498.0 2.0 copy-start.10

commit v6 on v5

--- a/solution.py
+++ b/solution.py
@@ -164,8 +164,7 @@
         self.outer = (self.t == 0) | (self.t == 3)
         inner = self.t * (3 - self.t) // 2
         self.order = [self.t, self.across[0], 2 - self.t // 2, 3 - self.t // 2 * 3]
-        self.far = [0, 1, 2 - inner, 3 - inner]
-        self.way = [0, 1 - self.t % 2, 1 - self.t // 2, 1 - self.t // 2]
+        self.away = [0, 1, 2 + inner, 3 - inner]
 
     def at(self, p, c, t):
         return {"dp": p * 2 + c, "tensor": t}
@@ -215,27 +214,15 @@
             return kv_out.at[:, :, c]
         return q_out.at[s, :, c] if k == 1 else outs[k].at[:, c]
 
-    def line_copy(k, chunk, way, step, own=False):
-        dst = piece(k, chunk, me.p, me.c)
-        src = sources[k] if own else dst
-        at = (k, way, step - 1)
-        return copy_to(src, dst, z_send.at[at], z_recv.at[at], me.line(me.t + 1 - 2 * way))
-
-    def line_first(k, action):
-        for way in range(2):
-
-            @pl.when(me.t < 3 if way == 0 else me.t > 0)
-            def _():
-                copy = line_copy(k, me.t, way, 1, True)
-                copy.start() if action == "start" else copy.wait_send()
-
-    def line_next(k, j, action):
-        target = me.t + 1 - 2 * me.way[j]
-
-        @pl.when((target >= 0) & (target <= 3))
-        def _():
-            copy = line_copy(k, me.order[j], me.way[j], me.far[j] + 1)
-            copy.start() if action == "start" else copy.wait_send()
+    def line_push(k, m):
+        return copy_to(sources[k], piece(k, me.t, me.p, me.c), z_send.at[k, m - 1], z_recv.at[k, m - 1], me.line(xor4(me.t, m)))
+
+    def line_first(k):
+        for m in (1, 2, 3):
+            line_push(k, m).start()
+
+    def arrive(k, j):
+        line_push(k, me.away[j]).wait_recv()
 
     def push(k, j, kind):
         s, i = me.order[j], (0, 1 + j, 5 + j, 9, 10, 11)[k]
@@ -253,10 +240,6 @@
     def keep(k):
         return pltpu.make_async_copy(sources[k], piece(k, me.t, me.p, me.c), local.at[k])
 
-    def arrive(k, j):
-        line_copy(k, me.order[j], me.way[j], me.far[j]).wait_recv()
-        line_next(k, j, "start")
-
     def first(k, j):
         if k == 0:
             keep(k).wait()
@@ -314,9 +297,9 @@
 
     own = pl.ds(pl.multiple_of(me.t * rows, rows), rows)
 
-    def kv_push(j):
-        part = rows_kv.at[:, own]
-        return copy_to(part, part, kv_send.at[j - 1], kv_recv.at[j - 1], me.line(me.across[j - 1]))
+    def kv_push(m, g):
+        part = rows_kv.at[g, own]
+        return copy_to(part, part, kv_send.at[m - 1, g], kv_recv.at[m - 1, g], me.line(xor4(me.t, m)))
 
     def gain(n):
         parts = [wkv[0, d // 2, d % 2, cols + 2 * n + e : cols + 2 * n + e + 1] for d in range(8) for e in range(2)]
@@ -331,24 +314,32 @@
         gains_ref[0:1] = gain(0)
         gains_ref[1:2] = gain(1)
         a1_ref[...] = (x * r1_ref[...] * gains_ref[0:1]).astype(BF)
-        for s in range(4):
-            weights = wkv[s, :, :, :cols].reshape(width, 2 * HD)
+        for m in (1, 2, 3, 0):
+            g = xor4(me.t, m)
+            weights = wkv[g, :, :, :cols].reshape(width, 2 * HD)
             kvt = dot_nn(a1_ref[...], weights).T
             kvt = jnp.concatenate([rope_t(kvt[:HD], cos_ref[...], sin_ref[...]), kvt[HD:]], 0).astype(BF)
-            rows_kv[s, own] = kvt.T
-
-    def attend(j):
+            rows_kv[g, own] = kvt.T
+            if m > 0:
+                kv_push(m, g).start()
+        for more in (1, 2, 3):
+            for m in (1, 2, 3):
+                kv_push(m, xor4(me.t, m ^ more)).start()
+
+    def attend(j, part):
         g = me.order[j]
-        qt_ref[...] = dot_nn(a1_ref[...], wq[j % 2].reshape(width, -1)).T
-        kv = rows_kv[g]
-        vt_ref[...] = jnp.concatenate([kv.T[HD:], jnp.ones((16, keys), BF)], 0)
+        if part == 0:
+            for m in (1, 2, 3):
+                kv_push(m, g).wait_recv()
+            qt_ref[...] = dot_nn(a1_ref[...], wq[j % 2].reshape(width, -1)).T
+            vt_ref[...] = jnp.concatenate([rows_kv[g].T[HD:], jnp.ones((16, keys), BF)], 0)
         cos, sin = cos_ref[...], sin_ref[...]
 
         def head(h, _):
             part = pl.ds(pl.multiple_of(h * HD, HD), HD)
             q = (rope_t(qt_ref[part], cos, sin) * HD ** (-0.5)).astype(BF)
             q_ref[g, part] = q
-            s_ref[...] = dot_nn(kv, jnp.concatenate([q, jnp.zeros_like(q)], 0)) + bias_ref[...]
+            s_ref[...] = dot_nn(rows_kv[g], jnp.concatenate([q, jnp.zeros_like(q)], 0)) + bias_ref[...]
             peak = jnp.max(s_ref[...], axis=0, keepdims=True)
             e = jnp.exp(s_ref[...] - peak).astype(BF)
             ot = dot_nn(vt_ref[...], e)
@@ -357,8 +348,9 @@
             lse_ref[g, pl.ds(h, 1)] = peak + jnp.log(total)
             return 0
 
-        lax.fori_loop(0, RATIO, head, 0, unroll=2)
-        o_rows[:, pl.ds(pl.multiple_of(g * 2 * cols, cols), 2 * cols)] = o_ref[g].T
+        lax.fori_loop(part * RATIO // 2, (part + 1) * RATIO // 2, head, 0, unroll=2)
+        if part == 1:
+            o_rows[:, pl.ds(pl.multiple_of(g * 2 * cols, cols), 2 * cols)] = o_ref[g].T
 
     def mix():
         for d in range(8):
@@ -370,89 +362,92 @@
 
     KV, Q, O, G, U, D = range(6)
     keep(KV).start()
-    line_first(KV, "start")
-    line_first(Q, "start")
+    line_first(KV)
     first(Q, 0)
+    own_rows(0).start()
+    arrive(KV, 1)
+    line_first(Q)
+    arrive(KV, 2)
+    arrive(KV, 3)
+    first(KV, 0)
     first(O, 0)
-    own_rows(0).start()
-    for j in (1, 2, 3):
-        arrive(KV, j)
-    first(KV, 0)
     bias_ref[...] = bias_of(first_ref[...], me.t * rows, keys, rows)
+    second(KV, 0)
     second(Q, 0)
+    third(KV, 0)
     arrive(Q, 1)
     first(Q, 1)
-    line_first(O, "start")
-    second(KV, 0)
+    last(KV, 0)
+    kv_load.start()
     second(O, 0)
+    kv_load.wait()
+    project_keys()
+    line_first(O)
     arrive(Q, 2)
     first(Q, 2)
-    third(KV, 0)
     third(Q, 0)
+    second(Q, 1)
     arrive(Q, 3)
-    second(Q, 1)
-    last(KV, 0)
-    kv_load.start()
+    first(Q, 3)
     last(Q, 0)
     wq_load(0).start()
-    first(Q, 3)
-    kv_load.wait()
-    project_keys()
-    for j in (1, 2, 3):
-        kv_push(j).start()
+    third(Q, 1)
+    third(O, 0)
+    second(Q, 2)
     arrive(O, 1)
-    third(Q, 1)
-    second(Q, 2)
     step(0, 1, "start")
     first(O, 1)
-    arrive(O, 2)
-    second(Q, 3)
+    wq_load(0).wait()
+    attend(0, 0)
     third(Q, 2)
-    first(O, 2)
     last(Q, 1)
     wq_load(1).start()
-    arrive(O, 3)
-    for j in (1, 2, 3):
-        kv_push(j).wait_recv()
-    kv_keep.start()
-    wq_load(0).wait()
-    attend(0)
-    first(O, 3)
+    second(Q, 3)
+    arrive(O, 2)
+    first(O, 2)
+    attend(0, 1)
     third(Q, 3)
     second(O, 1)
-    third(O, 0)
+    arrive(O, 3)
+    first(O, 3)
+    wq_load(1).wait()
+    attend(1, 0)
+    last(Q, 2)
+    wq_load(2).start()
+    third(O, 1)
+    second(O, 2)
     got(0, 1)
     step(0, 2, "start")
-    wq_load(1).wait()
-    attend(1)
-    last(Q, 2)
-    wq_load(2).start()
-    second(O, 2)
-    third(O, 1)
-    first(G, 0)
-    wq_load(2).wait()
-    attend(2)
+    attend(1, 1)
     last(Q, 3)
     wq_load(3).start()
     second(O, 3)
+    first(G, 0)
     third(O, 2)
+    wq_load(2).wait()
+    attend(2, 0)
+    third(O, 3)
     last(O, 0)
     wo_load(0).start()
     last(O, 1)
     wo_load(1).start()
-    wq_load(3).wait()
-    attend(3)
-    third(O, 3)
-    first(U, 0)
+    attend(2, 1)
     last(O, 2)
     wo_load(2).start()
     last(O, 3)
     wo_load(3).start()
+    first(U, 0)
+    wq_load(3).wait()
+    attend(3, 0)
+    got(0, 2)
+    step(0, 3, "start")
+    attend(3, 1)
     for j in range(4):
         wo_load(j).wait()
     mix()
     own_rows(1).start()
     step(1, 1, "start")
+    kv_keep.start()
     second(G, 0)
     first(D, 0)
     third(G, 0)
@@ -461,24 +456,21 @@
     step(1, 2, "start")
     third(U, 0)
     second(D, 0)
-    got(1, 2)
-    step(1, 3, "start")
     third(D, 0)
     for k in (G, U, D):
         last(k, 0)
-    got(0, 2)
-    got(1, 3)
+    got(0, 3)
+    got(1, 2)
     kv_keep.wait()
     for n in range(2):
         own_rows(n).wait()
-        for k in (1, 2, 3)[: 2 + n]:
+        for k in (1, 2, 3)[: 3 - n]:
             step(n, k, "wait")
     for j in (1, 2, 3):
-        kv_push(j).wait_send()
+        for g in range(4):
+            kv_push(j, g).wait_send()
         for k in (KV, Q, O):
-            line_next(k, j, "wait")
-    for k in (KV, Q, O):
-        line_first(k, "wait")
+            line_push(k, j).wait_send()
     for k in range(6):
         for j in range(4 if k in (Q, O) else 1):
             for kind in range(5):
@@ -504,7 +496,7 @@
         scratch_shapes=[
             vmem(4, 4, 2, *kv.shape), vmem(2, 4, 2, cols, heads), vmem(4, 2, width, cols), vmem(4, keys, 2 * HD),
             pltpu.VMEM((keys, rows), F32), pltpu.VMEM((keys, rows), F32), vmem(HD + 16, keys), pltpu.VMEM((heads, rows), F32), vmem(rows, width), vmem(rows, width),
-            dma((3, 2, 3)), dma((3, 2, 3)), dma((12, 5)), dma((12, 5)), dma((8,)), dma((8,)), dma((3,)), dma((3,)), dma((2, 2, 3)), dma((2, 2, 3)),
+            dma((3, 3)), dma((3, 3)), dma((12, 5)), dma((12, 5)), dma((8,)), dma((8,)), dma((3, 4)), dma((3, 4)), dma((2, 2, 3)), dma((2, 2, 3)),
         ],
         compiler_params=pltpu.CompilerParams(collective_id=1, has_side_effects=True, vmem_limit_bytes=56 * 2**20),
         name="attn_gather",
@@ -523,7 +515,7 @@
     return (left.astype(F32) + right.astype(F32)).astype(BF)
 
 
-def mlp_kernel(a2_in, ct_old, wg_in, wu_in, wd_in, ct_in, da2_out, mo_out, mo_got, gg_out, gu_out, gd_out, twin_g, twin_u, twin_d, wg, wu, wd, a2_buf, ct_buf, mo_buf, a2_col, ct_col, zt, dg, du, out_buf, in_buf, diag_gu, x_gu, y_gu, diag_d, x_d, y_d, stage_gu, stage_d, load, store, line_send, line_recv, ct_send, ct_recv, mo_send, mo_recv, twin_send, twin_recv, send, recv, stage_sem):
+def mlp_kernel(a2_old, ct_in, wg_in, wu_in, wd_in, a2_in, da2_out, mo_out, mo_got, gg_out, gu_out, gd_out, twin_g, twin_u, twin_d, wg, wu, wd, a2_buf, ct_buf, mo_buf, a2_col, ct_col, zt, dg, du, out_buf, in_buf, diag_gu, x_gu, y_gu, diag_d, x_d, y_d, stage_gu, stage_d, load, store, line_send, line_recv, a2_send, a2_recv, mo_send, mo_recv, twin_send, twin_recv, send, recv, stage_sem):
     me = Place()
     rows, width = da2_out.shape
     hidden = wg.shape[1]
@@ -536,7 +528,7 @@
     def away(j):
         return 2 * (1 - j % 2) + (j % 2 + j // 2) % 2
 
-    ct_push = copy_to(ct_in.at[xor4(me.t, 2)], ct_in.at[xor4(me.t, 2)], ct_send.at[0], ct_recv.at[0], me.line(xor4(me.t, 1)))
+    a2_push = copy_to(a2_in.at[xor4(me.t, 2)], a2_in.at[xor4(me.t, 2)], a2_send.at[0], a2_recv.at[0], me.line(xor4(me.t, 1)))
 
     def chunk_load(j, slot):
         s = xor4(me.t, away(j))
@@ -569,7 +561,7 @@
 
     @pl.when(me.inner)
     def _():
-        ct_push.start()
+        a2_push.start()
 
     def chunk(j, _):
         slot = j % 2
@@ -621,7 +613,7 @@
 
         @pl.when((j == 1) & me.outer)
         def _():
-            ct_push.wait_recv()
+            a2_push.wait_recv()
 
         @pl.when(j < 3)
         def _():
@@ -763,7 +755,7 @@
 
     @pl.when(me.inner)
     def _():
-        ct_push.wait_send()
+        a2_push.wait_send()
 
     near_send().wait_send()
     for m in (2, 3):
@@ -784,7 +776,7 @@
         out_shape=[shape(4, rows, width), jax.ShapeDtypeStruct((rows, width), F32), shape(4, rows, width), shape(2, rows, width), shape(cols, hidden), shape(cols, hidden), shape(hidden, cols), shape(4, cols, hidden), shape(4, cols, hidden), shape(4, hidden, cols)],
         in_specs=[ANY] * 5,
         out_specs=[ANY, pl.BlockSpec(memory_space=pltpu.VMEM)] + [ANY] * 8,
-        input_output_aliases={1: 0},
+        input_output_aliases={0: 0},
         scratch_shapes=[
             vmem(width, hidden), vmem(width, hidden), vmem(hidden, width),
             vmem(2, rows, width), vmem(2, rows, width), vmem(2, rows, width),

time: 505 us -> 493 us (0.976)
  Pallas kernels: 472 us -> 460 us
    pallas_call x1, Pallas kernels: 218 us -> 203 us  [attn_gather(): pl.pallas_call(attn_gather_kernel, out_shape=[full(rows, width), low(rows...]
where the time goes in v6:
time: 493 us; the launch traced here: 488 us
  Pallas kernels  460 us (93%)
  other arithmetic  20 us (4%)
  local copies, waits for them, and re-layouts  7.57 us (2%)
    pallas_call x1, Pallas kernels, attn_gather(): pl.pallas_call(attn_gather_kernel, out_shape=[full(rows, width), low(rows...  203 us
    pallas_call x1, Pallas kernels, mlp(): pl.pallas_call(mlp_kernel, out_shape=[shape(4, rows, width), jax.ShapeDty...  142 us
    pallas_call x1, Pallas kernels, attn_back(): pl.pallas_call(attn_back_kernel, out_shape=[full(rows, width)] + [full(*p...  114 us

profile of v6, /device:TPU:0, one launch (start us, length us, event | category | flops | bytes accessed | tf_op | source)
XLA Modules:
  0.0 488.3 jit_solution(214144129293396893)
XLA Ops:
  0.6 0.8 dynamic_slice.7
  1.4 0.9 convert_reduce_fusion
  2.4 0.2 multiply_sine_fusion
  2.6 0.9 copy.32
  3.5 0.9 copy.33
  4.4 1.4 maximum_maximum_fusion.kv_in
  5.8 0.7 pad_maximum_fusion
  6.5 203.4 %attn_gather.1 = (f32[256,2048]{1,0:T(8,128)}, bf16[256,2048]{1,0:T(8,128)(2,1)}, f32[256,1]{1,0:T(8,128)}, f32[256,1]{1,0:T(8,128)}, f32[2,2048]{1,0:T(2,128)},...) custom-call(bf16[288,128]{1,0:T(8,128)(2,1)} %maximum_maximum_fusion, ...), custom_call_target="tpu_custom_call" | custom-call | tf_op jit(solution)/shard_map/attn_gather/pallas_call | solution.py:487
  209.9 142.2 %mlp.1 = (bf16[4,256,2048]{2,1,0:T(8,128)(2,1)}, f32[256,2048]{1,0:T(8,128)}, bf16[4,256,2048]{2,1,0:T(8,128)(2,1)}, bf16[2,256,2048]{2,1,0:T(8,128)(2,1)}, bf16...) custom-call(bf16[4,256,2048]{2,1,0:T(8,128)(2,1)} %get-tuple-element, ...), custom_call_target="tpu_custom_call", output_to_operand_aliasing={{0}: (0, {})} | custom-call | tf_op jit(solution)/shard_map/mlp/pallas_call | solution.py:774
  352.5 3.5 multiply_reduce_fusion
  356.1 2.3 fusion.10
  358.4 114.0 %attn_back.1 = (f32[256,2048]{1,0:T(8,128)}, f32[512,256]{1,0:T(8,128)}, f32[256,512]{1,0:T(8,128)}, f32[288,128]{1,0:T(8,128)}, bf16[256,2048]{1,0:T(8,128)(2,1...) custom-call(bf16[8,4,512,256]{3,2,1,0:T(8,128)(2,1)} %bitcast.26, ...), custom_call_target="tpu_custom_call" | custom-call | tf_op jit(solution)/shard_map/attn_back/pallas_call | solution.py:1048
  472.5 4.8 fusion.5
  477.3 0.4 fusion.3
  477.6 1.2 copy-done.3
  478.9 1.9 fusion.2
  480.8 0.6 slice_bitcast_fusion
  481.4 0.7 copy.35
  482.1 0.7 copy.34
  482.9 1.2 convert_element_type.65
  484.1 1.2 convert_element_type.66
  485.3 1.2 convert_element_type.67
  486.5 0.8 copy.39
  487.3 0.8 copy.40
  (41 shorter events, 0.6 us)
Async XLA Ops:
  2.3 4.2 copy-start.15
  209.9 142.3 %copy-start.13 = (f32[256,1]{1,0:T(8,128)S(1)}, f32[256,1]{1,0:T(8,128)}, u32[]{:S(2)}) copy-start(f32[256,1]{1,0:T(8,128)} %get-tuple-element.54) | copy-start | bytes 3076
  209.9 142.4 %copy-start.9 = (f32[256,1]{1,0:T(8,128)S(1)}, f32[256,1]{1,0:T(8,128)}, u32[]{:S(2)}) copy-start(f32[256,1]{1,0:T(8,128)} %get-tuple-element.58.r1_ref) | copy-start | bytes 3076
  209.9 142.6 %copy-start.14 = (f32[2,2048]{1,0:T(2,128)S(1)}, f32[2,2048]{1,0:T(2,128)}, u32[]{:S(2)}) copy-start(f32[2,2048]{1,0:T(2,128)} %get-tuple-element.55) | copy-start | bytes 49156
  209.9 146.2 %copy-start.5 = (bf16[256,2048]{1,0:T(8,128)(2,1)S(1)}, bf16[256,2048]{1,0:T(8,128)(2,1)}, u32[]{:S(2)}) copy-start(bf16[256,2048]{1,0:T(8,128)(2,1)} %ct_in.1) | copy-start | bytes 3145732
  352.5 3.5 copy-start
  352.5 3.5 copy-start.4
  472.4 4.8 copy-start.1
  472.5 4.8 copy-start.2
  477.3 1.6 copy-start.3
  478.9 1.9 copy-start.12
  478.9 4.0 copy-start.8
  480.8 3.3 copy-start.7
  482.9 2.4 copy-start.6
  484.1 2.4 copy-start.11
  485.3 2.0 copy-start.10

commit v7 on v6

--- a/solution.py
+++ b/solution.py
@@ -515,7 +515,7 @@
     return (left.astype(F32) + right.astype(F32)).astype(BF)
 
 
-def mlp_kernel(a2_old, ct_in, wg_in, wu_in, wd_in, a2_in, da2_out, mo_out, mo_got, gg_out, gu_out, gd_out, twin_g, twin_u, twin_d, wg, wu, wd, a2_buf, ct_buf, mo_buf, a2_col, ct_col, zt, dg, du, out_buf, in_buf, diag_gu, x_gu, y_gu, diag_d, x_d, y_d, stage_gu, stage_d, load, store, line_send, line_recv, a2_send, a2_recv, mo_send, mo_recv, twin_send, twin_recv, send, recv, stage_sem):
+def mlp_kernel(a2_old, ct_in, wg_in, wu_in, wd_in, h_in, r2_ref, gain_ref, a2_in, da2_out, dhb_out, gain_out, mo_out, mo_got, gg_out, gu_out, gd_out, twin_g, twin_u, twin_d, wg, wu, wd, a2_buf, ct_buf, mo_buf, a2_col, ct_col, zt, dg, du, out_buf, in_buf, diag_gu, x_gu, y_gu, diag_d, x_d, y_d, stage_gu, stage_d, h_buf, load, store, line_send, line_recv, a2_send, a2_recv, mo_send, mo_recv, twin_send, twin_recv, send, recv, stage_sem):
     me = Place()
     rows, width = da2_out.shape
     hidden = wg.shape[1]
@@ -737,6 +737,13 @@
         part, extra = half_of(piece(k, me.py, me.c), 0), half_of(diag[k], 0)
         part[...] = add_low(part[...], extra[...])
         side(k, 3).start()
+    own_ct = pltpu.make_async_copy(ct_in.at[me.t], ct_buf.at[0], load.at[2])
+    own_ct.start()
+
+    def h_load(n):
+        return pltpu.make_async_copy(h_in.at[pl.ds(n * h_buf.shape[0], h_buf.shape[0])], h_buf, load.at[0])
+
+    h_load(0).start()
     results = []
     for k in range(3):
         side(k, 2).wait_recv()
@@ -745,9 +752,25 @@
         mine[...] = (mine[...].astype(F32) + from_x[k][...].astype(F32) + from_y[k][...].astype(F32)).astype(BF)
         results.append(pltpu.make_async_copy(mine, (gg_out, gu_out, gd_out)[k], stage_sem.at[k]))
         results[-1].start()
+    own_ct.wait()
     near_send().wait_recv()
     cross_send(2).wait_recv()
-    da2_out[...] += in_buf[0].astype(F32) + in_buf[1].astype(F32)
+    part_rows = h_buf.shape[0]
+    for n in range(rows // part_rows):
+        at = slice(n * part_rows, (n + 1) * part_rows)
+        h_load(n).wait()
+        da2 = da2_out[at] + in_buf[0, at].astype(F32) + in_buf[1, at].astype(F32)
+        scaled, h, r2 = gain_ref[1:2] * da2, h_buf[...], r2_ref[at]
+        gain = jnp.sum(da2 * h * r2, axis=0, keepdims=True)
+        gain_out[...] = gain if n == 0 else gain_out[...] + gain
+        dres = r2 * scaled - h * (r2 * r2 * r2) * jnp.mean(scaled * h, axis=-1, keepdims=True)
+        if n + 1 < rows // part_rows:
+            h_load(n + 1).start()
+        dh = ct_buf[0, at].astype(F32) + dres
+        da2_out[at] = dh
+        ct_buf[1, at] = dh.astype(BF)
+    results.append(pltpu.make_async_copy(ct_buf.at[1], dhb_out, load.at[1]))
+    results[-1].start()
     for copy in results:
         copy.wait()
     for m in (1, 2):
@@ -766,16 +789,18 @@
             side(k, i).wait_send()
 
 
-def mlp(a2, ct, wg, wu, wd):
+def mlp(a2, ct, wg, wu, wd, h, r2, gain):
     chunks, rows, width = a2.shape
     hidden, cols = wg.shape[1], width // 8
     dma, vmem = pltpu.SemaphoreType.DMA, lambda *shape: pltpu.VMEM(shape, BF)
     shape = lambda *dims: jax.ShapeDtypeStruct(dims, BF)
+    full = lambda *dims: jax.ShapeDtypeStruct(dims, F32)
+    inside = pl.BlockSpec(memory_space=pltpu.VMEM)
     return pl.pallas_call(
         mlp_kernel,
-        out_shape=[shape(4, rows, width), jax.ShapeDtypeStruct((rows, width), F32), shape(4, rows, width), shape(2, rows, width), shape(cols, hidden), shape(cols, hidden), shape(hidden, cols), shape(4, cols, hidden), shape(4, cols, hidden), shape(4, hidden, cols)],
-        in_specs=[ANY] * 5,
-        out_specs=[ANY, pl.BlockSpec(memory_space=pltpu.VMEM)] + [ANY] * 8,
+        out_shape=[shape(4, rows, width), full(rows, width), shape(rows, width), full(1, width), shape(4, rows, width), shape(2, rows, width), shape(cols, hidden), shape(cols, hidden), shape(hidden, cols), shape(4, cols, hidden), shape(4, cols, hidden), shape(4, hidden, cols)],
+        in_specs=[ANY] * 6 + [inside] * 2,
+        out_specs=[ANY, inside, ANY, inside] + [ANY] * 8,
         input_output_aliases={0: 0},
         scratch_shapes=[
             vmem(width, hidden), vmem(width, hidden), vmem(hidden, width),
@@ -785,12 +810,12 @@
             vmem(3, rows, width), vmem(4, rows, width),
             vmem(2, cols, hidden), vmem(2, cols, hidden), vmem(2, cols, hidden),
             vmem(hidden, cols), vmem(hidden, cols), vmem(hidden, cols),
-            vmem(2, cols, hidden), vmem(hidden, cols),
+            vmem(2, cols, hidden), vmem(hidden, cols), pltpu.VMEM((rows // 2, width), F32),
             dma((14,)), dma((2,)), dma((3,)), dma((4,)), dma((1,)), dma((1,)), dma((2,)), dma((2,)), dma((3, 4)), dma((3, 4)), dma((3, 4)), dma((3, 4)), dma((3,)),
         ],
-        compiler_params=pltpu.CompilerParams(collective_id=2, has_side_effects=True, vmem_limit_bytes=62 * 2**20),
+        compiler_params=pltpu.CompilerParams(collective_id=2, has_side_effects=True, vmem_limit_bytes=63 * 2**20),
         name="mlp",
-    )(a2, ct, wg, wu, wd)[1:7]
+    )(a2, ct, wg, wu, wd, h, r2, gain)[1:9]
 
 
 def home(v, dim):
@@ -814,7 +839,7 @@
     return output, da2, gg, gu, gd
 
 
-def attn_back_kernel(wo_in, wq_in, wkv_in, mo_in, q_ref, o_ref, kv_ref, lse_ref, dh_ref, a1_ref, x_ref, r1_ref, gain2_ref, cos_ref, sin_ref, first_ref, da1_ref, go_ref, gq_ref, gkv_ref, mo_got, twin_o, twin_q, twin_kv, grad_o, grad_q, grad_kv, diag_o, diag_q, diag_kv, x_o, x_q, x_kv, y_o, y_q, y_kv, z_o, z_q, z_kv, stage_o, stage_q, stage_kv, wo, wq, wkv, a1t, do_ref, bias_ref, acc_ref, dqt_ref, dkv_own, dkv_out, dkv_got, load, mo_sem, dkv_send, dkv_recv, twin_send, twin_recv, send, recv, line_send, line_recv):
+def attn_back_kernel(wo_in, wq_in, wkv_in, mo_in, dh_in, q_ref, o_ref, kv_ref, lse_ref, dh_ref, a1_ref, x_ref, r1_ref, gain2_ref, gains_ref, cos_ref, sin_ref, first_ref, da1_ref, go_ref, gq_ref, gkv_ref, mo_got, twin_o, twin_q, twin_kv, grad_o, grad_q, grad_kv, diag_o, diag_q, diag_kv, x_o, x_q, x_kv, y_o, y_q, y_kv, z_o, z_q, z_kv, stage_o, stage_q, stage_kv, wo, wq, wkv, a1t, do_ref, bias_ref, acc_ref, dqt_ref, dkv_own, dkv_out, dkv_got, dh_buf, load, mo_sem, dkv_send, dkv_recv, twin_send, twin_recv, send, recv, line_send, line_recv):
     me = Place()
     rows, width = dh_ref.shape
     keys, cols = kv_ref.shape[1], width // 8
@@ -978,7 +1003,22 @@
                 grad_kv[j, d // 2, d % 2, cols:] = jnp.concatenate(extra, 0).astype(BF)
             twin_push(2, j).start()
 
+    def dh_load(n):
+        return pltpu.make_async_copy(dh_in.at[pl.ds(n * dh_buf.shape[0], dh_buf.shape[0])], dh_buf, load.at[5])
+
+    def norm_back():
+        part_rows = dh_buf.shape[0]
+        for n in range(rows // part_rows):
+            at = slice(n * part_rows, (n + 1) * part_rows)
+            scaled, x, r1 = gains_ref[0:1] * da1_ref[at], x_ref[at].astype(F32), r1_ref[at]
+            din = r1 * scaled - x * (r1 * r1 * r1) * jnp.mean(scaled * x, axis=-1, keepdims=True)
+            dh_load(n).wait()
+            da1_ref[at] = dh_buf[...] + din
+            if n + 1 < rows // part_rows:
+                dh_load(n + 1).start()
+
     O, Q, KV = range(3)
+    dh_load(0).start()
     for j in range(4):
         out_group(j)
     for j in range(4):
@@ -1013,6 +1053,7 @@
     fourth(Q, 1)
     for j in range(4):
         first(KV, j)
+    norm_back()
     third(Q, 3)
     for j in range(4):
         second(KV, j)
@@ -1036,7 +1077,7 @@
                 side(k, j, kind).wait_send()
 
 
-def attn_back(wo, wq, wkv, mo, q, o, kv, lse, dh, a1, x, r1, gain2, cos, sin, first):
+def attn_back(wo, wq, wkv, mo, dh_full, q, o, kv, lse, dh, a1, x, r1, gain2, gains, cos, sin, first):
     rows, width = dh.shape
     groups, heads, _ = q.shape
     keys, cols = kv.shape[1], width // 8
@@ -1048,7 +1089,7 @@
     return pl.pallas_call(
         attn_back_kernel,
         out_shape=[full(rows, width)] + [full(*p) for p in pieces] + [low(rows, width)] + [low(4, 4, *p) for p in pieces],
-        in_specs=[ANY] * 4 + [inside] * 12,
+        in_specs=[ANY] * 5 + [inside] * 13,
         out_specs=[inside] * 4 + [ANY] * 4,
         scratch_shapes=[vmem(4, 4, 2, *p) for p in pieces]
         + [vmem(4, *p) for _ in range(3) for p in pieces]
@@ -1057,12 +1098,12 @@
         + [
             vmem(2, 8, heads, cols), vmem(width, heads), vmem(4, 8, cols + 32, 2 * HD), vmem(width, rows), vmem(4, heads, rows),
             pltpu.VMEM((keys, rows), F32), pltpu.VMEM((keys, 2 * HD), F32), vmem(heads, rows),
-            pltpu.VMEM((4, rows, 2 * HD), F32), vmem(4, keys, 2 * HD), vmem(3, 4, rows, 2 * HD),
-            dma((5,)), dma((2,)), dma((3, 4)), dma((3, 4)), dma((12,)), dma((12,)), dma((12, 4)), dma((12, 4)), dma((3, 3)), dma((3, 4)),
+            pltpu.VMEM((4, rows, 2 * HD), F32), vmem(4, keys, 2 * HD), vmem(3, 4, rows, 2 * HD), pltpu.VMEM((rows // 4, width), F32),
+            dma((6,)), dma((2,)), dma((3, 4)), dma((3, 4)), dma((12,)), dma((12,)), dma((12, 4)), dma((12, 4)), dma((3, 3)), dma((3, 4)),
         ],
         compiler_params=pltpu.CompilerParams(collective_id=3, has_side_effects=True, vmem_limit_bytes=63 * 2**20),
         name="attn_back",
-    )(wo, wq, wkv, mo, q, o, kv, lse, dh, a1, x, r1, gain2, cos, sin, first)[:5]
+    )(wo, wq, wkv, mo, dh_full, q, o, kv, lse, dh, a1, x, r1, gain2, gains, cos, sin, first)[:5]
 
 
 def rope_tables(segments, rows, row0):
@@ -1084,14 +1125,10 @@
     w_kv = jnp.concatenate([jnp.concatenate([w_key, w_value], 1), extra], 0)
     h, a1, r1, r2, gains, q, o, lse, kv, wkv, wq, wo, wg, wu, wd, a2, ct = attn_gather(w_kv, w_query, w_out, w_gate, w_up, w_down, cotangent, tokens, cos, sin, first)
     wkv, wq, wo = wkv.reshape(4, 8, -1, 2 * HD), wq.reshape(4, width, -1), wo.reshape(8, 4, -1, cols)
-    da2, mo, mo_near, gg, gu, gd = mlp(a2, ct, wg.reshape(width, -1), wu.reshape(width, -1), wd.reshape(8, hidden, -1))
-    dres, gain2_part = rms_backward(h, r2, gains[1:2], da2)
-    dh = cotangent.astype(F32) + dres
-    da1, go, gq, gkv, mo_far = attn_back(wo, wq, wkv, mo, q, o, kv, lse, dh.astype(BF), a1, tokens, r1, gain2_part[None, :], cos, sin, first)
+    dh, dhb, gain2_part, mo, mo_near, gg, gu, gd = mlp(a2, ct, wg.reshape(width, -1), wu.reshape(width, -1), wd.reshape(8, hidden, -1), h, r2, gains)
+    grad_tokens, go, gq, gkv, mo_far = attn_back(wo, wq, wkv, mo, dh, q, o, kv, lse, dhb, a1, tokens, r1, gain2_part, gains, cos, sin, first)
     mo_own = lax.dynamic_index_in_dim(mo, t, 0, keepdims=False)
     output = (h + mo_own.astype(F32) + mo_near[0].astype(F32) + mo_near[1].astype(F32) + mo_far.astype(F32)).astype(BF)
-    din, _ = rms_backward(tokens.astype(F32), r1, gains[0:1], da1)
-    grad_tokens = dh + din
     gain_grads = gkv[cols : cols + 4].reshape(2, -1)
     gkv = gkv[:cols]
     return (output, grad_tokens, gain_grads[0], gq, gkv[:, :HD], gkv[:, HD:], go, gain_grads[1], gg.astype(F32), gu.astype(F32), gd.astype(F32))

time: 493 us -> 486 us (0.986)
  other arithmetic: 20 us -> 11.5 us
where the time goes in v7:
time: 486 us; the launch traced here: 482 us
  Pallas kernels  461 us (95%)
  other arithmetic  11.5 us (2%)
  local copies, waits for them, and re-layouts  7.67 us (2%)
    pallas_call x1, Pallas kernels, attn_gather(): pl.pallas_call(attn_gather_kernel, out_shape=[full(rows, width), low(rows...  203 us
    pallas_call x1, Pallas kernels, mlp(): pl.pallas_call(mlp_kernel, out_shape=[shape(4, rows, width), full(rows, w...  146 us
    pallas_call x1, Pallas kernels, attn_back(): pl.pallas_call(attn_back_kernel, out_shape=[full(rows, width)] + [full(*p...  112 us

profile of v7, /device:TPU:0, one launch (start us, length us, event | category | flops | bytes accessed | tf_op | source)
XLA Modules:
  0.0 481.9 jit_solution(2090695085944785942)
XLA Ops:
  0.6 0.8 dynamic_slice.7
  1.4 0.9 convert_reduce_fusion
  2.3 0.1 pad.8.clone
  2.4 0.2 multiply_sine_fusion
  2.6 0.9 copy.28
  3.5 0.9 copy.29
  4.4 1.4 maximum_maximum_fusion.kv_in
  5.8 0.7 pad_maximum_fusion
  6.5 0.0 copy-done.7
  6.5 203.4 %attn_gather.1 = (f32[256,2048]{1,0:T(8,128)}, bf16[256,2048]{1,0:T(8,128)(2,1)}, f32[256,1]{1,0:T(8,128)}, f32[256,1]{1,0:T(8,128)}, f32[2,2048]{1,0:T(2,128)},...) custom-call(bf16[288,128]{1,0:T(8,128)(2,1)} %maximum_maximum_fusion, ...), custom_call_target="tpu_custom_call" | custom-call | tf_op jit(solution)/shard_map/attn_gather/pallas_call | solution.py:487
  209.9 145.9 %mlp.1 = (bf16[4,256,2048]{2,1,0:T(8,128)(2,1)}, f32[256,2048]{1,0:T(8,128)}, bf16[256,2048]{1,0:T(8,128)(2,1)}, f32[1,2048]{1,0:T(1,128)}, bf16[4,256,2048]{2,1...) custom-call(bf16[4,256,2048]{2,1,0:T(8,128)(2,1)} %get-tuple-element, ...), custom_call_target="tpu_custom_call", output_to_operand_aliasing={{0}: (0, {})} | custom-call | tf_op jit(solution)/shard_map/mlp/pallas_call | solution.py:799
  355.8 112.2 %attn_back.1 = (f32[256,2048]{1,0:T(8,128)}, f32[512,256]{1,0:T(8,128)}, f32[256,512]{1,0:T(8,128)}, f32[288,128]{1,0:T(8,128)}, bf16[256,2048]{1,0:T(8,128)(2,1...) custom-call(bf16[8,4,512,256]{3,2,1,0:T(8,128)(2,1)} %bitcast.23, ...), custom_call_target="tpu_custom_call" | custom-call | tf_op jit(solution)/shard_map/attn_back/pallas_call | solution.py:1089
  468.0 4.7 fusion.1
  472.7 0.6 slice_bitcast_fusion
  473.3 0.1 fusion.2
  473.4 0.7 copy.31
  474.1 0.7 copy.30
  474.9 1.2 convert_element_type.53
  476.1 1.2 convert_element_type.54
  477.2 1.2 convert_element_type.55
  478.5 1.3 copy.36
  479.8 0.1 copy-done.5
  479.8 0.8 copy.37
  480.6 0.8 copy.38
  (17 shorter events, 0.0 us)
Async XLA Ops:
  2.3 4.2 copy-start.7
  468.0 4.7 copy-start.6
  468.0 6.8 %copy-start.3 = (bf16[256,1408]{1,0:T(8,128)(2,1)S(1)}, bf16[256,1408]{1,0:T(8,128)(2,1)}, u32[]{:S(2)}) copy-start(bf16[256,1408]{1,0:T(8,128)(2,1)} %get-tuple-element.68) | copy-start | bytes 2162692
  472.7 3.3 copy-start.2
  474.8 2.4 copy-start.1
  476.0 2.4 copy-start
  478.5 1.4 copy-start.5
  478.5 2.2 copy-start.4

commit v8 on v7

--- a/solution.py
+++ b/solution.py
@@ -439,14 +439,14 @@
     first(U, 0)
     wq_load(3).wait()
     attend(3, 0)
-    got(0, 2)
-    step(0, 3, "start")
     attend(3, 1)
     for j in range(4):
         wo_load(j).wait()
     mix()
     own_rows(1).start()
     step(1, 1, "start")
+    got(0, 2)
+    step(0, 3, "start")
     kv_keep.start()
     second(G, 0)
     first(D, 0)

time: 486 us -> 484 us (level)
  no operation moved by 1% of the time
where the time goes in v8:
time: 484 us; the launch traced here: 479 us
  Pallas kernels  459 us (95%)
  other arithmetic  11.5 us (2%)
  local copies, waits for them, and re-layouts  7.67 us (2%)
    pallas_call x1, Pallas kernels, attn_gather(): pl.pallas_call(attn_gather_kernel, out_shape=[full(rows, width), low(rows...  202 us
    pallas_call x1, Pallas kernels, mlp(): pl.pallas_call(mlp_kernel, out_shape=[shape(4, rows, width), full(rows, w...  145 us
    pallas_call x1, Pallas kernels, attn_back(): pl.pallas_call(attn_back_kernel, out_shape=[full(rows, width)] + [full(*p...  112 us

profile of v8, /device:TPU:0, one launch (start us, length us, event | category | flops | bytes accessed | tf_op | source)
XLA Modules:
  0.0 479.4 jit_solution(9982350550863399189)
XLA Ops:
  0.6 0.8 dynamic_slice.7
  1.4 0.9 convert_reduce_fusion
  2.3 0.0 copy-start.7
  2.3 0.1 pad.8.clone
  2.4 0.2 multiply_sine_fusion
  2.6 0.9 copy.28
  3.5 0.9 copy.29
  4.4 1.4 maximum_maximum_fusion.kv_in
  5.8 0.7 pad_maximum_fusion
  6.5 201.7 %attn_gather.1 = (f32[256,2048]{1,0:T(8,128)}, bf16[256,2048]{1,0:T(8,128)(2,1)}, f32[256,1]{1,0:T(8,128)}, f32[256,1]{1,0:T(8,128)}, f32[2,2048]{1,0:T(2,128)},...) custom-call(bf16[288,128]{1,0:T(8,128)(2,1)} %maximum_maximum_fusion, ...), custom_call_target="tpu_custom_call" | custom-call | tf_op jit(solution)/shard_map/attn_gather/pallas_call | solution.py:487
  208.2 145.4 %mlp.1 = (bf16[4,256,2048]{2,1,0:T(8,128)(2,1)}, f32[256,2048]{1,0:T(8,128)}, bf16[256,2048]{1,0:T(8,128)(2,1)}, f32[1,2048]{1,0:T(1,128)}, bf16[4,256,2048]{2,1...) custom-call(bf16[4,256,2048]{2,1,0:T(8,128)(2,1)} %get-tuple-element, ...), custom_call_target="tpu_custom_call", output_to_operand_aliasing={{0}: (0, {})} | custom-call | tf_op jit(solution)/shard_map/mlp/pallas_call | solution.py:799
  353.6 111.9 %attn_back.1 = (f32[256,2048]{1,0:T(8,128)}, f32[512,256]{1,0:T(8,128)}, f32[256,512]{1,0:T(8,128)}, f32[288,128]{1,0:T(8,128)}, bf16[256,2048]{1,0:T(8,128)(2,1...) custom-call(bf16[8,4,512,256]{3,2,1,0:T(8,128)(2,1)} %bitcast.23, ...), custom_call_target="tpu_custom_call" | custom-call | tf_op jit(solution)/shard_map/attn_back/pallas_call | solution.py:1089
  465.5 4.7 fusion.1
  470.3 0.6 slice_bitcast_fusion
  470.8 0.1 fusion.2
  470.9 0.7 copy.31
  471.7 0.7 copy.30
  472.4 1.2 convert_element_type.53
  473.6 1.2 convert_element_type.54
  474.8 1.2 convert_element_type.55
  476.0 1.3 copy.36
  477.3 0.1 copy-done.5
  477.3 0.8 copy.37
  478.1 0.8 copy.38
  (17 shorter events, 0.0 us)
Async XLA Ops:
  2.3 4.2 copy-start.7
  465.5 4.7 copy-start.6
  465.5 6.8 %copy-start.3 = (bf16[256,1408]{1,0:T(8,128)(2,1)S(1)}, bf16[256,1408]{1,0:T(8,128)(2,1)}, u32[]{:S(2)}) copy-start(bf16[256,1408]{1,0:T(8,128)(2,1)} %get-tuple-element.68) | copy-start | bytes 2162692
  470.3 3.3 copy-start.2
  472.4 2.4 copy-start.1
  473.6 2.4 copy-start
  476.0 1.4 copy-start.5
  476.0 2.2 copy-start.4
